TPU v7x, 128 devices: a whole 4x4x4 slice. The times are simulated.
128 devices in a mesh: dp: 16 (over x, y_hi, core), llm: 8 (over z, y_lo).
Axes of the slice: x: 4, y: 4 (y_hi: 2, y_lo: 2; y = y_hi * 2 + y_lo), z: 4, core: 2. Of those that a mesh axis runs over, the one named last changes fastest.
Arguments:
- token_grads: bfloat16 [8192, 8192], P(('dp', 'llm')), may hold values from -6 to 6
- token_dest: int32 [8192, 1], P(('dp', 'llm')), may hold values from 0 to 15; in each aligned block of 64 rows (0 to 63, 64 to 127, ...) at most 8 rows name the same one
- merger_down: bfloat16 [5120, 8192], P('llm'), may hold values from -0.078125 to 0.078125
- merger_up: bfloat16 [5120, 5120], P(None, 'llm'), may hold values from -0.078125 to 0.078125
- merger_pre: bfloat16 [8192, 5120], P('dp', 'llm'), may hold values from -6 to 6
- layer_input: bfloat16 [65536, 1280], P(('dp', 'llm')), may hold values from -6 to 6
- window_ids: int32 [128, 512], P(('dp', 'llm')), may hold values from 0 to 15, never falling along the last dimension, each value on 1 to 64 neighbouring positions
- norm_gain: float32 [1280], replicated, may hold values from 0.25 to 1.75
- merge_gain: float32 [1280], replicated, may hold values from 0.25 to 1.75
- qkv_weight: bfloat16 [1280, 1920], P('dp'), may hold values from -1.5 to 1.5
- proj_weight: bfloat16 [640, 1280], P('dp'), may hold values from -0.25 to 0.25
Outputs:
- layer_grad: bfloat16 [65536, 1280], P(('dp', 'llm'))
- qkv_grad: float32 [1280, 1920], P('dp')
- proj_grad: float32 [640, 1280], P('dp')
Inputs may be any that keep to these rules, and one draw needn't show every extreme that they name: `token_dest`: among the 64 tokens of one device, at most 8 name the same vision group. `window_ids`: windows are runs of consecutive patch slots of one vision device, each at most 64 long.
All inputs are finite; a program needn't handle non-finite values.
Results may differ from a plain program's by a relative error of at most 0.035.
The roundings to bfloat16 on the way count: a program that leaves them out, or rounds other values in their place, can miss the bound.
Values may be sent and summed in bfloat16 or wider, within the bound.
A program may use at most 128 MiB of HBM per device.

v0:
```python
import jax
import jax.numpy as jnp
from jax import lax
from jax.sharding import PartitionSpec as P

HEAD_DIM = 80
CAP = 8


EPSILON = 1e-06


def gelu_slope(values):
    return (
        0.5 * (1.0 + jax.scipy.special.erf(values * 0.7071067811865476))
        + values * jnp.exp(-0.5 * values * values) * 0.3989422804014327
    )


def rms_scale(values, scaling):
    return values * lax.rsqrt(jnp.mean(values * values, axis=-1, keepdims=True) + EPSILON) * scaling


def vision_forward(layer_in, packed_weight, output_weight, windows, norm_gain, merge_gain):
    patches = layer_in.shape[0]
    head_count = output_weight.shape[0] // HEAD_DIM
    widened = layer_in.astype(jnp.float32)
    normed = rms_scale(widened, norm_gain).astype(jnp.bfloat16)
    projected = jnp.dot(normed, packed_weight, preferred_element_type=jnp.float32).astype(
        jnp.bfloat16
    )
    triple = projected.reshape(patches, 3, head_count, HEAD_DIM).astype(jnp.float32)
    scores = jnp.einsum("qhd,khd->hqk", triple[:, 0], triple[:, 1]) * HEAD_DIM ** (-0.5)
    same_window = windows[:, None] == windows[None, :]
    scores = jnp.where(same_window[None], scores, -1e30)
    attention = jax.nn.softmax(scores, axis=-1).astype(jnp.bfloat16)
    combined = jnp.einsum("hqk,khd->qhd", attention.astype(jnp.float32), triple[:, 2])
    combined = combined.reshape(patches, head_count * HEAD_DIM).astype(jnp.bfloat16)
    output = widened + jnp.dot(combined, output_weight, preferred_element_type=jnp.float32)
    return rms_scale(output, merge_gain)


def vision_backward(
    layer_in, packed_weight, output_weight, windows, norm_gain, merge_gain, cotangent
):

    def forward(layer_arg, packed_arg, output_arg):
        return vision_forward(layer_arg, packed_arg, output_arg, windows, norm_gain, merge_gain)

    _, pullback = jax.vjp(forward, layer_in, packed_weight, output_weight)
    return pullback(cotangent.astype(jnp.float32))


def local(
    token_grads,
    token_dest,
    merger_down,
    merger_up,
    merger_pre,
    layer_input,
    window_ids,
    norm_gain,
    merge_gain,
    qkv_weight,
    proj_weight,
):
    dp_count = lax.axis_size("dp")
    device_count = dp_count * lax.axis_size("llm")
    hidden_grad = lax.dot_general(
        lax.all_gather(token_grads, "llm", axis=0, tiled=True),
        merger_down,
        (((1,), (1,)), ((), ())),
        preferred_element_type=jnp.float32,
    )
    pre_grad = (hidden_grad * gelu_slope(merger_pre.astype(jnp.float32))).astype(jnp.bfloat16)
    merged = lax.psum_scatter(
        lax.dot_general(
            pre_grad, merger_up, (((1,), (1,)), ((), ())), preferred_element_type=jnp.float32
        ),
        "llm",
        scatter_dimension=0,
        tiled=True,
    ).astype(jnp.bfloat16)
    targets = token_dest[:, 0]
    onehot = (targets[:, None] == jnp.arange(dp_count, dtype=jnp.int32)[None, :]).astype(jnp.int32)
    slot_rank = jnp.sum((jnp.cumsum(onehot, axis=0) - onehot) * onehot, axis=1)
    slot_index = targets * CAP + slot_rank
    placing = (jnp.arange(dp_count * CAP, dtype=jnp.int32)[:, None] == slot_index[None, :]).astype(
        jnp.bfloat16
    )
    outgoing = jnp.dot(placing, merged, preferred_element_type=jnp.float32).astype(jnp.bfloat16)
    outgoing = outgoing.reshape(dp_count, CAP, merged.shape[1])
    arrived = lax.all_to_all(outgoing, "dp", split_axis=0, concat_axis=0, tiled=True)
    cotangent = arrived.reshape(layer_input.shape)
    packed_full, output_full = (
        lax.all_gather(qkv_weight, "dp", axis=0, tiled=True),
        lax.all_gather(proj_weight, "dp", axis=0, tiled=True),
    )
    layer_grad, packed_term, output_term = vision_backward(
        layer_input, packed_full, output_full, window_ids[0], norm_gain, merge_gain, cotangent
    )
    packed_part = packed_term.astype(jnp.float32)
    output_part = output_term.astype(jnp.float32)
    summed_rows = (
        lax.psum_scatter(packed_part, "dp", scatter_dimension=0, tiled=True),
        lax.psum_scatter(output_part, "dp", scatter_dimension=0, tiled=True),
    )
    packed_sum, output_sum = lax.psum((summed_rows[0], summed_rows[1]), "llm")
    return (layer_grad, packed_sum / device_count, output_sum / device_count)


def solution(mesh):
    return jax.shard_map(
        local,
        mesh=mesh,
        in_specs=(
            P(("dp", "llm"), None),
            P(("dp", "llm"), None),
            P("llm", None),
            P(None, "llm"),
            P("dp", "llm"),
            P(("dp", "llm"), None),
            P(("dp", "llm"), None),
            P(),
            P(),
            P("dp", None),
            P("dp", None),
        ),
        out_specs=(P(("dp", "llm"), None), P("dp", None), P("dp", None)),
        check_vma=False,
    )
```

profile of v0, /device:TPU:0, one launch (start us, length us, event | category | flops | bytes accessed | tf_op | source)
XLA Modules:
  0.0 796.5 jit_solution(10845639571331557698)
XLA Ops:
  7.2 0.0 all-gather.4.cloned.1.call-start
  7.2 0.7 all-gather.4.cloned.1.call-update
  7.9 0.0 all-gather.6.cloned.1.call-start
  8.0 0.7 all-gather.6.cloned.1.call-update
  8.7 0.0 reduce-scatter.4.cloned.1.call-start
  8.7 171.8 %all-gather.4.cloned.1.call-done = bf16[512,8192]{1,0:T(8,128)(2,1)} async-done(((bf16[64,8192]{1,0:T(8,128)(2,1)}), bf16[512,8192]{1,0:T(8,128)(2,1)}) %all-gather.4.cloned.1.call-update) | async-done | bytes 8388624 | tf_op jit(solution)/shard_map/all_gather | solution.py:70
  180.5 28.9 %fusion.22 = f32[512,5120]{1,0:T(8,128)} fusion(bf16[5120,640]{1,0:T(8,128)(2,1)} %param.14, bf16[512,8192]{1,0:T(8,128)(2,1)} %all-gather.4.cloned.1.call-done, bf16[640,8192]{1,0:T(8,128)(2,1)} %param.13, bf16[512,640]{1,0:T(8,128)(2,1)S(1)} %copy-done.6), kind=kOutput, calls=%fused_computation.53 | convolution fusion | flops 8727756800 | bytes 36569088 | tf_op jit(solution)/shard_map/dot_general | solution.py:77
  209.4 0.0 copy-start.17
  209.4 0.0 reduce-scatter.4.cloned.1.call-update
  209.4 0.0 all-gather.8.cloned.1.call-start
  209.5 0.5 all-gather.8.cloned.1.call-update
  210.0 0.7 copy-done.4
  210.7 0.3 fusion.17
  211.1 0.0 copy-start.14
  211.1 0.5 copy-done.11
  211.6 0.1 fusion.43
  211.7 0.1 reduce_window_sum.11
  211.8 0.2 select_reduce_fusion
  212.0 0.0 copy-done.13
  212.0 0.2 broadcast_compare_fusion
  212.2 30.3 %all-gather.6.cloned.1.call-done = bf16[1280,1920]{1,0:T(8,128)(2,1)} async-done(((bf16[80,1920]{1,0:T(8,128)(2,1)}), bf16[1280,1920]{1,0:T(8,128)(2,1)}) %all-gather.6.cloned.1.call-update) | async-done | bytes 4915216 | tf_op jit(solution)/shard_map/all_gather | solution.py:96
  242.5 6.6 convolution_convert_fusion.3
  249.2 2.7 copy.22
  251.9 5.5 fusion.55
  257.4 0.6 multiply_divide_fusion
  258.0 194.4 %reduce-scatter.4.cloned.1.call-done = f32[64,5120]{1,0:T(8,128)} async-done(((f32[512,5120]{1,0:T(8,128)}), f32[64,5120]{1,0:T(8,128)}) %reduce-scatter.4.cloned.1.call-update) | async-done | bytes 1310736 | tf_op jit(solution)/shard_map/reduce_scatter | solution.py:76
  452.4 2.9 fusion.9
  455.3 6.6 all-to-all-start
  461.9 0.2 reduce-scatter.8.cloned.1.call-start
  462.1 4.6 divide_convert_fusion
  466.7 1.9 copy-done
  468.7 0.8 convolution_convert_fusion.7
  469.5 14.8 %all-to-all-done = bf16[16,8,5120]{2,1,0:T(8,128)(2,1)} async-done(((bf16[16,8,5120]{2,1,0:T(8,128)(2,1)}), bf16[16,8,5120]{2,1,0:T(8,128)(2,1)}, u32[]{:S(2)}, u32[]{:S(2)}) %all-to-all-start) | async-done | bytes 1310752 | tf_op jit(solution)/shard_map/all_to_all | solution.py:93
  484.3 2.4 reshape.111
  486.7 22.8 %all-gather.8.cloned.1.call-done = bf16[640,1280]{1,0:T(8,128)(2,1)} async-done(((bf16[40,1280]{1,0:T(8,128)(2,1)}), bf16[640,1280]{1,0:T(8,128)(2,1)}) %all-gather.8.cloned.1.call-update) | async-done | bytes 1638416 | tf_op jit(solution)/shard_map/all_gather | solution.py:97
  509.6 3.4 multiply_reduce_fusion.1
  513.0 0.5 add_add_fusion.1
  513.6 1.5 copy-done.2
  515.1 2.8 fusion.13
  517.8 0.0 reduce-scatter.8.cloned.1.call-update
  517.9 0.0 reduce-scatter.6.cloned.1.call-start
  517.9 1.7 copy-done.3
  519.6 3.5 fusion.56
  523.1 1.3 copy.24
  524.4 7.2 fusion.6
  531.6 0.0 slice-start
  531.6 1.4 convolution_bitcast_fusion.2
  533.0 0.2 copy-done.8
  533.3 8.9 %convolution_bitcast_fusion = f32[512,1,8,80]{0,3,2,1:T(8,128)} fusion(bf16[512,3,8,80]{0,3,2,1:T(8,128)(2,1)S(1)} %bitcast.81, f32[8,512,512]{1,2,0:T(8,128)} %get-tuple-element.10, bf16[8,512,512]{1,2,0:T(8,128)(2,1)} %get-tuple-element.13, f32[8,512]{1,0:T(8,128)S(1)} %neg.6, f32[8,512]{1,0:T(8,128)S(1)} %get-tuple-element.9, ...), kind=kOutput, calls=%fused_computation.47 | convolution fusion | flops 348127232 | bytes 14843904 | tf_op jit(solution)/shard_map/transpose(jvp(qhd,khd->hqk))/dot_general | solution.py:33
  542.2 5.3 convolution_bitcast_fusion.1
  547.5 2.1 add_convert_fusion
  549.6 1.3 copy-done.9
  550.9 5.9 fusion.7
  556.8 0.0 reduce-scatter.6.cloned.1.call-update
  556.8 0.0 copy-start.12
  556.8 0.3 all-reduce.6.cloned.1.call-start
  557.1 7.9 fusion.20
  564.9 27.7 %reduce-scatter.8.cloned.1.call-done = f32[40,1280]{1,0:T(8,128)} async-done(((f32[640,1280]{1,0:T(8,128)}), f32[40,1280]{1,0:T(8,128)}) %reduce-scatter.8.cloned.1.call-update) | async-done | bytes 204816 | tf_op jit(solution)/shard_map/reduce_scatter | solution.py:106
  592.6 112.8 %reduce-scatter.6.cloned.1.call-done = f32[80,1920]{1,0:T(8,128)} async-done(((f32[1280,1920]{1,0:T(8,128)}), f32[80,1920]{1,0:T(8,128)}) %reduce-scatter.6.cloned.1.call-update) | async-done | bytes 614416 | tf_op jit(solution)/shard_map/reduce_scatter | solution.py:105
  705.4 0.0 all-reduce.6.cloned.1.call-update
  705.4 3.8 fusion.16
  709.3 76.8 %all-reduce.6.cloned.1.call-done = (f32[80,1920]{1,0:T(8,128)}, f32[40,1280]{1,0:T(8,128)}) async-done(((f32[80,1920]{1,0:T(8,128)}, f32[40,1280]{1,0:T(8,128)}), (f32[80,1920]{1,0:T(8,128)}, f32[40,1280]{1,0:T(8,128)})) %all-reduce.6.cloned.1.call-update) | async-done | bytes 819216 | tf_op jit(solution)/shard_map/psum | solution.py:108
  786.0 1.9 broadcast_multiply_fusion
  788.0 1.6 broadcast_multiply_fusion.1
  (36 shorter events, 0.1 us)
Async XLA Ops:
  7.2 173.4 %copy-start.6 = (bf16[512,640]{1,0:T(8,128)(2,1)S(1)}, bf16[512,640]{1,0:T(8,128)(2,1)}, u32[]{:S(2)}) copy-start(bf16[512,640]{1,0:T(8,128)(2,1)} %param.15) | copy-start | bytes 1966084
  7.2 173.3 %all-gather.4.cloned.1.call-start = ((), (), s32[]{:S(2)}) async-start(), calls=%async_computation.4 | async-start | bytes 9437184 | tf_op jit(solution)/shard_map/all_gather | solution.py:70
  7.9 234.6 %all-gather.6.cloned.1.call-start = ((), (), s32[]{:S(2)}) async-start(), calls=%async_computation.6 | async-start | bytes 5222400 | tf_op jit(solution)/shard_map/all_gather | solution.py:96
  8.7 443.8 %reduce-scatter.4.cloned.1.call-start = ((), (), s32[]{:S(2)}) async-start(), calls=%async_computation.5 | async-start | bytes 11796480 | tf_op jit(solution)/shard_map/reduce_scatter | solution.py:76
  209.4 1.3 copy-start.4
  209.4 2.2 copy-start.16
  209.4 2.6 copy-start.13
  209.4 33.1 %copy-start.17 = (f32[1280]{0:T(1024)S(1)}, f32[1280]{0:T(1024)}, u32[]{:S(2)}) copy-start(f32[1280]{0:T(1024)} %param.18) | copy-start | bytes 15364
  209.4 300.1 %all-gather.8.cloned.1.call-start = ((), (), s32[]{:S(2)}) async-start(), calls=%async_computation.7 | async-start | bytes 1740800 | tf_op jit(solution)/shard_map/all_gather | solution.py:97
  211.0 0.6 copy-start.11
  211.1 31.5 %copy-start.14 = (f32[512]{0:T(512)}, f32[512]{0:T(512)S(1)}, u32[]{:S(2)}) copy-start(f32[512]{0:T(512)S(1)} %fusion.44) | copy-start | bytes 6148
  251.9 214.9 %copy-start.7 = (bf16[512,1920]{0,1:T(8,128)(2,1)}, bf16[512,1920]{0,1:T(8,128)(2,1)S(1)}, u32[]{:S(2)}) copy-start(bf16[512,1920]{0,1:T(8,128)(2,1)S(1)} %copy.22) | copy-start | bytes 5898244
  455.3 29.0 %all-to-all-start = ((bf16[16,8,5120]{2,1,0:T(8,128)(2,1)}), bf16[16,8,5120]{2,1,0:T(8,128)(2,1)}, u32[]{:S(2)}, u32[]{:S(2)}) async-start(bf16[16,8,5120]{2,1,0:T(8,128)(2,1)} %fusion.9), calls=%async_computation.1 | async-start | bytes 2621440 | tf_op jit(solution)/shard_map/all_to_all | solution.py:93
  461.9 130.8 %reduce-scatter.8.cloned.1.call-start = ((), (), s32[]{:S(2)}) async-start(), calls=%async_computation.9 | async-start | bytes 3481600 | tf_op jit(solution)/shard_map/reduce_scatter | solution.py:106
  466.7 1.9 copy-start
  509.6 3.5 copy-start.10
  513.5 1.5 copy-start.2
  517.8 1.7 copy-start.3
  517.9 187.5 %reduce-scatter.6.cloned.1.call-start = ((), (), s32[]{:S(2)}) async-start(), calls=%async_computation.8 | async-start | bytes 10444800 | tf_op jit(solution)/shard_map/reduce_scatter | solution.py:105
  524.4 7.2 copy-start.1
  531.6 1.6 copy-start.8
  531.6 10.5 %slice-start = ((s8[8388608]{0:T(1024)(128)(4,1)}), s8[4194304]{0:T(1024)(128)(4,1)S(1)}, s32[]{:S(2)}) async-start(s8[8388608]{0:T(1024)(128)(4,1)} %bitcast.72), calls=%async_computation.11 | async-start | bytes 8388608
  533.3 8.9 %slice-start.1 = ((s8[8388608]{0:T(1024)(128)(4,1)}), s8[4194304]{0:T(1024)(128)(4,1)S(1)}, s32[]{:S(2)}) async-start(s8[8388608]{0:T(1024)(128)(4,1)} %bitcast.72), calls=%async_computation.12 | async-start | bytes 8388608
  547.5 3.4 copy-start.5
  547.5 3.4 copy-start.15
  547.5 3.4 copy-start.18
  549.6 1.3 copy-start.9
  556.8 148.6 %copy-start.12 = (f32[512]{0:T(512)S(1)}, f32[512]{0:T(512)}, u32[]{:S(2)}) copy-start(f32[512]{0:T(512)} %copy-done.11) | copy-start | bytes 6148
  556.8 229.2 %all-reduce.6.cloned.1.call-start = ((), (), s32[]{:S(2)}) async-start(), calls=%async_computation.10 | async-start | bytes 1638400 | tf_op jit(solution)/shard_map/psum | solution.py:108
Sparse Core Ops, SparseCore 0:
  9.7 170.8 all-gather.3
  182.8 59.6 all-gather.5
  244.9 207.4 reduce-scatter.3
  454.6 54.8 all-gather.7
  518.0 74.5 reduce-scatter.7
  597.6 107.7 reduce-scatter.5
  708.0 78.0 all-reduce.5
where the time goes:
time: 797 us; the launch traced here: 796 us
  waiting for transfers between devices  653 us (82%)
  matrix products  90.9 us (11%)
  other arithmetic  16.2 us (2%)
  local copies, waits for them, and re-layouts  14.4 us (2%)
  between operations  14.4 us (2%)
    reduce_scatter x1, waiting for transfers between devices, local(): lax.psum_scatter(lax.dot_general(pre_grad, merger_up, (((1,), (1,)), ((),...  194 us
    all_gather x1, waiting for transfers between devices, local(): lax.all_gather(token_grads, 'llm', axis=0, tiled=True)  172 us
    reduce_scatter x1, waiting for transfers between devices, local(): lax.psum_scatter(packed_part, 'dp', scatter_dimension=0, tiled=True)  113 us
    psum x1, waiting for transfers between devices, local(): packed_sum, output_sum = lax.psum((summed_rows[0], summed_rows[1]), 'llm')  76.8 us
    all_gather x1, waiting for transfers between devices, local(): lax.all_gather(qkv_weight, 'dp', axis=0, tiled=True)  30.3 us
    dot_general x1, matrix products, local(): lax.dot_general(pre_grad, merger_up, (((1,), (1,)), ((), ())), preferred_...  28.9 us
    reduce_scatter x1, waiting for transfers between devices, local(): lax.psum_scatter(output_part, 'dp', scatter_dimension=0, tiled=True)  27.7 us
    all_gather x1, waiting for transfers between devices, local(): lax.all_gather(proj_weight, 'dp', axis=0, tiled=True)  22.8 us
  transfers between devices with their start and end apart: 8, of which 8 were waited for; matrix products, arithmetic and copies ran while one was open for 13% of the time, Pallas kernels for 0%

commit v1 on v0

v1 whole, which is shorter than its diff:
```python
import jax
import jax.numpy as jnp
from jax import lax
from jax.experimental import pallas as pl
from jax.experimental.pallas import tpu as pltpu
from jax.sharding import PartitionSpec as P

MESH = pl.DeviceIdType.MESH
HEAD_DIM = 80
CAP = 8
EPSILON = 1e-06
BF16 = jnp.bfloat16
F32 = jnp.float32

NT = (((1,), (1,)), ((), ()))
TN = (((0,), (0,)), ((), ()))

N_TOK = 8
N_FEAT = 8


def gelu_slope(values):
    return (
        0.5 * (1.0 + lax.erf(values * 0.7071067811865476))
        + values * jnp.exp(-0.5 * values * values) * 0.3989422804014327
    )


def rms_scale(values, scaling):
    return values * lax.rsqrt(jnp.mean(values * values, axis=-1, keepdims=True) + EPSILON) * scaling


def place():
    d, l = lax.axis_index("dp"), lax.axis_index("llm")
    return d // 4, (d // 2) % 2, d % 2, l // 2, l % 2


def at(x, yh, c, z, yl):
    return (x * 2 + yh) * 2 + c, z * 2 + yl


def remote(src, dst, send, recv, device):
    return pltpu.make_async_remote_copy(
        src_ref=src, dst_ref=dst, send_sem=send, recv_sem=recv, device_id=device, device_id_type=MESH
    )


def greet(devices):
    barrier = pltpu.get_barrier_semaphore()
    for device in devices:
        pl.semaphore_signal(barrier, inc=1, device_id=device, device_id_type=MESH)
    pl.semaphore_wait(barrier, len(devices))


def merger_kernel(
    tok, dest, down, up, pre, qw, ow,
    cot, wq, wo,
    G, down_v, up_v, slope, acc, pg, pre2,
    S, R, own, T, T0, ZR, M, OUT, A,
    loc, zs, zr, ys, yr, ps, pr, ws, wr, xs, xr, cs, cr, rys, ryr, rzs, rzr, as_, ar,
):
    x, yh, c, z, yl = place()
    d = (x * 2 + yh) * 2 + c
    l = z * 2 + yl
    zp = [at(x, yh, c, (z + s) % 4, yl) for s in (1, 2, 3)]
    p1 = at(x, yh, c, z, 1 - yl)
    p2 = at(x, 1 - yh, c, z, 1 - yl)
    yhp = at(x, 1 - yh, c, z, yl)
    xp = [at((x + s) % 4, yh, c, z, yl) for s in (1, 2, 3)]
    core = at(x, yh, 1 - c, z, yl)
    dps = [((d + s) % 16, l) for s in range(1, 16)]

    cp_tok = pltpu.make_async_copy(tok, G.at[0, pl.ds(0, 64)], loc.at[0])
    cp_down = pltpu.make_async_copy(down, down_v, loc.at[1])
    cp_up = pltpu.make_async_copy(up, up_v, loc.at[2])
    cp_tok.start()
    cp_down.start()
    cp_up.start()
    greet(zp + [p1, p2] + dps)
    cp_tok.wait()

    W = G.shape[2] // N_TOK

    def col(k):
        return pl.ds(pl.multiple_of(k * W, W), W)

    def z_copy(k, i):
        return remote(
            G.at[0, pl.ds(0, 64), col(k)], G.at[3 - i, pl.ds(0, 64), col(k)], zs.at[k, i], zr.at[k, i], zp[i]
        )

    def y_copy(k, i):
        return remote(
            G.at[:, pl.ds(32 * i, 32), col(k)],
            G.at[:, pl.ds(64 + 32 * i, 32), col(k)],
            ys.at[k, i],
            yr.at[k, i],
            (p1, p2)[i],
        )

    for k in range(2):
        for i in (0, 2, 1):
            z_copy(k, i).start()

    def pre_copy(zz):
        rows = pl.ds(pl.multiple_of((2 * zz + 1 - yl) * 64 + 32, 32), 32)
        return remote(pre.at[rows], pre2.at[pl.ds(32 * zz, 32)], ps.at[zz], pr.at[zz], yhp)

    for zz in range(4):
        pre_copy(zz).start()

    def w_copies(source, index, sends, recvs, device):
        first = wq.at[index] if source is None else source[0]
        second = wo.at[index] if source is None else source[1]
        return [
            remote(first, wq.at[index], sends.at[0], recvs.at[0], device),
            remote(second, wo.at[index], sends.at[1], recvs.at[1], device),
        ]

    def flipped(dd):
        return dd + 2 - 4 * ((dd // 2) % 2)

    wq[d] = qw[...]
    wo[d] = ow[...]
    d2 = flipped(d)
    for cp in w_copies((qw, ow), d, ws.at[0], wr.at[0], p2):
        cp.start()
    for i in (0, 2, 1):
        for cp in w_copies((qw, ow), d, xs.at[0, i], xr.at[0, i], xp[i]):
            cp.start()
    for cp in w_copies((qw, ow), d, cs.at[0], cr.at[0], core):
        cp.start()

    for zz in range(4):
        pre_copy(zz).wait_recv()
    for r in range(4):
        zz = (z + r) % 4
        mine = pre[pl.ds(pl.multiple_of((2 * zz + yl) * 64, 64), 64), :]
        first = pre[pl.ds(pl.multiple_of((2 * zz + 1 - yl) * 64, 64), 32), :]
        second = pre2[pl.ds(pl.multiple_of(zz * 32, 32), 32), :]
        slope[r, 0:64, :] = gelu_slope(mine.astype(F32))
        slope[r, 64:96, :] = gelu_slope(first.astype(F32))
        slope[r, 96:128, :] = gelu_slope(second.astype(F32))
    acc[...] = jnp.zeros_like(acc)

    def multiply(k):
        for i in range(2):
            y_copy(k, i).wait_recv()
        tile = G[:, :, col(k)].reshape(512, W)
        acc[...] += lax.dot_general(tile, down_v[:, col(k)], NT, preferred_element_type=F32)

    cp_down.wait()

    def gather_step(k, carry):
        @pl.when(k + 2 < N_TOK)
        def _():
            for i in (0, 2, 1):
                z_copy(k + 2, i).start()

        for i in range(3):
            z_copy(k, i).wait_recv()
        for i in range(2):
            y_copy(k, i).start()

        @pl.when(k == 1)
        def _():
            for cp in w_copies((qw, ow), d2, ws.at[0], wr.at[0], p2):
                cp.wait_recv()
            for i in (0, 2, 1):
                for cp in w_copies(None, d2, xs.at[1, i], xr.at[1, i], xp[i]):
                    cp.start()
            for cp in w_copies(None, d2, cs.at[1], cr.at[1], core):
                cp.start()

        @pl.when(k >= 1)
        def _():
            multiply(k - 1)

        return carry

    lax.fori_loop(0, N_TOK, gather_step, 0)
    multiply(N_TOK - 1)

    def x_arrive(h):
        for i in range(3):
            other = ((x + i + 1) % 4 * 2 + yh) * 2 + c
            other = flipped(other) if h else other
            for cp in w_copies(None, other, xs.at[h, 2 - i], xr.at[h, 2 - i], xp[2 - i]):
                cp.wait_recv()
            for cp in w_copies(None, other, cs.at[2 + 3 * h + i], cr.at[2 + 3 * h + i], core):
                cp.start()

    x_arrive(0)

    pg[...] = (acc[...] * slope[...].reshape(512, slope.shape[2])).astype(BF16)
    cp_up.wait()

    token = dest[...]
    hot = (lax.broadcasted_iota(jnp.int32, (16, 64), 0) == token).astype(F32)
    before = (
        lax.broadcasted_iota(jnp.int32, (64, 64), 0) < lax.broadcasted_iota(jnp.int32, (64, 64), 1)
    ).astype(F32)
    rank = jnp.sum(jnp.dot(hot, before, preferred_element_type=F32) * hot, axis=0, keepdims=True)
    target = token * 16 + rank.astype(jnp.int32)
    row = lax.broadcasted_iota(jnp.int32, (256, 64), 0)
    placing = jnp.concatenate(
        [(row == target).astype(F32), (row == target + 8).astype(F32)], axis=1
    ).astype(BF16)

    V = M.shape[2]

    def ry_copy(f, i):
        return remote(S.at[f, i], R.at[f, i], rys.at[f, i], ryr.at[f, i], (p1, p2)[i])

    def rz_copy(f, i):
        return remote(T.at[f, i], ZR.at[f, i], rzs.at[f, i], rzr.at[f, i], zp[i])

    def a_copy(j, s):
        dd = (d + s) % 16
        return remote(
            OUT.at[j, pl.ds(pl.multiple_of(dd * 16, 16), 16)],
            A.at[j, pl.ds(pl.multiple_of(d * 16, 16), 16)],
            as_.at[j],
            ar.at[j],
            dps[s - 1],
        )

    def sum_step(i, carry):
        @pl.when(i < N_FEAT)
        def _():
            rows = pl.ds(pl.multiple_of(i * V, V), V)
            part = lax.dot_general(pg[...], up_v[rows, :], NT, preferred_element_type=F32)
            part = part.reshape(4, 128, V)
            S[i, 0] = part[:, 64:96, :].astype(BF16)
            S[i, 1] = part[:, 96:128, :].astype(BF16)
            for h in range(2):
                ry_copy(i, h).start()
            own[i % 2] = part[:, 0:64, :]

        @pl.when((i >= 1) & (i < N_FEAT + 1))
        def _():
            f = i - 1
            for h in range(2):
                ry_copy(f, h).wait_recv()
            total = own[f % 2] + jnp.concatenate([R[f, 0].astype(F32), R[f, 1].astype(F32)], axis=1)
            T[f] = total[1:4].astype(BF16)
            T0[f % 2] = total[0]
            for h in (0, 2, 1):
                rz_copy(f, h).start()

        @pl.when(i >= 2)
        def _():
            f = i - 2
            for h in range(3):
                rz_copy(f, h).wait_recv()
            M[f] = (
                T0[f % 2] + ZR[f, 0].astype(F32) + ZR[f, 1].astype(F32) + ZR[f, 2].astype(F32)
            ).astype(BF16)

            @pl.when(f % 2 == 1)
            def _():
                j = f // 2
                both = jnp.concatenate([M[f - 1], M[f]], axis=0)
                OUT[j] = jnp.dot(placing, both, preferred_element_type=F32).astype(BF16)
                for s in range(1, 16):
                    a_copy(j, s).start()
                here = pl.ds(pl.multiple_of(d * 16, 16), 16)
                A[j, here, :] = OUT[j, here, :]

        return carry

    lax.fori_loop(0, N_FEAT + 2, sum_step, 0)

    x_arrive(1)

    fifteen = pl.ds(0, 240)
    for j in range(4):
        pltpu.make_async_copy(A.at[j, fifteen], A.at[j, fifteen], ar.at[j]).wait()
    out_row = lax.broadcasted_iota(jnp.int32, (128, 256), 0)
    in_row = lax.broadcasted_iota(jnp.int32, (128, 256), 1)
    wanted = (out_row % 4) * 64 + (out_row // 32) * 16 + (out_row // 4) % 8
    for h in range(2):
        order = (in_row == wanted + 8 * h).astype(F32).astype(BF16)
        for g in range(4):
            stacked = A[:, 64 * g : 64 * g + 64, :].reshape(256, V)
            cot[128 * g : 128 * g + 128, V * h : V * h + V] = jnp.dot(
                order, stacked, preferred_element_type=F32
            ).astype(BF16)

    cidx = [d, d2]
    for h in range(2):
        for i in range(3):
            other = ((x + i + 1) % 4 * 2 + yh) * 2 + c
            cidx.append(flipped(other) if h else other)
    for n, index in enumerate(cidx):
        for cp in w_copies(None, index, cs.at[n], cr.at[n], core):
            cp.wait_send()
        theirs = index + 1 - 2 * c
        for cp in w_copies(None, theirs, cs.at[n], cr.at[n], core):
            cp.wait_recv()
    for cp in w_copies((qw, ow), d, ws.at[0], wr.at[0], p2):
        cp.wait_send()
    for h in range(2):
        for i in range(3):
            for cp in w_copies(None, d2 if h else d, xs.at[h, i], xr.at[h, i], xp[i]):
                cp.wait_send()
    for zz in range(4):
        pre_copy(zz).wait_send()

    def drain(k, carry):
        for i in range(3):
            z_copy(k, i).wait_send()
        for i in range(2):
            y_copy(k, i).wait_send()
        return carry

    lax.fori_loop(0, N_TOK, drain, 0)

    def drain2(f, carry):
        for i in range(2):
            ry_copy(f, i).wait_send()
        for i in range(3):
            rz_copy(f, i).wait_send()
        return carry

    lax.fori_loop(0, N_FEAT, drain2, 0)
    for j in range(4):
        pltpu.make_async_copy(OUT.at[j, fifteen], OUT.at[j, fifteen], as_.at[j]).wait()


def merger(tok, dest, down, up, pre, qw, ow):
    vm = pl.BlockSpec(memory_space=pltpu.VMEM)
    hbm = pl.BlockSpec(memory_space=pl.ANY)
    dma = pltpu.SemaphoreType.DMA
    hid = pre.shape[1]
    feat = up.shape[0]
    V = feat // N_FEAT
    return pl.pallas_call(
        merger_kernel,
        name="merger",
        out_shape=(
            jax.ShapeDtypeStruct((512, feat // 4), BF16),
            jax.ShapeDtypeStruct((16,) + qw.shape, BF16),
            jax.ShapeDtypeStruct((16,) + ow.shape, BF16),
        ),
        in_specs=[hbm, vm, hbm, hbm, vm, vm, vm],
        out_specs=(vm, vm, vm),
        scratch_shapes=[
            pltpu.VMEM((4, 128, tok.shape[1]), BF16),
            pltpu.VMEM(down.shape, BF16),
            pltpu.VMEM(up.shape, BF16),
            pltpu.VMEM((4, 128, hid), F32),
            pltpu.VMEM((512, hid), F32),
            pltpu.VMEM((512, hid), BF16),
            pltpu.VMEM((128, hid), BF16),
            pltpu.VMEM((N_FEAT, 2, 4, 32, V), BF16),
            pltpu.VMEM((N_FEAT, 2, 4, 32, V), BF16),
            pltpu.VMEM((2, 4, 64, V), F32),
            pltpu.VMEM((N_FEAT, 3, 64, V), BF16),
            pltpu.VMEM((2, 64, V), F32),
            pltpu.VMEM((N_FEAT, 3, 64, V), BF16),
            pltpu.VMEM((N_FEAT, 64, V), BF16),
            pltpu.VMEM((4, 256, V), BF16),
            pltpu.VMEM((4, 256, V), BF16),
            dma((3,)),
            dma((N_TOK, 3)), dma((N_TOK, 3)), dma((N_TOK, 2)), dma((N_TOK, 2)),
            dma((4,)), dma((4,)),
            dma((1, 2)), dma((1, 2)),
            dma((2, 3, 2)), dma((2, 3, 2)),
            dma((8, 2)), dma((8, 2)),
            dma((N_FEAT, 2)), dma((N_FEAT, 2)),
            dma((N_FEAT, 3)), dma((N_FEAT, 3)),
            dma((4,)), dma((4,)),
        ],
        compiler_params=pltpu.CompilerParams(
            collective_id=1, has_side_effects=True, vmem_limit_bytes=60 << 20
        ),
        cost_estimate=pl.CostEstimate(flops=9 * 10**9, bytes_accessed=40 * 10**6, transcendentals=0),
    )(tok, dest, down, up, pre, qw, ow)


def reduce_kernel(
    g, out,
    C, S, XR, ZR, E1, E2, XR2, ZR2, E, YR, F, FR,
    cs, cr, xs, xr, zs, zr, x2s, x2r, z2s, z2r, ys, yr, fs, fr,
):
    x, yh, c, z, yl = place()
    zp = [at(x, yh, c, (z + s) % 4, yl) for s in (1, 2, 3)]
    xp = [at((x + s) % 4, yh, c, z, yl) for s in (1, 2, 3)]
    core = at(x, yh, 1 - c, z, yl)
    p1 = at(x, yh, c, z, 1 - yl)
    p2 = at(x, 1 - yh, c, z, 1 - yl)
    yhp = at(x, 1 - yh, c, z, yl)
    greet(zp + xp + [core, p1, p2, yhp])

    def core_copy(p):
        return remote(g.at[1 - c, p], C.at[p], cs.at[p], cr.at[p], core)

    for p in (2, 0, 3, 1):
        core_copy(p).start()

    def x_copy(p, i):
        return remote(S.at[p, (x + i + 1) % 4], XR.at[i, p], xs.at[p, i], xr.at[p, i], xp[i])

    def z_copy(i):
        t = (z + i + 1) % 4
        return remote(
            S.at[2 + t % 2, :, t // 2], ZR.at[i], zs.at[i], zr.at[i], zp[i]
        )

    def summed(p):
        core_copy(p).wait_recv()
        S[p] = (g[c, p].astype(F32) + C[p].astype(F32)).astype(BF16)

    summed(2)
    summed(0)
    for i in (0, 2, 1):
        x_copy(0, i).start()
    summed(3)
    for i in (0, 2, 1):
        z_copy(i).start()
    summed(1)
    for i in (0, 2, 1):
        x_copy(1, i).start()

    for i in range(3):
        z_copy(i).wait_recv()
    mine = S[2 + z % 2, :, z // 2].astype(F32)
    for i in range(3):
        mine = mine + ZR[i].astype(F32)
    E2[...] = mine.astype(BF16)

    def x2_copy(i):
        return remote(E2.at[(x + i + 1) % 4], XR2.at[i], x2s.at[i], x2r.at[i], xp[i])

    for i in (0, 2, 1):
        x2_copy(i).start()
    for p in range(2):
        for i in range(3):
            x_copy(p, i).wait_recv()
        mine = S[p, x].astype(F32)
        for i in range(3):
            mine = mine + XR[i, p].astype(F32)
        E1[0, p] = mine[0].astype(BF16)
        E1[1, p] = mine[1].astype(BF16)

    def z2_copy(i):
        t = (z + i + 1) % 4
        return remote(E1.at[t // 2, t % 2], ZR2.at[i], z2s.at[i], z2r.at[i], zp[i])

    for i in (0, 2, 1):
        z2_copy(i).start()
    for i in range(3):
        x2_copy(i).wait_recv()
    mine = E2[x].astype(F32)
    for i in range(3):
        mine = mine + XR2[i].astype(F32)
    E[1] = mine.astype(BF16)
    for i in range(3):
        z2_copy(i).wait_recv()
    mine = E1[z // 2, z % 2].astype(F32)
    for i in range(3):
        mine = mine + ZR2[i].astype(F32)
    E[0] = mine.astype(BF16)

    def y_copy(i):
        return remote(E, YR.at[i], ys.at[i], yr.at[i], (p1, p2, yhp)[i])

    owner = yh == z // 2

    @pl.when(owner)
    def _():
        y_copy(0).start()
        for i in range(3):
            y_copy(i).wait_recv()
        F[...] = (
            (E[...].astype(F32) + YR[0].astype(F32) + YR[1].astype(F32) + YR[2].astype(F32)) * (1.0 / 128.0)
        ).astype(BF16)
        y_copy(0).wait_send()

    @pl.when(jnp.logical_not(owner))
    def _():
        for i in (1, 2):
            y_copy(i).start()
        for i in (1, 2):
            y_copy(i).wait_send()

    def f_copy(i):
        return remote(F, FR.at[z % 2], fs.at[i], fr.at[z % 2], zp[i])

    @pl.when(owner)
    def _():
        for i in range(3):
            f_copy(i).start()
        FR[z % 2] = F[...]

    def f_wait(slot):
        pltpu.make_async_copy(FR.at[slot], FR.at[slot], fr.at[slot]).wait()

    @pl.when(owner)
    def _():
        f_wait(1 - z % 2)
        for i in range(3):
            f_copy(i).wait_send()

    @pl.when(jnp.logical_not(owner))
    def _():
        f_wait(0)
        f_wait(1)

    for t in range(2):
        for p in range(2):
            out[2 * p + t] = FR[t, p].astype(F32)

    for p in range(4):
        core_copy(p).wait_send()
    for i in range(3):
        for p in range(2):
            x_copy(p, i).wait_send()
        z_copy(i).wait_send()
        x2_copy(i).wait_send()
        z2_copy(i).wait_send()


def reduce_grads(g):
    vm = pl.BlockSpec(memory_space=pltpu.VMEM)
    dma = pltpu.SemaphoreType.DMA
    rows, cols = g.shape[4:]
    t = (rows, cols)
    return pl.pallas_call(
        reduce_kernel,
        name="reduce",
        out_shape=jax.ShapeDtypeStruct((4,) + t, F32),
        in_specs=[vm],
        out_specs=vm,
        scratch_shapes=[
            pltpu.VMEM((4, 4, 2) + t, BF16),
            pltpu.VMEM((4, 4, 2) + t, BF16),
            pltpu.VMEM((3, 2, 2) + t, BF16),
            pltpu.VMEM((3, 4) + t, BF16),
            pltpu.VMEM((2, 2) + t, BF16),
            pltpu.VMEM((4,) + t, BF16),
            pltpu.VMEM((3,) + t, BF16),
            pltpu.VMEM((3,) + t, BF16),
            pltpu.VMEM((2,) + t, BF16),
            pltpu.VMEM((3, 2) + t, BF16),
            pltpu.VMEM((2,) + t, BF16),
            pltpu.VMEM((2, 2) + t, BF16),
            dma((4,)), dma((4,)),
            dma((2, 3)), dma((2, 3)),
            dma((3,)), dma((3,)),
            dma((3,)), dma((3,)),
            dma((3,)), dma((3,)),
            dma((3,)), dma((3,)),
            dma((3,)), dma((2,)),
        ],
        compiler_params=pltpu.CompilerParams(
            collective_id=2, has_side_effects=True, vmem_limit_bytes=60 << 20
        ),
        cost_estimate=pl.CostEstimate(flops=10**7, bytes_accessed=40 * 10**6, transcendentals=0),
    )(g)


def vision_forward(layer_in, packed_weight, output_weight, windows, norm_gain, merge_gain):
    patches = layer_in.shape[0]
    head_count = output_weight.shape[0] // HEAD_DIM
    widened = layer_in.astype(F32)
    normed = rms_scale(widened, norm_gain).astype(BF16)
    projected = jnp.dot(normed, packed_weight, preferred_element_type=F32).astype(BF16)
    triple = projected.reshape(patches, 3, head_count, HEAD_DIM).astype(F32)
    scores = jnp.einsum("qhd,khd->hqk", triple[:, 0], triple[:, 1]) * HEAD_DIM ** (-0.5)
    same_window = windows[:, None] == windows[None, :]
    scores = jnp.where(same_window[None], scores, -1e30)
    attention = jax.nn.softmax(scores, axis=-1).astype(BF16)
    combined = jnp.einsum("hqk,khd->qhd", attention.astype(F32), triple[:, 2])
    combined = combined.reshape(patches, head_count * HEAD_DIM).astype(BF16)
    output = widened + jnp.dot(combined, output_weight, preferred_element_type=F32)
    return rms_scale(output, merge_gain)


def vision_backward(
    layer_in, packed_weight, output_weight, windows, norm_gain, merge_gain, cotangent
):

    def forward(layer_arg, packed_arg, output_arg):
        return vision_forward(layer_arg, packed_arg, output_arg, windows, norm_gain, merge_gain)

    _, pullback = jax.vjp(forward, layer_in, packed_weight, output_weight)
    return pullback(cotangent.astype(F32))


def local(
    token_grads,
    token_dest,
    merger_down,
    merger_up,
    merger_pre,
    layer_input,
    window_ids,
    norm_gain,
    merge_gain,
    qkv_weight,
    proj_weight,
):
    cotangent, packed_full, output_full = merger(
        token_grads, token_dest.reshape(1, 64), merger_down, merger_up, merger_pre, qkv_weight, proj_weight
    )
    packed_full = packed_full.reshape(1280, 1920)
    output_full = output_full.reshape(640, 1280)
    layer_grad, packed_term, output_term = vision_backward(
        layer_input, packed_full, output_full, window_ids[0], norm_gain, merge_gain, cotangent
    )
    packed_term = packed_term.reshape(4, 2, 2, 80, 3, 640).transpose(2, 4, 0, 1, 3, 5)
    output_term = output_term.reshape(4, 2, 2, 40, 2, 640).transpose(2, 0, 1, 4, 3, 5)
    output_term = output_term.reshape(2, 1, 4, 2, 80, 640)
    sums = reduce_grads(jnp.concatenate([packed_term, output_term], axis=1))
    packed_sum = jnp.concatenate([sums[0], sums[1], sums[2]], axis=1)
    output_sum = jnp.concatenate([sums[3, :40], sums[3, 40:]], axis=1)
    return (layer_grad, packed_sum, output_sum)


def solution(mesh):
    return jax.shard_map(
        local,
        mesh=mesh,
        in_specs=(
            P(("dp", "llm"), None),
            P(("dp", "llm"), None),
            P("llm", None),
            P(None, "llm"),
            P("dp", "llm"),
            P(("dp", "llm"), None),
            P(("dp", "llm"), None),
            P(),
            P(),
            P("dp", None),
            P("dp", None),
        ),
        out_specs=(P(("dp", "llm"), None), P("dp", None), P("dp", None)),
        check_vma=False,
    )
```

time: 797 us -> 286 us (0.36)
  waiting for transfers between devices: 653 us -> 0 us
  Pallas kernels: 0 us -> 189 us
  matrix products: 90.9 us -> 45 us
  local copies, waits for them, and re-layouts: 14.4 us -> 33.1 us
  between operations: 14.4 us -> 1.02 us
    reduce_scatter x3 -> x0, waiting for transfers between devices: 335 us -> none  [the longest x1 194 us: local(): lax.psum_scatter(lax.dot_general(pre_grad, merger_up, (((1,), (1,)), ((),...]
    all_gather x3 -> x0, waiting for transfers between devices: 225 us -> none  [the longest x1 172 us: local(): lax.all_gather(token_grads, 'llm', axis=0, tiled=True)]
    pallas_call x0 -> x2, Pallas kernels: none -> 189 us  [the longest x1 129 us: merger(): pl.pallas_call(merger_kernel, name='merger', out_shape=(jax.ShapeDtypeStr...]
    psum x1 -> x0, waiting for transfers between devices: 76.8 us -> none  [local(): packed_sum, output_sum = lax.psum((summed_rows[0], summed_rows[1]), 'llm')]
    dot_general x11 -> x9, matrix products: 71.2 us -> 32.6 us  [the longest x3 17.4 us: vision_forward(): jnp.dot(normed, packed_weight, preferred_element_type=F32).astype(BF16)]
    reshape x0 -> x4, local copies, waits for them, and re-layouts: none -> 20.8 us  [the longest x2 17.1 us: local(): packed_term.reshape(4, 2, 2, 80, 3, 640).transpose(2, 4, 0, 1, 3, 5)]
    all_to_all x1 -> x0, waiting for transfers between devices: 14.8 us -> none  [local(): lax.all_to_all(outgoing, 'dp', split_axis=0, concat_axis=0, tiled=True)]
  transfers between devices with their start and end apart: 8 -> 0, of which waited for: 8 -> 0; matrix products, arithmetic and copies ran while one was open for 13% -> 0% of each run, Pallas kernels for 0% -> 0%
where the time goes in v1:
time: 286 us; the launch traced here: 285 us
  Pallas kernels  189 us (66%)
  matrix products  45 us (16%)
  local copies, waits for them, and re-layouts  33.1 us (12%)
  other arithmetic  16.8 us (6%)
    pallas_call x1, Pallas kernels, merger(): pl.pallas_call(merger_kernel, name='merger', out_shape=(jax.ShapeDtypeStr...  129 us
    pallas_call x1, Pallas kernels, reduce_grads(): pl.pallas_call(reduce_kernel, name='reduce', out_shape=jax.ShapeDtypeStru...  60.7 us
    dot_general x3, matrix products, vision_forward(): jnp.dot(normed, packed_weight, preferred_element_type=F32).astype(BF16)  17.4 us
    reshape x2, local copies, waits for them, and re-layouts, local(): packed_term.reshape(4, 2, 2, 80, 3, 640).transpose(2, 4, 0, 1, 3, 5)  17.1 us
    dot_general x3, matrix products, vision_forward(): combined = jnp.einsum('hqk,khd->qhd', attention.astype(F32), triple[:, 2])  9.45 us
    unnamed x60, local copies, waits for them, and re-layouts  7.16 us
    dot_general x2, matrix products, vision_forward(): jnp.einsum('qhd,khd->hqk', triple[:, 0], triple[:, 1]) * HEAD_DIM ** (-0.5)  6.97 us
    concatenate x1, other arithmetic, local(): sums = reduce_grads(jnp.concatenate([packed_term, output_term], axis=1))  5.8 us

profile of v1, /device:TPU:0, one launch (start us, length us, event | category | flops | bytes accessed | tf_op | source)
XLA Modules:
  0.0 285.4 jit_solution(7726401021732099597)
XLA Ops:
  0.6 0.0 copy-start.1
  0.6 0.0 copy-start.25
  0.7 128.7 %merger.1 = (bf16[512,1280]{1,0:T(8,128)(2,1)}, bf16[16,80,1920]{2,1,0:T(8,128)(2,1)}, bf16[16,40,1280]{2,1,0:T(8,128)(2,1)}) custom-call(bf16[64,8192]{1,0:T(8,128)(2,1)} %tok.1, s32[1,64]{1,0:T(1,128)} %bitcast.98, bf16[640,8192]{1,0:T(8,128)(2,1)} %down.1, bf16[5120,640]{1,0:T(8,128)(2,1)} %up.1, bf16[512,640]{1,0:T(8,128)(2,1)} %pre.1, ...), custom_call_target="tpu_custom_call" | custom-call | flops 8999999488 | bytes 40000000 | tf_op jit(solution)/shard_map/merger/pallas_call | solution.py:338
  129.3 0.0 copy-done.1
  129.4 0.3 fusion.14
  129.7 0.6 copy-done.14
  130.3 0.6 copy-done.19
  130.9 0.0 copy-done.25
  130.9 6.6 %convolution_convert_fusion.2 = bf16[512,1920]{1,0:T(8,128)(2,1)} fusion(bf16[1280,1920]{1,0:T(8,128)(2,1)} %bitcast.99, bf16[512,1280]{1,0:T(8,128)(2,1)S(1)} %copy-done.1, f32[1280]{0:T(1024)S(1)} %copy-done.25, f32[512]{0:T(512)S(1)} %fusion.23), kind=kOutput, calls=%fused_computation.28 | convolution fusion | flops 2520186880 | bytes 8199168 | tf_op jit(solution)/shard_map/jvp()/dot_general | solution.py:569
  137.5 2.7 copy.23
  140.2 0.0 copy-done.18
  140.2 0.2 broadcast_compare_fusion
  140.4 5.5 %fusion.29 = (f32[8,512]{1,0:T(8,128)S(1)}, f32[8,512,512]{1,2,0:T(8,128)}) fusion(pred[512,512]{0,1:T(8,128)(4,1)S(1)} %broadcast_compare_fusion, bf16[512,3,8,80]{0,3,2,1:T(8,128)(2,1)S(1)} %bitcast.88), kind=kOutput, calls=%fused_computation.68 | convolution fusion | flops 343933440 | bytes 9977856 | tf_op jit(solution)/shard_map/jvp()/sub | solution.py:574
  145.9 4.6 %divide_convert_fusion = bf16[8,512,512]{1,2,0:T(8,128)(2,1)S(1)} fusion(f32[8,512,512]{1,2,0:T(8,128)} %get-tuple-element.19, f32[8,512]{1,0:T(8,128)S(1)} %get-tuple-element.18), kind=kLoop, calls=%fused_computation.9 | loop fusion | flops 4194304 | bytes 12599296 | tf_op jit(solution)/shard_map/jvp()/convert_element_type | solution.py:574
  150.5 0.0 copy-start
  150.5 0.0 copy-start.2
  150.5 0.0 copy-start.9
  150.5 0.0 copy-start.16
  150.5 0.0 copy-start.27
  150.6 0.8 convolution_convert_fusion.6
  151.4 1.2 copy-done
  152.6 0.2 copy-done.2
  152.8 1.2 copy-done.9
  154.0 0.5 copy-done.27
  154.5 1.8 multiply_reduce_fusion.1
  156.3 0.0 copy-start.4
  156.3 0.0 copy-start.23
  156.3 1.5 copy-done.4
  157.8 0.0 copy-done.23
  157.8 1.5 convolution_convert_fusion.5
  159.3 0.3 copy.25
  159.6 0.0 slice-start
  159.6 3.7 %convolution_bitcast_fusion.2 = f32[512,1,8,80]{0,3,2,1:T(8,128)S(1)} fusion(bf16[8,80,512]{2,1,0:T(8,128)(2,1)S(1)} %bitcast.86, bf16[8,512,512]{1,2,0:T(8,128)(2,1)} %copy-done), kind=kOutput, calls=%fused_computation.43 | convolution fusion | flops 335544320 | bytes 6160384 | tf_op jit(solution)/shard_map/transpose(jvp(hqk,khd->qhd))/dot_general | solution.py:575
  163.3 0.0 slice-start.1
  163.4 4.9 %fusion.6 = (f32[8,512]{1,0:T(8,128)S(1)}, bf16[8,512,512]{1,2,0:T(8,128)(2,1)S(1)}) fusion(f32[8,512,512]{1,2,0:T(8,128)} %get-tuple-element.19, f32[8,512]{1,0:T(8,128)S(1)} %multiply_divide_fusion, bf16[8,80,512]{2,1,0:T(8,128)(2,1)S(1)} %bitcast.87, bf16[512,3,8,80]{0,3,2,1:T(8,128)(2,1)S(1)} %bitcast.90), kind=kOutput, calls=%fused_computation.8 | convolution fusion | flops 346025984 | bytes 13926400 | tf_op jit(solution)/shard_map/transpose(jvp(hqk,khd->qhd))/dot_general | solution.py:575
  168.3 0.0 slice-done
  168.3 0.0 slice-done.1
  168.3 3.7 %convolution_bitcast_fusion.1 = f32[512,1,8,80]{0,3,2,1:T(8,128)} fusion(bf16[512,3,8,80]{0,3,2,1:T(8,128)(2,1)S(1)} %bitcast.91, f32[8,512,512]{1,2,0:T(8,128)S(1)} %bitcast.83, bf16[8,512,512]{1,2,0:T(8,128)(2,1)S(1)} %get-tuple-element.22, f32[8,512]{1,0:T(8,128)S(1)} %neg.6, f32[8,512]{1,0:T(8,128)S(1)} %get-tuple-element.18, ...), kind=kOutput, calls=%fused_computation.42 | convolution fusion | flops 348127232 | bytes 14843904 | tf_op jit(solution)/shard_map/transpose(jvp(qhd,khd->hqk))/dot_general | solution.py:571
  172.0 3.3 %convolution_bitcast_fusion = f32[512,1,8,80]{0,3,2,1:T(8,128)} fusion(bf16[512,3,8,80]{0,3,2,1:T(8,128)(2,1)S(1)} %bitcast.92, f32[8,512,512]{1,2,0:T(8,128)S(1)} %bitcast.83, bf16[8,512,512]{1,2,0:T(8,128)(2,1)S(1)} %get-tuple-element.22, f32[8,512]{1,0:T(8,128)S(1)} %neg.6, f32[8,512]{1,0:T(8,128)S(1)} %get-tuple-element.18, ...), kind=kOutput, calls=%fused_computation.41 | convolution fusion | flops 348127232 | bytes 14843904 | tf_op jit(solution)/shard_map/transpose(jvp(qhd,khd->hqk))/dot_general | solution.py:571
  175.3 2.1 add_convert_fusion
  177.4 1.3 copy-done.7
  178.7 0.0 copy-done.20
  178.7 5.0 %convolution_convert_fusion = bf16[1280,1920]{1,0:T(8,128)(2,1)} fusion(bf16[512,1920]{0,1:T(8,128)(2,1)S(1)} %bitcast.93, bf16[512,1280]{1,0:T(8,128)(2,1)S(1)} %copy-done.3, f32[1280]{0:T(1024)S(1)} %copy-done.26, f32[512]{0:T(512)S(1)} %copy-done.20), kind=kOutput, calls=%fused_computation.12 | convolution fusion | flops 2521661440 | bytes 8199168 | tf_op jit(solution)/shard_map/transpose(jvp())/dot_general | solution.py:569
  183.7 11.1 %reshape.118 = bf16[4,2,2,80,3,640]{5,4,3,2,1,0:T(4,128)(2,1)} reshape(bf16[1280,1920]{1,0:T(8,128)(2,1)} %convolution_convert_fusion) | data formatting | bytes 9830400 | tf_op jit(solution)/shard_map/reshape | solution.py:613
  194.9 0.0 copy-start.17
  194.9 0.0 copy-start.22
  194.9 0.0 copy-start.24
  194.9 5.9 %copy.36 = bf16[4,2,2,80,3,640]{5,3,1,0,4,2:T(8,128)(2,1)} copy(bf16[4,2,2,80,3,640]{5,4,3,2,1,0:T(4,128)(2,1)} %reshape.118) | data formatting | bytes 9830400 | tf_op jit(solution)/shard_map/reshape | solution.py:613
  200.8 0.0 copy-done.13
  200.8 0.0 copy-done.17
  200.8 0.0 copy-done.22
  200.9 0.0 copy-done.24
  200.9 2.5 convolution_convert_fusion.1
  203.4 3.5 %reshape.119 = bf16[4,2,2,40,2,640]{5,4,3,2,1,0:T(2,128)(2,1)S(1)} reshape(bf16[640,1280]{1,0:T(8,128)(2,1)} %convolution_convert_fusion.1) | data formatting | bytes 3276800 | tf_op jit(solution)/shard_map/reshape | solution.py:614
  206.9 0.2 copy.30
  207.1 5.8 %pad_maximum_fusion.g = bf16[2,4,4,2,80,640]{5,4,3,2,1,0:T(8,128)(2,1)} fusion(bf16[2,1,4,2,80,640]{5,4,3,2,1,0:T(8,128)(2,1)S(1)} %bitcast.85, bf16[2,3,4,2,80,640]{5,4,3,2,1,0:T(8,128)(2,1)} %bitcast.84), kind=kLoop, calls=%fused_computation.13 | loop fusion | flops 3276800 | bytes 13107200 | tf_op jit(solution)/shard_map/concatenate | solution.py:616
  212.9 60.7 %reduce.1 = f32[4,80,640]{2,1,0:T(8,128)} custom-call(bf16[2,4,4,2,80,640]{5,4,3,2,1,0:T(8,128)(2,1)} %pad_maximum_fusion.g), custom_call_target="tpu_custom_call" | custom-call | flops 10000000 | bytes 40000000 | tf_op jit(solution)/shard_map/reduce/pallas_call | solution.py:530
  273.6 0.0 copy-start.8
  273.6 1.1 slice_bitcast_fusion.21
  274.7 0.7 pad_maximum_fusion.2
  275.4 1.2 slice_bitcast_fusion.19
  276.5 0.9 pad_maximum_fusion.1
  277.4 5.7 %fusion.17 = (f32[512]{0:T(512)S(1)}, f32[512,1280]{1,0:T(8,128)S(1)}) fusion(bf16[512,1280]{1,0:T(8,128)(2,1)S(1)} %copy-done.3, f32[1280]{0:T(1024)S(1)} %copy-done.26, bf16[512,1920]{0,1:T(8,128)(2,1)S(1)} %bitcast.94, bf16[1280,1920]{1,0:T(8,128)(2,1)} %bitcast.100), kind=kOutput, calls=%fused_computation.37 | convolution fusion | flops 2520514048 | bytes 10820608 | tf_op jit(solution)/shard_map/transpose(jvp())/dot_general | solution.py:569
  283.2 2.2 fusion.13
  (32 shorter events, 0.1 us)
Async XLA Ops:
  0.6 128.7 %copy-start.1 = (bf16[512,1280]{1,0:T(8,128)(2,1)S(1)}, bf16[512,1280]{1,0:T(8,128)(2,1)}, u32[]{:S(2)}) copy-start(bf16[512,1280]{1,0:T(8,128)(2,1)} %param.16) | copy-start | bytes 3932164
  0.6 130.2 %copy-start.25 = (f32[1280]{0:T(1024)S(1)}, f32[1280]{0:T(1024)}, u32[]{:S(2)}) copy-start(f32[1280]{0:T(1024)} %param.18) | copy-start | bytes 15364
  129.7 0.6 copy-start.14
  130.3 0.6 copy-start.19
  137.5 2.7 copy-start.18
  150.5 2.1 copy-start
  150.5 2.3 copy-start.2
  150.5 3.5 %copy-start.9 = (bf16[512,1280]{1,0:T(8,128)(2,1)S(1)}, bf16[512,1280]{1,0:T(8,128)(2,1)}, u32[]{:S(2)}) copy-start(bf16[512,1280]{1,0:T(8,128)(2,1)} %get-tuple-element.6) | copy-start | bytes 3932164
  150.5 3.4 %copy-start.16 = (f32[1280]{0:T(1024)S(1)}, f32[1280]{0:T(1024)}, u32[]{:S(2)}) copy-start(f32[1280]{0:T(1024)} %param.19) | copy-start | bytes 15364
  150.5 4.0 %copy-start.27 = (bf16[16,40,1280]{2,1,0:T(8,128)(2,1)S(1)}, bf16[16,40,1280]{2,1,0:T(8,128)(2,1)}, u32[]{:S(2)}) copy-start(bf16[16,40,1280]{2,1,0:T(8,128)(2,1)} %get-tuple-element.8) | copy-start | bytes 4915204
  152.6 3.6 %copy-start.12 = (bf16[8,80,512]{2,1,0:T(8,128)(2,1)}, bf16[8,80,512]{2,1,0:T(8,128)(2,1)S(1)}, u32[]{:S(2)}) copy-start(bf16[8,80,512]{2,1,0:T(8,128)(2,1)S(1)} %convolution_convert_fusion.6) | copy-start | bytes 1966084
  156.3 1.6 copy-start.4
  156.3 1.5 copy-start.21
  156.3 1.5 copy-start.23
  159.6 8.7 %slice-start = ((s8[8388608]{0:T(1024)(128)(4,1)}), s8[4194304]{0:T(1024)(128)(4,1)S(1)}, s32[]{:S(2)}) async-start(s8[8388608]{0:T(1024)(128)(4,1)} %bitcast.82), calls=%async_computation | async-start | bytes 8388608
  163.3 4.9 %slice-start.1 = ((s8[8388608]{0:T(1024)(128)(4,1)}), s8[4194304]{0:T(1024)(128)(4,1)S(1)}, s32[]{:S(2)}) async-start(s8[8388608]{0:T(1024)(128)(4,1)} %bitcast.82), calls=%async_computation.1 | async-start | bytes 8388608
  175.3 3.4 %copy-start.3 = (bf16[512,1280]{1,0:T(8,128)(2,1)S(1)}, bf16[512,1280]{1,0:T(8,128)(2,1)}, u32[]{:S(2)}) copy-start(bf16[512,1280]{1,0:T(8,128)(2,1)} %param.16) | copy-start | bytes 3932164
  175.3 3.4 %copy-start.20 = (f32[512]{0:T(512)S(1)}, f32[512]{0:T(512)}, u32[]{:S(2)}) copy-start(f32[512]{0:T(512)} %copy-done.19) | copy-start | bytes 6148
  175.3 3.4 %copy-start.26 = (f32[1280]{0:T(1024)S(1)}, f32[1280]{0:T(1024)}, u32[]{:S(2)}) copy-start(f32[1280]{0:T(1024)} %param.18) | copy-start | bytes 15364
  177.4 1.3 copy-start.7
  194.8 6.0 %copy-start.5 = (f32[512,1280]{1,0:T(8,128)S(1)}, f32[512,1280]{1,0:T(8,128)}, u32[]{:S(2)}) copy-start(f32[512,1280]{1,0:T(8,128)} %copy-done.4) | copy-start | bytes 7864324
  194.8 6.0 %copy-start.10 = (bf16[512,1280]{1,0:T(8,128)(2,1)S(1)}, bf16[512,1280]{1,0:T(8,128)(2,1)}, u32[]{:S(2)}) copy-start(bf16[512,1280]{1,0:T(8,128)(2,1)} %get-tuple-element.6) | copy-start | bytes 3932164
  194.8 6.0 %copy-start.13 = (bf16[8,80,512]{2,1,0:T(8,128)(2,1)S(1)}, bf16[8,80,512]{2,1,0:T(8,128)(2,1)}, u32[]{:S(2)}) copy-start(bf16[8,80,512]{2,1,0:T(8,128)(2,1)} %copy-done.12) | copy-start | bytes 1966084
  194.9 6.0 %copy-start.17 = (f32[1280]{0:T(1024)S(1)}, f32[1280]{0:T(1024)}, u32[]{:S(2)}) copy-start(f32[1280]{0:T(1024)} %param.19) | copy-start | bytes 15364
  194.9 6.0 %copy-start.22 = (f32[512]{0:T(512)S(1)}, f32[512]{0:T(512)}, u32[]{:S(2)}) copy-start(f32[512]{0:T(512)} %copy-done.21) | copy-start | bytes 6148
  194.9 6.0 %copy-start.24 = (f32[512]{0:T(512)S(1)}, f32[512]{0:T(512)}, u32[]{:S(2)}) copy-start(f32[512]{0:T(512)} %copy-done.23) | copy-start | bytes 6148
  273.6 3.8 %copy-start.8 = (bf16[512,3,8,80]{0,3,2,1:T(8,128)(2,1)S(1)}, bf16[512,3,8,80]{0,3,2,1:T(8,128)(2,1)}, u32[]{:S(2)}) copy-start(bf16[512,3,8,80]{0,3,2,1:T(8,128)(2,1)} %copy-done.7) | copy-start | bytes 5898244
  277.4 5.7 %copy-start.15 = (f32[512]{0:T(512)S(1)}, f32[512]{0:T(512)}, u32[]{:S(2)}) copy-start(f32[512]{0:T(512)} %copy-done.14) | copy-start | bytes 6148
  277.4 5.7 %copy-start.6 = (f32[512,1280]{1,0:T(8,128)S(1)}, f32[512,1280]{1,0:T(8,128)}, u32[]{:S(2)}) copy-start(f32[512,1280]{1,0:T(8,128)} %copy-done.4) | copy-start | bytes 7864324
  277.4 5.7 %copy-start.11 = (bf16[512,1280]{1,0:T(8,128)(2,1)S(1)}, bf16[512,1280]{1,0:T(8,128)(2,1)}, u32[]{:S(2)}) copy-start(bf16[512,1280]{1,0:T(8,128)(2,1)} %get-tuple-element.6) | copy-start | bytes 3932164

commit v2 on v1

--- a/solution.py
+++ b/solution.py
@@ -30,6 +30,16 @@
     return values * lax.rsqrt(jnp.mean(values * values, axis=-1, keepdims=True) + EPSILON) * scaling
 
 
+KEYS = (0, 64, 192, 256)
+
+
+def head_lanes(h):
+    start = 128 * jnp.minimum(5 * h // 8, 3)
+    lane = lax.broadcasted_iota(jnp.int32, (1, 256), 1) + start
+    mask = ((lane >= HEAD_DIM * h) & (lane < HEAD_DIM * h + HEAD_DIM)).astype(F32).astype(BF16)
+    return pl.ds(pl.multiple_of(start, 128), 256), mask
+
+
 def place():
     d, l = lax.axis_index("dp"), lax.axis_index("llm")
     return d // 4, (d // 2) % 2, d % 2, l // 2, l % 2
@@ -53,11 +63,12 @@
 
 
 def merger_kernel(
-    tok, dest, down, up, pre, qw, ow,
-    cot, wq, wo,
-    G, down_v, up_v, slope, acc, pg, pre2,
+    tok, dest, down, up, pre, qw, ow, xin, win, ng, mg,
+    cot_o, wq_o, wo_o, normt_o, proj_o, prob_o, combt_o, n2_o, r2_o,
+    G, down_v, slope, acc, pg, pre2,
     S, R, own, T, T0, ZR, M, OUT, A,
-    loc, zs, zr, ys, yr, ps, pr, ws, wr, xs, xr, cs, cr, rys, ryr, rzs, rzr, as_, ar,
+    cot, wq, wo, wo2, norm, normt, proj, prob, combt, n2, r2, bias,
+    loc, dsem, outs, zs, zr, ys, yr, ps, pr, ws, wr, xs, xr, cs, cr, rys, ryr, rzs, rzr, as_, ar,
 ):
     x, yh, c, z, yl = place()
     d = (x * 2 + yh) * 2 + c
@@ -71,11 +82,9 @@
     dps = [((d + s) % 16, l) for s in range(1, 16)]
 
     cp_tok = pltpu.make_async_copy(tok, G.at[0, pl.ds(0, 64)], loc.at[0])
-    cp_down = pltpu.make_async_copy(down, down_v, loc.at[1])
-    cp_up = pltpu.make_async_copy(up, up_v, loc.at[2])
     cp_tok.start()
-    cp_down.start()
-    cp_up.start()
+    for k in range(4):
+        pltpu.make_async_copy(down.at[:, pl.ds(1024 * k, 1024)], down_v.at[k], dsem.at[k]).start()
     greet(zp + [p1, p2] + dps)
     cp_tok.wait()
 
@@ -83,6 +92,15 @@
 
     def col(k):
         return pl.ds(pl.multiple_of(k * W, W), W)
+
+    def down_copy(k):
+        return pltpu.make_async_copy(down.at[:, col(k)], down_v.at[k % 4], dsem.at[k % 4])
+
+    V = M.shape[2]
+
+    def up_copy(f):
+        rows = pl.ds(pl.multiple_of(f * V, V), V)
+        return pltpu.make_async_copy(up.at[rows], down_v.at[f % 4, :, pl.ds(0, V)], dsem.at[f % 4])
 
     def z_copy(k, i):
         return remote(
@@ -131,25 +149,89 @@
     for cp in w_copies((qw, ow), d, cs.at[0], cr.at[0], core):
         cp.start()
 
+    def emit(n, source, target):
+        return pltpu.make_async_copy(source, target, outs.at[n])
+
+    def slope_step(k):
+        r = k // 2
+        zz = (z + r) % 4
+
+        @pl.when(k % 2 == 0)
+        def _():
+            mine = pre[pl.ds(pl.multiple_of((2 * zz + yl) * 64, 64), 64), :]
+            slope[r, 0:64, :] = gelu_slope(mine.astype(F32))
+
+        @pl.when(k % 2 == 1)
+        def _():
+            first = pre[pl.ds(pl.multiple_of((2 * zz + 1 - yl) * 64, 64), 32), :]
+            second = pre2[pl.ds(pl.multiple_of(zz * 32, 32), 32), :]
+            slope[r, 64:96, :] = gelu_slope(first.astype(F32))
+            slope[r, 96:128, :] = gelu_slope(second.astype(F32))
+
+    def norm_step(k):
+        rows = pl.ds(pl.multiple_of(k * 64, 64), 64)
+        norm[rows, :] = rms_scale(xin[rows, :].astype(F32), ng[...]).astype(BF16)
+
+    def bias_step():
+        for b in range(4):
+            queries = jnp.broadcast_to(win[:, 128 * b : 128 * b + 128].astype(F32), (128, 128)).T
+            for h in range(2):
+                keys = win[:, KEYS[b] + 128 * h : KEYS[b] + 128 * h + 128].astype(F32)
+                bias[b, :, 128 * h : 128 * h + 128] = jnp.where(queries == keys, 0.0, -1e30)
+
+    def qkv_step(p, carry):
+        cols = pl.ds(pl.multiple_of(p * 640, 128), 640)
+        weight = wq[:, :, cols].reshape(1280, 640)
+        proj[p] = jnp.dot(norm[...], weight, preferred_element_type=F32).astype(BF16)
+        return carry
+
+    def head_step(h):
+        lanes, mask = head_lanes(h)
+        for b in range(4):
+            rows, keys = pl.ds(128 * b, 128), pl.ds(KEYS[b], 256)
+            scores = lax.dot_general(
+                proj[0, rows, lanes] * mask, proj[1, keys, lanes], NT, preferred_element_type=F32
+            )
+            scores = scores * HEAD_DIM ** (-0.5) + bias[b]
+            powers = jnp.exp(scores - jnp.max(scores, axis=-1, keepdims=True))
+            share = (powers / jnp.sum(powers, axis=-1, keepdims=True)).astype(BF16)
+            prob[h, b] = share
+            combf[rows, lanes] += jnp.dot(share, proj[2, keys, lanes] * mask, preferred_element_type=F32)
+
+    def output_step():
+        comb = combf[...].astype(BF16)
+        combt[...] = combf[...].T.astype(BF16)
+        emit(6, combt, combt_o).start()
+        for t in range(4):
+            rows = pl.ds(128 * t, 128)
+            value = xin[rows, :].astype(F32) + jnp.dot(
+                comb[128 * t : 128 * t + 128], wo2[...], preferred_element_type=F32
+            )
+            factor = lax.rsqrt(jnp.mean(value * value, axis=-1, keepdims=True) + EPSILON)
+            n2[rows, :] = value * factor
+            r2[rows, :] = factor
+        emit(7, n2, n2_o).start()
+        emit(8, r2, r2_o).start()
+
     for zz in range(4):
         pre_copy(zz).wait_recv()
-    for r in range(4):
-        zz = (z + r) % 4
-        mine = pre[pl.ds(pl.multiple_of((2 * zz + yl) * 64, 64), 64), :]
-        first = pre[pl.ds(pl.multiple_of((2 * zz + 1 - yl) * 64, 64), 32), :]
-        second = pre2[pl.ds(pl.multiple_of(zz * 32, 32), 32), :]
-        slope[r, 0:64, :] = gelu_slope(mine.astype(F32))
-        slope[r, 64:96, :] = gelu_slope(first.astype(F32))
-        slope[r, 96:128, :] = gelu_slope(second.astype(F32))
     acc[...] = jnp.zeros_like(acc)
 
     def multiply(k):
         for i in range(2):
             y_copy(k, i).wait_recv()
         tile = G[:, :, col(k)].reshape(512, W)
-        acc[...] += lax.dot_general(tile, down_v[:, col(k)], NT, preferred_element_type=F32)
-
-    cp_down.wait()
+        down_copy(k).wait()
+        acc[...] += lax.dot_general(tile, down_v[k % 4], NT, preferred_element_type=F32)
+
+        @pl.when(k + 4 < N_TOK)
+        def _():
+            down_copy(k + 4).start()
+
+        @pl.when(k >= 4)
+        def _():
+            up_copy(k - 4).start()
+
 
     def gather_step(k, carry):
         @pl.when(k + 2 < N_TOK)
@@ -176,10 +258,13 @@
         def _():
             multiply(k - 1)
 
+        slope_step(k)
+        norm_step(k)
         return carry
 
     lax.fori_loop(0, N_TOK, gather_step, 0)
-    multiply(N_TOK - 1)
+    bias_step()
+    multiply(jnp.int32(N_TOK - 1))
 
     def x_arrive(h):
         for i in range(3):
@@ -190,10 +275,9 @@
             for cp in w_copies(None, other, cs.at[2 + 3 * h + i], cr.at[2 + 3 * h + i], core):
                 cp.start()
 
-    x_arrive(0)
-
     pg[...] = (acc[...] * slope[...].reshape(512, slope.shape[2])).astype(BF16)
-    cp_up.wait()
+    combf = acc
+    combf[...] = jnp.zeros_like(combf)
 
     token = dest[...]
     hot = (lax.broadcasted_iota(jnp.int32, (16, 64), 0) == token).astype(F32)
@@ -207,8 +291,6 @@
         [(row == target).astype(F32), (row == target + 8).astype(F32)], axis=1
     ).astype(BF16)
 
-    V = M.shape[2]
-
     def ry_copy(f, i):
         return remote(S.at[f, i], R.at[f, i], rys.at[f, i], ryr.at[f, i], (p1, p2)[i])
 
@@ -225,53 +307,102 @@
             dps[s - 1],
         )
 
-    def sum_step(i, carry):
-        @pl.when(i < N_FEAT)
-        def _():
-            rows = pl.ds(pl.multiple_of(i * V, V), V)
-            part = lax.dot_general(pg[...], up_v[rows, :], NT, preferred_element_type=F32)
-            part = part.reshape(4, 128, V)
-            S[i, 0] = part[:, 64:96, :].astype(BF16)
-            S[i, 1] = part[:, 96:128, :].astype(BF16)
-            for h in range(2):
-                ry_copy(i, h).start()
-            own[i % 2] = part[:, 0:64, :]
-
-        @pl.when((i >= 1) & (i < N_FEAT + 1))
-        def _():
-            f = i - 1
-            for h in range(2):
-                ry_copy(f, h).wait_recv()
-            total = own[f % 2] + jnp.concatenate([R[f, 0].astype(F32), R[f, 1].astype(F32)], axis=1)
-            T[f] = total[1:4].astype(BF16)
-            T0[f % 2] = total[0]
-            for h in (0, 2, 1):
-                rz_copy(f, h).start()
-
-        @pl.when(i >= 2)
-        def _():
-            f = i - 2
-            for h in range(3):
-                rz_copy(f, h).wait_recv()
-            M[f] = (
-                T0[f % 2] + ZR[f, 0].astype(F32) + ZR[f, 1].astype(F32) + ZR[f, 2].astype(F32)
-            ).astype(BF16)
-
-            @pl.when(f % 2 == 1)
-            def _():
-                j = f // 2
-                both = jnp.concatenate([M[f - 1], M[f]], axis=0)
-                OUT[j] = jnp.dot(placing, both, preferred_element_type=F32).astype(BF16)
-                for s in range(1, 16):
-                    a_copy(j, s).start()
-                here = pl.ds(pl.multiple_of(d * 16, 16), 16)
-                A[j, here, :] = OUT[j, here, :]
-
-        return carry
-
-    lax.fori_loop(0, N_FEAT + 2, sum_step, 0)
-
+    cidx = [d, d2]
+    for h in range(2):
+        for i in range(3):
+            other = ((x + i + 1) % 4 * 2 + yh) * 2 + c
+            cidx.append(flipped(other) if h else other)
+
+    def weights_arrive():
+        for n, index in enumerate(cidx):
+            for cp in w_copies(None, index + 1 - 2 * c, cs.at[n], cr.at[n], core):
+                cp.wait_recv()
+        wo2[...] = wo[...].astype(F32).reshape(wo2.shape).astype(BF16)
+        emit(1, wq, wq_o).start()
+        emit(2, wo2, wo_o).start()
+
+    def first_product(i):
+        up_copy(i).wait()
+        part = lax.dot_general(pg[...], down_v[i % 4, :, 0:V], NT, preferred_element_type=F32)
+
+        @pl.when(i + 4 < N_FEAT)
+        def _():
+            up_copy(i + 4).start()
+
+        part = part.reshape(4, 128, V)
+        S[i, 0] = part[:, 64:96, :].astype(BF16)
+        S[i, 1] = part[:, 96:128, :].astype(BF16)
+        for h in range(2):
+            ry_copy(i, h).start()
+        own[i % 4] = part[:, 0:64, :]
+
+    def over_y(f):
+        for h in range(2):
+            ry_copy(f, h).wait_recv()
+        total = own[f % 4] + jnp.concatenate([R[f, 0].astype(F32), R[f, 1].astype(F32)], axis=1)
+        T[f] = total[1:4].astype(BF16)
+        T0[f % 2] = total[0]
+        for h in (0, 2, 1):
+            rz_copy(f, h).start()
+
+    def over_z(f):
+        for h in range(3):
+            rz_copy(f, h).wait_recv()
+        M[f] = (
+            T0[f % 2] + ZR[f, 0].astype(F32) + ZR[f, 1].astype(F32) + ZR[f, 2].astype(F32)
+        ).astype(BF16)
+
+    def send_rows(j):
+        both = jnp.concatenate([M[2 * j], M[2 * j + 1]], axis=0)
+        OUT[j] = jnp.dot(placing, both, preferred_element_type=F32).astype(BF16)
+        for s in range(1, 16):
+            a_copy(j, s).start()
+        here = pl.ds(pl.multiple_of(d * 16, 16), 16)
+        A[j, here, :] = OUT[j, here, :]
+
+    def open_step(i, carry):
+        first_product(i)
+        return carry
+
+    lax.fori_loop(0, 3, open_step, 0)
+    x_arrive(0)
     x_arrive(1)
+
+    def sum_step(f, carry):
+        over_y(f)
+
+        @pl.when(f + 3 < N_FEAT)
+        def _():
+            first_product(f + 3)
+
+        @pl.when(f >= 1)
+        def _():
+            over_z(f - 1)
+
+        @pl.when((f >= 2) & (f % 2 == 0))
+        def _():
+            send_rows(f // 2 - 1)
+
+        @pl.when(f == 0)
+        def _():
+            weights_arrive()
+            lax.fori_loop(0, 3, qkv_step, 0)
+            emit(4, proj, proj_o).start()
+
+        @pl.when(f >= 1)
+        def _():
+            head_step(f - 1)
+
+        return carry
+
+    lax.fori_loop(0, N_FEAT, sum_step, 0)
+    head_step(7)
+    emit(5, prob, prob_o).start()
+    over_z(N_FEAT - 1)
+    send_rows(3)
+    normt[...] = norm[...].astype(F32).T.astype(BF16)
+    emit(3, normt, normt_o).start()
+    output_step()
 
     fifteen = pl.ds(0, 240)
     for j in range(4):
@@ -286,18 +417,11 @@
             cot[128 * g : 128 * g + 128, V * h : V * h + V] = jnp.dot(
                 order, stacked, preferred_element_type=F32
             ).astype(BF16)
-
-    cidx = [d, d2]
-    for h in range(2):
-        for i in range(3):
-            other = ((x + i + 1) % 4 * 2 + yh) * 2 + c
-            cidx.append(flipped(other) if h else other)
+    emit(0, cot, cot_o).start()
+
     for n, index in enumerate(cidx):
         for cp in w_copies(None, index, cs.at[n], cr.at[n], core):
             cp.wait_send()
-        theirs = index + 1 - 2 * c
-        for cp in w_copies(None, theirs, cs.at[n], cr.at[n], core):
-            cp.wait_recv()
     for cp in w_copies((qw, ow), d, ws.at[0], wr.at[0], p2):
         cp.wait_send()
     for h in range(2):
@@ -326,43 +450,69 @@
     lax.fori_loop(0, N_FEAT, drain2, 0)
     for j in range(4):
         pltpu.make_async_copy(OUT.at[j, fifteen], OUT.at[j, fifteen], as_.at[j]).wait()
-
-
-def merger(tok, dest, down, up, pre, qw, ow):
+    pairs = [
+        (cot, cot_o), (wq, wq_o), (wo2, wo_o), (normt, normt_o), (proj, proj_o),
+        (prob, prob_o), (combt, combt_o), (n2, n2_o), (r2, r2_o),
+    ]
+    for n, (source, target) in enumerate(pairs):
+        emit(n, source, target).wait()
+
+
+def merger(tok, dest, down, up, pre, qw, ow, xin, win, ng, mg):
     vm = pl.BlockSpec(memory_space=pltpu.VMEM)
     hbm = pl.BlockSpec(memory_space=pl.ANY)
     dma = pltpu.SemaphoreType.DMA
     hid = pre.shape[1]
     feat = up.shape[0]
     V = feat // N_FEAT
+    kept = [
+        ((512, 1280), BF16),
+        ((16,) + qw.shape, BF16),
+        ((640, 1280), BF16),
+        ((1280, 512), BF16),
+        ((3, 512, 640), BF16),
+        ((8, 4, 128, 256), BF16),
+        ((640, 512), BF16),
+        ((512, 1280), F32),
+        ((512, 1), F32),
+    ]
     return pl.pallas_call(
         merger_kernel,
         name="merger",
-        out_shape=(
-            jax.ShapeDtypeStruct((512, feat // 4), BF16),
-            jax.ShapeDtypeStruct((16,) + qw.shape, BF16),
-            jax.ShapeDtypeStruct((16,) + ow.shape, BF16),
-        ),
-        in_specs=[hbm, vm, hbm, hbm, vm, vm, vm],
-        out_specs=(vm, vm, vm),
+        out_shape=tuple(jax.ShapeDtypeStruct(*k) for k in kept),
+        in_specs=[hbm, vm, hbm, hbm, vm, vm, vm, vm, vm, vm, vm],
+        out_specs=(hbm,) * len(kept),
         scratch_shapes=[
             pltpu.VMEM((4, 128, tok.shape[1]), BF16),
-            pltpu.VMEM(down.shape, BF16),
-            pltpu.VMEM(up.shape, BF16),
+            pltpu.VMEM((4, 640, 1024), BF16),
             pltpu.VMEM((4, 128, hid), F32),
             pltpu.VMEM((512, hid), F32),
             pltpu.VMEM((512, hid), BF16),
             pltpu.VMEM((128, hid), BF16),
             pltpu.VMEM((N_FEAT, 2, 4, 32, V), BF16),
             pltpu.VMEM((N_FEAT, 2, 4, 32, V), BF16),
-            pltpu.VMEM((2, 4, 64, V), F32),
+            pltpu.VMEM((4, 4, 64, V), F32),
             pltpu.VMEM((N_FEAT, 3, 64, V), BF16),
             pltpu.VMEM((2, 64, V), F32),
             pltpu.VMEM((N_FEAT, 3, 64, V), BF16),
             pltpu.VMEM((N_FEAT, 64, V), BF16),
             pltpu.VMEM((4, 256, V), BF16),
             pltpu.VMEM((4, 256, V), BF16),
-            dma((3,)),
+            pltpu.VMEM((512, 1280), BF16),
+            pltpu.VMEM((16,) + qw.shape, BF16),
+            pltpu.VMEM((16,) + ow.shape, BF16),
+            pltpu.VMEM((640, 1280), BF16),
+            pltpu.VMEM((512, 1280), BF16),
+            pltpu.VMEM((1280, 512), BF16),
+            pltpu.VMEM((3, 512, 640), BF16),
+            pltpu.VMEM((8, 4, 128, 256), BF16),
+            pltpu.VMEM((640, 512), BF16),
+            pltpu.VMEM((512, 1280), F32),
+            pltpu.VMEM((512, 1), F32),
+            pltpu.VMEM((4, 128, 256), F32),
+            dma((1,)),
+            dma((4,)),
+            dma((9,)),
             dma((N_TOK, 3)), dma((N_TOK, 3)), dma((N_TOK, 2)), dma((N_TOK, 2)),
             dma((4,)), dma((4,)),
             dma((1, 2)), dma((1, 2)),
@@ -373,18 +523,28 @@
             dma((4,)), dma((4,)),
         ],
         compiler_params=pltpu.CompilerParams(
-            collective_id=1, has_side_effects=True, vmem_limit_bytes=60 << 20
+            collective_id=1, has_side_effects=True, vmem_limit_bytes=62 << 20
         ),
         cost_estimate=pl.CostEstimate(flops=9 * 10**9, bytes_accessed=40 * 10**6, transcendentals=0),
-    )(tok, dest, down, up, pre, qw, ow)
-
-
-def reduce_kernel(
-    g, out,
-    C, S, XR, ZR, E1, E2, XR2, ZR2, E, YR, F, FR,
-    cs, cr, xs, xr, zs, zr, x2s, x2r, z2s, z2r, ys, yr, fs, fr,
+    )(tok, dest, down, up, pre, qw, ow, xin, win, ng, mg)
+
+
+def block_kernel(
+    cot_i, wq_i, wo_i, normt_i, proj_i, prob_i, combt_i, n2_i, r2_i, xin, ng, mg,
+    lg, pout, oout,
+    cot, wq, wo, normt, proj, prob, combt, n2, r2,
+    db, dc, wof, DP, dpb, g,
+    C, S, Z, XR, ZR, E1, E2, XR2, ZR2, E, YR, F, FR,
+    ins, cs, cr, xs, xr, zs, zr, x2s, x2r, z2s, z2r, ys, yr, fs, fr,
 ):
     x, yh, c, z, yl = place()
+    pairs = [
+        (cot_i, cot), (n2_i, n2), (r2_i, r2), (wo_i, wo), (combt_i, combt), (prob_i, prob), (proj_i, proj),
+        (normt_i, normt), (wq_i, wq),
+    ]
+    loads = [pltpu.make_async_copy(a, b, ins.at[n]) for n, (a, b) in enumerate(pairs)]
+    for cp in loads:
+        cp.start()
     zp = [at(x, yh, c, (z + s) % 4, yl) for s in (1, 2, 3)]
     xp = [at((x + s) % 4, yh, c, z, yl) for s in (1, 2, 3)]
     core = at(x, yh, 1 - c, z, yl)
@@ -394,38 +554,140 @@
     greet(zp + xp + [core, p1, p2, yhp])
 
     def core_copy(p):
-        return remote(g.at[1 - c, p], C.at[p], cs.at[p], cr.at[p], core)
-
-    for p in (2, 0, 3, 1):
-        core_copy(p).start()
+        return remote(g.at[p, :, 1 - c], C.at[p], cs.at[p], cr.at[p], core)
 
     def x_copy(p, i):
-        return remote(S.at[p, (x + i + 1) % 4], XR.at[i, p], xs.at[p, i], xr.at[p, i], xp[i])
+        return remote(
+            S.at[p, pl.ds((x + i + 1) % 4 * 2, 2)], XR.at[i, p], xs.at[p, i], xr.at[p, i], xp[i]
+        )
 
     def z_copy(i):
         t = (z + i + 1) % 4
-        return remote(
-            S.at[2 + t % 2, :, t // 2], ZR.at[i], zs.at[i], zr.at[i], zp[i]
-        )
+        return remote(Z.at[t % 2, t // 2], ZR.at[i], zs.at[i], zr.at[i], zp[i])
 
     def summed(p):
         core_copy(p).wait_recv()
-        S[p] = (g[c, p].astype(F32) + C[p].astype(F32)).astype(BF16)
-
-    summed(2)
+        total = (g[p, :, c].astype(F32) + C[p].astype(F32)).astype(BF16)
+        if p < 2:
+            S[p] = total
+        else:
+            total = total.reshape(4, 2, 80, 640)
+            Z[p - 2, 0] = total[:, 0]
+            Z[p - 2, 1] = total[:, 1]
+
+    def z_start(part):
+        for i in (0, 2, 1):
+
+            @pl.when((z + i + 1) % 2 == part)
+            def _():
+                z_copy(i).start()
+
+    loads[0].wait()
+    loads[1].wait()
+    loads[2].wait()
+    loads[3].wait()
+
+    def out_step(t, carry):
+        rows = pl.ds(pl.multiple_of(t * 128, 128), 128)
+        slope = cot[rows, :].astype(F32) * mg[...]
+        unit = n2[rows, :]
+        grad = r2[rows, :] * (slope - unit * jnp.mean(slope * unit, axis=-1, keepdims=True))
+        n2[rows, :] = grad
+        db[rows, :] = grad.astype(BF16)
+        dc[rows, :] = lax.dot_general(
+            grad.astype(BF16), wo[...], NT, preferred_element_type=F32
+        ).astype(BF16)
+        return carry
+
+    lax.fori_loop(0, 4, out_step, 0)
+    loads[4].wait()
+
+    def wo_step(t, carry):
+        cols = pl.ds(pl.multiple_of(t * 640, 128), 640)
+        wof[t] = jnp.dot(combt[...], db[:, cols], preferred_element_type=F32)
+        return carry
+
+    lax.fori_loop(0, 2, wo_step, 0)
+    g[3] = (
+        jnp.concatenate([wof[0].reshape(16, 40, 640), wof[1].reshape(16, 40, 640)], axis=1)
+        .astype(BF16)
+        .reshape(8, 2, 80, 640)
+    )
+    core_copy(3).start()
+
+    DP[...] = jnp.zeros_like(DP)
+    loads[5].wait()
+    loads[6].wait()
+
+    def head_step(h, carry):
+        lanes, mask = head_lanes(h)
+        for b in range(4):
+            rows, keys = pl.ds(128 * b, 128), pl.ds(KEYS[b], 256)
+            query = proj[0, rows, lanes] * mask
+            key = proj[1, keys, lanes] * mask
+            grad = dc[rows, lanes] * mask
+            share = prob[h, b]
+            wide = share.astype(F32)
+            slope = lax.dot_general(grad, proj[2, keys, lanes], NT, preferred_element_type=F32)
+            slope = wide * (slope - jnp.sum(slope * wide, axis=-1, keepdims=True)) * HEAD_DIM ** (-0.5)
+            slope = slope.astype(BF16)
+            DP[0, rows, lanes] += jnp.dot(slope, key, preferred_element_type=F32)
+            DP[1, keys, lanes] += lax.dot_general(slope, query, TN, preferred_element_type=F32)
+            DP[2, keys, lanes] += lax.dot_general(share, grad, TN, preferred_element_type=F32)
+
+        @pl.when(h == 3)
+        def _():
+            summed(3)
+            z_start(1)
+
+        return carry
+
+    lax.fori_loop(0, 8, head_step, 0)
+    loads[7].wait()
+    loads[8].wait()
+
+    def weight_grad(p):
+        dpb[p] = DP[p].astype(BF16)
+        g[p] = (
+            jnp.dot(normt[...], dpb[p], preferred_element_type=F32).astype(BF16).reshape(8, 2, 80, 640)
+        )
+        core_copy(p).start()
+
+    def input_step(t, carry):
+        rows = pl.ds(pl.multiple_of(t * 128, 128), 128)
+        slope = jnp.zeros((128, 1280), F32)
+        for p in range(3):
+            slope += lax.dot_general(
+                dpb[p, rows, :],
+                wq[:, :, 640 * p : 640 * p + 640].reshape(1280, 640),
+                NT,
+                preferred_element_type=F32,
+            )
+        slope = slope.astype(BF16).astype(F32) * ng[...]
+        value = xin[rows, :].astype(F32)
+        factor = lax.rsqrt(jnp.mean(value * value, axis=-1, keepdims=True) + EPSILON)
+        unit = value * factor
+        grad = factor * (slope - unit * jnp.mean(slope * unit, axis=-1, keepdims=True))
+        lg[rows, :] = (grad + n2[rows, :]).astype(BF16)
+        return carry
+
+    weight_grad(0)
+    weight_grad(1)
     summed(0)
     for i in (0, 2, 1):
         x_copy(0, i).start()
-    summed(3)
-    for i in (0, 2, 1):
-        z_copy(i).start()
+    weight_grad(2)
     summed(1)
     for i in (0, 2, 1):
         x_copy(1, i).start()
+    lax.fori_loop(0, 1, input_step, 0)
+    summed(2)
+    z_start(0)
+    lax.fori_loop(1, 4, input_step, 0)
 
     for i in range(3):
         z_copy(i).wait_recv()
-    mine = S[2 + z % 2, :, z // 2].astype(F32)
+    mine = Z[z % 2, z // 2].astype(F32)
     for i in range(3):
         mine = mine + ZR[i].astype(F32)
     E2[...] = mine.astype(BF16)
@@ -438,7 +700,7 @@
     for p in range(2):
         for i in range(3):
             x_copy(p, i).wait_recv()
-        mine = S[p, x].astype(F32)
+        mine = S[p, pl.ds(2 * x, 2)].astype(F32)
         for i in range(3):
             mine = mine + XR[i, p].astype(F32)
         E1[0, p] = mine[0].astype(BF16)
@@ -508,9 +770,11 @@
         f_wait(0)
         f_wait(1)
 
-    for t in range(2):
-        for p in range(2):
-            out[2 * p + t] = FR[t, p].astype(F32)
+    for p in range(3):
+        pout[:, 640 * p : 640 * p + 640] = FR[p % 2, p // 2].astype(F32)
+    last = FR[1, 1].astype(F32)
+    oout[:, 0:640] = last[0:40]
+    oout[:, 640:1280] = last[40:80]
 
     for p in range(4):
         core_copy(p).wait_send()
@@ -522,20 +786,33 @@
         z2_copy(i).wait_send()
 
 
-def reduce_grads(g):
+def block_grads(cot, wq, wo, normt, proj, prob, combt, n2, r2, xin, ng, mg):
     vm = pl.BlockSpec(memory_space=pltpu.VMEM)
+    hbm = pl.BlockSpec(memory_space=pl.ANY)
     dma = pltpu.SemaphoreType.DMA
-    rows, cols = g.shape[4:]
-    t = (rows, cols)
+    t = (80, 640)
+    held = (cot, wq, wo, normt, proj, prob, combt, n2, r2)
     return pl.pallas_call(
-        reduce_kernel,
-        name="reduce",
-        out_shape=jax.ShapeDtypeStruct((4,) + t, F32),
-        in_specs=[vm],
-        out_specs=vm,
-        scratch_shapes=[
-            pltpu.VMEM((4, 4, 2) + t, BF16),
-            pltpu.VMEM((4, 4, 2) + t, BF16),
+        block_kernel,
+        name="block",
+        out_shape=(
+            jax.ShapeDtypeStruct((512, 1280), BF16),
+            jax.ShapeDtypeStruct((80, 1920), F32),
+            jax.ShapeDtypeStruct((40, 1280), F32),
+        ),
+        in_specs=[hbm] * 9 + [vm] * 3,
+        out_specs=(vm, vm, vm),
+        scratch_shapes=[pltpu.VMEM(k.shape, k.dtype) for k in held]
+        + [
+            pltpu.VMEM((512, 1280), BF16),
+            pltpu.VMEM((512, 640), BF16),
+            pltpu.VMEM((2, 640, 640), F32),
+            pltpu.VMEM((3, 512, 640), F32),
+            pltpu.VMEM((3, 512, 640), BF16),
+            pltpu.VMEM((4, 8, 2) + t, BF16),
+            pltpu.VMEM((4, 8) + t, BF16),
+            pltpu.VMEM((2, 8) + t, BF16),
+            pltpu.VMEM((2, 2, 4) + t, BF16),
             pltpu.VMEM((3, 2, 2) + t, BF16),
             pltpu.VMEM((3, 4) + t, BF16),
             pltpu.VMEM((2, 2) + t, BF16),
@@ -546,6 +823,7 @@
             pltpu.VMEM((3, 2) + t, BF16),
             pltpu.VMEM((2,) + t, BF16),
             pltpu.VMEM((2, 2) + t, BF16),
+            dma((9,)),
             dma((4,)), dma((4,)),
             dma((2, 3)), dma((2, 3)),
             dma((3,)), dma((3,)),
@@ -555,38 +833,10 @@
             dma((3,)), dma((2,)),
         ],
         compiler_params=pltpu.CompilerParams(
-            collective_id=2, has_side_effects=True, vmem_limit_bytes=60 << 20
+            collective_id=2, has_side_effects=True, vmem_limit_bytes=62 << 20
         ),
-        cost_estimate=pl.CostEstimate(flops=10**7, bytes_accessed=40 * 10**6, transcendentals=0),
-    )(g)
-
-
-def vision_forward(layer_in, packed_weight, output_weight, windows, norm_gain, merge_gain):
-    patches = layer_in.shape[0]
-    head_count = output_weight.shape[0] // HEAD_DIM
-    widened = layer_in.astype(F32)
-    normed = rms_scale(widened, norm_gain).astype(BF16)
-    projected = jnp.dot(normed, packed_weight, preferred_element_type=F32).astype(BF16)
-    triple = projected.reshape(patches, 3, head_count, HEAD_DIM).astype(F32)
-    scores = jnp.einsum("qhd,khd->hqk", triple[:, 0], triple[:, 1]) * HEAD_DIM ** (-0.5)
-    same_window = windows[:, None] == windows[None, :]
-    scores = jnp.where(same_window[None], scores, -1e30)
-    attention = jax.nn.softmax(scores, axis=-1).astype(BF16)
-    combined = jnp.einsum("hqk,khd->qhd", attention.astype(F32), triple[:, 2])
-    combined = combined.reshape(patches, head_count * HEAD_DIM).astype(BF16)
-    output = widened + jnp.dot(combined, output_weight, preferred_element_type=F32)
-    return rms_scale(output, merge_gain)
-
-
-def vision_backward(
-    layer_in, packed_weight, output_weight, windows, norm_gain, merge_gain, cotangent
-):
-
-    def forward(layer_arg, packed_arg, output_arg):
-        return vision_forward(layer_arg, packed_arg, output_arg, windows, norm_gain, merge_gain)
-
-    _, pullback = jax.vjp(forward, layer_in, packed_weight, output_weight)
-    return pullback(cotangent.astype(F32))
+        cost_estimate=pl.CostEstimate(flops=8 * 10**9, bytes_accessed=40 * 10**6, transcendentals=0),
+    )(cot, wq, wo, normt, proj, prob, combt, n2, r2, xin, ng, mg)
 
 
 def local(
@@ -602,21 +852,12 @@
     qkv_weight,
     proj_weight,
 ):
-    cotangent, packed_full, output_full = merger(
-        token_grads, token_dest.reshape(1, 64), merger_down, merger_up, merger_pre, qkv_weight, proj_weight
+    norm_row, merge_row = norm_gain.reshape(1, 1280), merge_gain.reshape(1, 1280)
+    kept = merger(
+        token_grads, token_dest.reshape(1, 64), merger_down, merger_up, merger_pre, qkv_weight, proj_weight,
+        layer_input, window_ids, norm_row, merge_row,
     )
-    packed_full = packed_full.reshape(1280, 1920)
-    output_full = output_full.reshape(640, 1280)
-    layer_grad, packed_term, output_term = vision_backward(
-        layer_input, packed_full, output_full, window_ids[0], norm_gain, merge_gain, cotangent
-    )
-    packed_term = packed_term.reshape(4, 2, 2, 80, 3, 640).transpose(2, 4, 0, 1, 3, 5)
-    output_term = output_term.reshape(4, 2, 2, 40, 2, 640).transpose(2, 0, 1, 4, 3, 5)
-    output_term = output_term.reshape(2, 1, 4, 2, 80, 640)
-    sums = reduce_grads(jnp.concatenate([packed_term, output_term], axis=1))
-    packed_sum = jnp.concatenate([sums[0], sums[1], sums[2]], axis=1)
-    output_sum = jnp.concatenate([sums[3, :40], sums[3, 40:]], axis=1)
-    return (layer_grad, packed_sum, output_sum)
+    return block_grads(*kept, layer_input, norm_row, merge_row)
 
 
 def solution(mesh):

time: 286 us -> 216 us (0.76); the launches traced: 285 us -> 211 us
  matrix products: 45 us -> 0 us
  local copies, waits for them, and re-layouts: 33.1 us -> 6.63 us
  other arithmetic: 16.8 us -> 0 us
  Pallas kernels: 189 us -> 204 us
    dot_general x11 -> x0, matrix products: 39.5 us -> none  [the longest x3 17.4 us: vision_forward(): jnp.dot(normed, packed_weight, preferred_element_type=F32).astype(BF16)]
    reshape x4 -> x2, local copies, waits for them, and re-layouts: 20.8 us -> 2.59 us  [the longest x1 1.29 us: local(): norm_gain.reshape(1, 1280)]
    pallas_call x2, Pallas kernels: 189 us -> 204 us  [the longest x1 126 us: merger(): pl.pallas_call(merger_kernel, name='merger', out_shape=tuple((jax.ShapeDt...]
    convert_element_type x3 -> x0, other arithmetic: 8.9 us -> none  [the longest x1 4.59 us: vision_forward(): attention = jax.nn.softmax(scores, axis=-1).astype(BF16)]
    concatenate x3 -> x0, other arithmetic: 7.35 us -> none  [the longest x1 5.8 us: local(): sums = reduce_grads(jnp.concatenate([packed_term, output_term], axis=1))]
    sub x1 -> x0, matrix products: 5.5 us -> none  [vision_forward(): attention = jax.nn.softmax(scores, axis=-1).astype(BF16)]
    unnamed x60 -> x7, local copies, waits for them, and re-layouts: 7.16 us -> 4.04 us
    convert_element_type x2 -> x0, local copies, waits for them, and re-layouts: 2.95 us -> none  [the longest x1 2.7 us: vision_forward(): jnp.dot(normed, packed_weight, preferred_element_type=F32).astype(BF16)]
where the time goes in v2:
time: 216 us; the launch traced here: 211 us
  Pallas kernels  204 us (94%)
  local copies, waits for them, and re-layouts  6.63 us (3%)
    pallas_call x1, Pallas kernels, merger(): pl.pallas_call(merger_kernel, name='merger', out_shape=tuple((jax.ShapeDt...  126 us
    pallas_call x1, Pallas kernels, block_grads(): pl.pallas_call(block_kernel, name='block', out_shape=(jax.ShapeDtypeStruc...  78.2 us

profile of v2, /device:TPU:0, one launch (start us, length us, event | category | flops | bytes accessed | tf_op | source)
XLA Modules:
  0.0 211.4 jit_solution(16355289572423692132)
XLA Ops:
  0.6 1.3 reshape.16.ng
  1.9 1.3 reshape.17.mg
  3.2 125.8 %merger.1 = (bf16[512,1280]{1,0:T(8,128)(2,1)}, bf16[16,80,1920]{2,1,0:T(8,128)(2,1)}, bf16[640,1280]{1,0:T(8,128)(2,1)}, bf16[1280,512]{1,0:T(8,128)(2,1)}, bf1...) custom-call(bf16[64,8192]{1,0:T(8,128)(2,1)} %tok.1, ...), custom_call_target="tpu_custom_call" | custom-call | flops 8999999488 | bytes 40000000 | tf_op jit(solution)/shard_map/merger/pallas_call | solution.py:479
  129.1 78.2 %block.1 = (bf16[512,1280]{1,0:T(8,128)(2,1)}, f32[80,1920]{1,0:T(8,128)}, f32[40,1280]{1,0:T(8,128)}) custom-call(bf16[512,1280]{1,0:T(8,128)(2,1)} %get-tuple-element.12.cot_i, bf16[16,80,1920]{2,1,0:T(8,128)(2,1)} %get-tuple-element.13.wq_i, bf16[640,1280]{1,0:T(8,128)(2,1)} %get-tuple-element.14.wo_i, bf16[1280,512]{1,0:T(8,128)(2,1)} %get-tuple-element.15.normt_i, ...), custom_call_target="tpu_custom_call" | custom-call | flops 8000000000 | bytes 40000000 | tf_op jit(solution)/shard_map/block/pallas_call | solution.py:795
  207.3 0.0 copy-start
  207.3 0.0 copy-start.1
  207.3 2.5 %copy.17 = bf16[512,1280]{1,0:T(8,128)(2,1)} copy(bf16[512,1280]{1,0:T(8,128)(2,1)} %get-tuple-element.24) | data formatting | bytes 2621440
  209.9 0.0 copy-done
  209.9 0.8 copy.18
  210.7 0.0 copy-done.1
  210.7 0.7 copy.19
Async XLA Ops:
  207.3 2.6 %copy-start = (f32[80,1920]{1,0:T(8,128)S(1)}, f32[80,1920]{1,0:T(8,128)}, u32[]{:S(2)}) copy-start(f32[80,1920]{1,0:T(8,128)} %get-tuple-element.25) | copy-start | bytes 1843204
  207.3 3.4 %copy-start.1 = (f32[40,1280]{1,0:T(8,128)S(1)}, f32[40,1280]{1,0:T(8,128)}, u32[]{:S(2)}) copy-start(f32[40,1280]{1,0:T(8,128)} %get-tuple-element.26) | copy-start | bytes 614404

commit v3 on v2

--- a/solution.py
+++ b/solution.py
@@ -16,6 +16,8 @@
 TN = (((0,), (0,)), ((), ()))
 
 N_TOK = 8
+N_NARROW = 5
+N_LEFT = 384
 N_FEAT = 8
 
 
@@ -68,7 +70,7 @@
     G, down_v, slope, acc, pg, pre2,
     S, R, own, T, T0, ZR, M, OUT, A,
     cot, wq, wo, wo2, norm, normt, proj, prob, combt, n2, r2, bias,
-    loc, dsem, outs, zs, zr, ys, yr, ps, pr, ws, wr, xs, xr, cs, cr, rys, ryr, rzs, rzr, as_, ar,
+    loc, dsem, os_, or_, outs, zs, zr, ns, nr, ys, yr, ps, pr, ws, wr, xs, xr, cs, cr, rys, ryr, rzs, rzr, as_, ar,
 ):
     x, yh, c, z, yl = place()
     d = (x * 2 + yh) * 2 + c
@@ -102,10 +104,33 @@
         rows = pl.ds(pl.multiple_of(f * V, V), V)
         return pltpu.make_async_copy(up.at[rows], down_v.at[f % 4, :, pl.ds(0, V)], dsem.at[f % 4])
 
-    def z_copy(k, i):
+    def z_copy(k, i, rows):
         return remote(
-            G.at[0, pl.ds(0, 64), col(k)], G.at[3 - i, pl.ds(0, 64), col(k)], zs.at[k, i], zr.at[k, i], zp[i]
+            G.at[0, pl.ds(0, rows), col(k)],
+            G.at[(3, 1)[i], pl.ds(0, rows), col(k)],
+            zs.at[k, i],
+            zr.at[k, i],
+            (zp[0], zp[2])[i],
         )
+
+    def on_copy(k, i, rows):
+        half = pl.ds(pl.multiple_of(k * W + i * (W // 2), W // 2), W // 2)
+        return remote(
+            G.at[(3, 1)[i], pl.ds(0, rows), half],
+            G.at[2, pl.ds(0, rows), half],
+            ns.at[k, i],
+            nr.at[k, i],
+            (zp[0], zp[2])[i],
+        )
+
+    def each(k, act):
+        @pl.when(k < N_NARROW)
+        def _():
+            act(64)
+
+        @pl.when(k >= N_NARROW)
+        def _():
+            act(128)
 
     def y_copy(k, i):
         return remote(
@@ -116,16 +141,24 @@
             (p1, p2)[i],
         )
 
+    def o_copy(i):
+        wide = pl.ds(N_NARROW * W, (N_TOK - N_NARROW) * W)
+        return remote(
+            G.at[0, pl.ds(32 * i, 32), wide],
+            G.at[0, pl.ds(64 + 32 * i, 32), wide],
+            os_.at[i],
+            or_.at[i],
+            (p1, p2)[i],
+        )
+
+    o_copy(0).start()
     for k in range(2):
-        for i in (0, 2, 1):
-            z_copy(k, i).start()
+        for i in range(2):
+            z_copy(k, i, 64).start()
 
     def pre_copy(zz):
         rows = pl.ds(pl.multiple_of((2 * zz + 1 - yl) * 64 + 32, 32), 32)
         return remote(pre.at[rows], pre2.at[pl.ds(32 * zz, 32)], ps.at[zz], pr.at[zz], yhp)
-
-    for zz in range(4):
-        pre_copy(zz).start()
 
     def w_copies(source, index, sends, recvs, device):
         first = wq.at[index] if source is None else source[0]
@@ -143,34 +176,35 @@
     d2 = flipped(d)
     for cp in w_copies((qw, ow), d, ws.at[0], wr.at[0], p2):
         cp.start()
+    o_copy(1).start()
     for i in (0, 2, 1):
         for cp in w_copies((qw, ow), d, xs.at[0, i], xr.at[0, i], xp[i]):
             cp.start()
     for cp in w_copies((qw, ow), d, cs.at[0], cr.at[0], core):
         cp.start()
+    for zz in range(4):
+        pre_copy(zz).start()
 
     def emit(n, source, target):
         return pltpu.make_async_copy(source, target, outs.at[n])
 
-    def slope_step(k):
-        r = k // 2
+    def slope_step(r):
+        @pl.when(r == 0)
+        def _():
+            for zz in range(4):
+                pre_copy(zz).wait_recv()
+
         zz = (z + r) % 4
-
-        @pl.when(k % 2 == 0)
-        def _():
-            mine = pre[pl.ds(pl.multiple_of((2 * zz + yl) * 64, 64), 64), :]
-            slope[r, 0:64, :] = gelu_slope(mine.astype(F32))
-
-        @pl.when(k % 2 == 1)
-        def _():
-            first = pre[pl.ds(pl.multiple_of((2 * zz + 1 - yl) * 64, 64), 32), :]
-            second = pre2[pl.ds(pl.multiple_of(zz * 32, 32), 32), :]
-            slope[r, 64:96, :] = gelu_slope(first.astype(F32))
-            slope[r, 96:128, :] = gelu_slope(second.astype(F32))
+        mine = pre[pl.ds(pl.multiple_of((2 * zz + yl) * 64, 64), 64), :]
+        slope[r, 0:64, :] = gelu_slope(mine.astype(F32))
+        first = pre[pl.ds(pl.multiple_of((2 * zz + 1 - yl) * 64, 64), 32), :]
+        second = pre2[pl.ds(pl.multiple_of(zz * 32, 32), 32), :]
+        slope[r, 64:96, :] = gelu_slope(first.astype(F32))
+        slope[r, 96:128, :] = gelu_slope(second.astype(F32))
 
     def norm_step(k):
-        rows = pl.ds(pl.multiple_of(k * 64, 64), 64)
-        norm[rows, :] = rms_scale(xin[rows, :].astype(F32), ng[...]).astype(BF16)
+        rows = pl.ds(pl.multiple_of(k * 128, 128), 128)
+        norm[rows, :] = rms_scale(xin[rows, :].astype(F32), ng[...].reshape(1, 1280)).astype(BF16)
 
     def bias_step():
         for b in range(4):
@@ -213,13 +247,14 @@
         emit(7, n2, n2_o).start()
         emit(8, r2, r2_o).start()
 
-    for zz in range(4):
-        pre_copy(zz).wait_recv()
     acc[...] = jnp.zeros_like(acc)
 
     def multiply(k):
-        for i in range(2):
-            y_copy(k, i).wait_recv()
+        @pl.when(k < N_NARROW)
+        def _():
+            for i in range(2):
+                y_copy(k, i).wait_recv()
+
         tile = G[:, :, col(k)].reshape(512, W)
         down_copy(k).wait()
         acc[...] += lax.dot_general(tile, down_v[k % 4], NT, preferred_element_type=F32)
@@ -232,39 +267,6 @@
         def _():
             up_copy(k - 4).start()
 
-
-    def gather_step(k, carry):
-        @pl.when(k + 2 < N_TOK)
-        def _():
-            for i in (0, 2, 1):
-                z_copy(k + 2, i).start()
-
-        for i in range(3):
-            z_copy(k, i).wait_recv()
-        for i in range(2):
-            y_copy(k, i).start()
-
-        @pl.when(k == 1)
-        def _():
-            for cp in w_copies((qw, ow), d2, ws.at[0], wr.at[0], p2):
-                cp.wait_recv()
-            for i in (0, 2, 1):
-                for cp in w_copies(None, d2, xs.at[1, i], xr.at[1, i], xp[i]):
-                    cp.start()
-            for cp in w_copies(None, d2, cs.at[1], cr.at[1], core):
-                cp.start()
-
-        @pl.when(k >= 1)
-        def _():
-            multiply(k - 1)
-
-        slope_step(k)
-        norm_step(k)
-        return carry
-
-    lax.fori_loop(0, N_TOK, gather_step, 0)
-    bias_step()
-    multiply(jnp.int32(N_TOK - 1))
 
     def x_arrive(h):
         for i in range(3):
@@ -274,6 +276,88 @@
                 cp.wait_recv()
             for cp in w_copies(None, other, cs.at[2 + 3 * h + i], cr.at[2 + 3 * h + i], core):
                 cp.start()
+
+    def z_send(k):
+        def act(rows):
+            for i in range(2):
+                z_copy(k, i, rows).start()
+
+        each(k, act)
+
+    def z_forward(k):
+        def act(rows):
+            for i in range(2):
+                z_copy(k, i, rows).wait_recv()
+                on_copy(k, i, rows).start()
+
+        each(k, act)
+
+    def y_forward(k):
+        def act(rows):
+            for i in range(2):
+                on_copy(k, i, rows).wait_recv()
+            if rows == 64:
+                for i in range(2):
+                    y_copy(k, i).start()
+
+        each(k, act)
+
+    def gather_step(k, carry):
+        @pl.when(k == 3)
+        def _():
+            o_copy(0).wait_recv()
+            o_copy(1).wait_recv()
+
+        @pl.when(k + 2 < N_TOK)
+        def _():
+            z_send(k + 2)
+
+        @pl.when(k < N_TOK)
+        def _():
+            z_forward(k)
+
+        @pl.when(k == N_TOK)
+        def _():
+            multiply(k - 2)
+
+        @pl.when(k >= 1)
+        def _():
+            y_forward(k - 1)
+
+        @pl.when(k == 2)
+        def _():
+            for cp in w_copies((qw, ow), d2, ws.at[0], wr.at[0], p2):
+                cp.wait_recv()
+            for i in (0, 2, 1):
+                for cp in w_copies(None, d2, xs.at[1, i], xr.at[1, i], xp[i]):
+                    cp.start()
+            for cp in w_copies(None, d2, cs.at[1], cr.at[1], core):
+                cp.start()
+
+        @pl.when((k >= 3) & (k < N_TOK))
+        def _():
+            multiply(k - 3)
+
+        @pl.when(k >= N_TOK - 1)
+        def _():
+            multiply(jnp.where(k == N_TOK, N_TOK - 1, N_TOK - 3))
+
+        @pl.when(k < 4)
+        def _():
+            norm_step(k)
+
+        @pl.when((k >= 4) & (k < 8))
+        def _():
+            slope_step(k - 4)
+
+        @pl.when(k == 6)
+        def _():
+            x_arrive(0)
+
+        return carry
+
+    lax.fori_loop(0, N_TOK + 1, gather_step, 0)
+    bias_step()
 
     pg[...] = (acc[...] * slope[...].reshape(512, slope.shape[2])).astype(BF16)
     combf = acc
@@ -341,7 +425,7 @@
             ry_copy(f, h).wait_recv()
         total = own[f % 4] + jnp.concatenate([R[f, 0].astype(F32), R[f, 1].astype(F32)], axis=1)
         T[f] = total[1:4].astype(BF16)
-        T0[f % 2] = total[0]
+        T0[f % 4] = total[0]
         for h in (0, 2, 1):
             rz_copy(f, h).start()
 
@@ -349,7 +433,7 @@
         for h in range(3):
             rz_copy(f, h).wait_recv()
         M[f] = (
-            T0[f % 2] + ZR[f, 0].astype(F32) + ZR[f, 1].astype(F32) + ZR[f, 2].astype(F32)
+            T0[f % 4] + ZR[f, 0].astype(F32) + ZR[f, 1].astype(F32) + ZR[f, 2].astype(F32)
         ).astype(BF16)
 
     def send_rows(j):
@@ -365,7 +449,6 @@
         return carry
 
     lax.fori_loop(0, 3, open_step, 0)
-    x_arrive(0)
     x_arrive(1)
 
     def sum_step(f, carry):
@@ -375,11 +458,11 @@
         def _():
             first_product(f + 3)
 
-        @pl.when(f >= 1)
-        def _():
-            over_z(f - 1)
-
-        @pl.when((f >= 2) & (f % 2 == 0))
+        @pl.when(f >= 2)
+        def _():
+            over_z(f - 2)
+
+        @pl.when((f >= 3) & (f % 2 == 1))
         def _():
             send_rows(f // 2 - 1)
 
@@ -396,6 +479,7 @@
         return carry
 
     lax.fori_loop(0, N_FEAT, sum_step, 0)
+    over_z(N_FEAT - 2)
     head_step(7)
     emit(5, prob, prob_o).start()
     over_z(N_FEAT - 1)
@@ -432,13 +516,19 @@
         pre_copy(zz).wait_send()
 
     def drain(k, carry):
-        for i in range(3):
-            z_copy(k, i).wait_send()
-        for i in range(2):
-            y_copy(k, i).wait_send()
+        def act(rows):
+            for i in range(2):
+                z_copy(k, i, rows).wait_send()
+                on_copy(k, i, rows).wait_send()
+                if rows == 64:
+                    y_copy(k, i).wait_send()
+
+        each(k, act)
         return carry
 
     lax.fori_loop(0, N_TOK, drain, 0)
+    o_copy(0).wait_send()
+    o_copy(1).wait_send()
 
     def drain2(f, carry):
         for i in range(2):
@@ -493,7 +583,7 @@
             pltpu.VMEM((N_FEAT, 2, 4, 32, V), BF16),
             pltpu.VMEM((4, 4, 64, V), F32),
             pltpu.VMEM((N_FEAT, 3, 64, V), BF16),
-            pltpu.VMEM((2, 64, V), F32),
+            pltpu.VMEM((4, 64, V), F32),
             pltpu.VMEM((N_FEAT, 3, 64, V), BF16),
             pltpu.VMEM((N_FEAT, 64, V), BF16),
             pltpu.VMEM((4, 256, V), BF16),
@@ -512,8 +602,9 @@
             pltpu.VMEM((4, 128, 256), F32),
             dma((1,)),
             dma((4,)),
+            dma((2,)), dma((2,)),
             dma((9,)),
-            dma((N_TOK, 3)), dma((N_TOK, 3)), dma((N_TOK, 2)), dma((N_TOK, 2)),
+            dma((N_TOK, 2)), dma((N_TOK, 2)), dma((N_TOK, 2)), dma((N_TOK, 2)), dma((N_TOK, 2)), dma((N_TOK, 2)),
             dma((4,)), dma((4,)),
             dma((1, 2)), dma((1, 2)),
             dma((2, 3, 2)), dma((2, 3, 2)),
@@ -533,9 +624,11 @@
     cot_i, wq_i, wo_i, normt_i, proj_i, prob_i, combt_i, n2_i, r2_i, xin, ng, mg,
     lg, pout, oout,
     cot, wq, wo, normt, proj, prob, combt, n2, r2,
-    db, dc, wof, DP, dpb, g,
-    C, S, Z, XR, ZR, E1, E2, XR2, ZR2, E, YR, F, FR,
-    ins, cs, cr, xs, xr, zs, zr, x2s, x2r, z2s, z2r, ys, yr, fs, fr,
+    db, dc, wof, DP, dpb,
+    gl, ga, gb, Cl, Ca, Cb, Z, ZR, E2, XR2, El, YRl, Fl, FRl,
+    Sa, XRa, E1, ZR2, Ea, YRa, Fa, FRa, Sb, YRb, Eb2, XRb, Zb, Fb,
+    ins, cls, clr, cas, car, cbs, cbr, zs, zr, x2s, x2r, yls, ylr, fls, flr,
+    xas, xar, z2s, z2r, yas, yar, fas, far, ybs, ybr, xbs, xbr, zbs, zbr, pbs, pbr,
 ):
     x, yh, c, z, yl = place()
     pairs = [
@@ -553,34 +646,122 @@
     yhp = at(x, 1 - yh, c, z, yl)
     greet(zp + xp + [core, p1, p2, yhp])
 
-    def core_copy(p):
-        return remote(g.at[p, :, 1 - c], C.at[p], cs.at[p], cr.at[p], core)
-
-    def x_copy(p, i):
-        return remote(
-            S.at[p, pl.ds((x + i + 1) % 4 * 2, 2)], XR.at[i, p], xs.at[p, i], xr.at[p, i], xp[i]
-        )
+    def cl_copy(p):
+        return remote(gl.at[p, :, 1 - c], Cl.at[p], cls.at[p], clr.at[p], core)
+
+    def ca_copy(p):
+        return remote(ga.at[p, :, 1 - c], Ca.at[p], cas.at[p], car.at[p], core)
+
+    def cb_copy(p):
+        return remote(gb.at[p, :, 1 - c], Cb.at[p], cbs.at[p], cbr.at[p], core)
 
     def z_copy(i):
         t = (z + i + 1) % 4
         return remote(Z.at[t % 2, t // 2], ZR.at[i], zs.at[i], zr.at[i], zp[i])
 
-    def summed(p):
-        core_copy(p).wait_recv()
-        total = (g[p, :, c].astype(F32) + C[p].astype(F32)).astype(BF16)
-        if p < 2:
-            S[p] = total
-        else:
-            total = total.reshape(4, 2, 80, 640)
-            Z[p - 2, 0] = total[:, 0]
-            Z[p - 2, 1] = total[:, 1]
-
-    def z_start(part):
+    def summed_l(p):
+        cl_copy(p).wait_recv()
+        total = (gl[p, :, c].astype(F32) + Cl[p].astype(F32)).astype(BF16).reshape(4, 2, 80, 640)
+        Z[p, 0] = total[:, 0]
+        Z[p, 1] = total[:, 1]
         for i in (0, 2, 1):
 
-            @pl.when((z + i + 1) % 2 == part)
+            @pl.when((z + i + 1) % 2 == p)
             def _():
                 z_copy(i).start()
+
+    def x2_copy(i):
+        return remote(E2.at[(x + i + 1) % 4], XR2.at[i], x2s.at[i], x2r.at[i], xp[i])
+
+    def xa_copy(p, i):
+        return remote(
+            Sa.at[p, pl.ds((x + i + 1) % 4 * 2, 2)], XRa.at[i, p], xas.at[p, i], xar.at[p, i], xp[i]
+        )
+
+    def summed_a(p):
+        ca_copy(p).wait_recv()
+        Sa[p] = (ga[p, :, c].astype(F32) + Ca[p].astype(F32)).astype(BF16)
+        for i in (0, 2, 1):
+            xa_copy(p, i).start()
+
+    def z2_copy(i):
+        t = (z + i + 1) % 4
+        return remote(E1.at[t // 2, t % 2], ZR2.at[i], z2s.at[i], z2r.at[i], zp[i])
+
+    def yb_copy(i):
+        return remote(
+            Sb.at[(1 - yl, 1 - yl, yl)[i], (yh, 1 - yh, 1 - yh)[i]],
+            YRb.at[i],
+            ybs.at[i],
+            ybr.at[i],
+            (p1, p2, yhp)[i],
+        )
+
+    def summed_b(p):
+        cb_copy(p).wait_recv()
+        total = (gb[p, :, c].astype(F32) + Cb[p].astype(F32)).astype(BF16)
+        total = total.reshape((4, 2) + total.shape[1:])
+        Sb[p, 0] = total[:, 0]
+        Sb[p, 1] = total[:, 1]
+
+    def xb_copy(i):
+        return remote(Eb2.at[(x + i + 1) % 4], XRb.at[i], xbs.at[i], xbr.at[i], xp[i])
+
+    def zb_copy(i):
+        return remote(Zb.at[z], Zb.at[z], zbs.at[i], zbr.at[i], zp[i])
+
+    def pb_copy():
+        return remote(Fb.at[yl], Fb.at[yl], pbs.at[0], pbr.at[0], p1)
+
+    owner = yh == z // 2
+
+    def y_copy(i, e, yr, s_sem, r_sem):
+        return remote(e, yr.at[i], s_sem.at[i], r_sem.at[i], (p1, p2, yhp)[i])
+
+    def f_copy(i, f, fr, s_sem, r_sem):
+        return remote(f, fr.at[z % 2], s_sem.at[i], r_sem.at[z % 2], zp[i])
+
+    def owners_send(e, yr, s_sem, r_sem):
+        @pl.when(owner)
+        def _():
+            y_copy(0, e, yr, s_sem, r_sem).start()
+
+        @pl.when(jnp.logical_not(owner))
+        def _():
+            for i in (1, 2):
+                y_copy(i, e, yr, s_sem, r_sem).start()
+
+    def owners_sum(e, yr, s_sem, r_sem, f, fr, fs_sem, fr_sem):
+        @pl.when(owner)
+        def _():
+            for i in range(3):
+                y_copy(i, e, yr, s_sem, r_sem).wait_recv()
+            total = (e[...].astype(F32) + yr[0].astype(F32)) + (yr[1].astype(F32) + yr[2].astype(F32))
+            f[...] = (total * (1.0 / 128.0)).astype(BF16)
+            for i in (0, 2, 1):
+                f_copy(i, f, fr, fs_sem, fr_sem).start()
+            fr[z % 2] = f[...]
+
+    def owners_end(e, yr, s_sem, r_sem, f, fr, fs_sem, fr_sem):
+        @pl.when(owner)
+        def _():
+            y_copy(0, e, yr, s_sem, r_sem).wait_send()
+            there = 1 - z % 2
+            pltpu.make_async_copy(fr.at[there], fr.at[there], fr_sem.at[there]).wait()
+            for i in range(3):
+                f_copy(i, f, fr, fs_sem, fr_sem).wait_send()
+
+        @pl.when(jnp.logical_not(owner))
+        def _():
+            for i in (1, 2):
+                y_copy(i, e, yr, s_sem, r_sem).wait_send()
+            for there in range(2):
+                pltpu.make_async_copy(fr.at[there], fr.at[there], fr_sem.at[there]).wait()
+
+    last_l = (El, YRl, yls, ylr)
+    last_a = (Ea, YRa, yas, yar)
+    more_l = (Fl, FRl, fls, flr)
+    more_a = (Fa, FRa, fas, far)
 
     loads[0].wait()
     loads[1].wait()
@@ -589,17 +770,15 @@
 
     def out_step(t, carry):
         rows = pl.ds(pl.multiple_of(t * 128, 128), 128)
-        slope = cot[rows, :].astype(F32) * mg[...]
+        slope = cot[rows, :].astype(F32) * mg[...].reshape(1, 1280)
         unit = n2[rows, :]
         grad = r2[rows, :] * (slope - unit * jnp.mean(slope * unit, axis=-1, keepdims=True))
         n2[rows, :] = grad
         db[rows, :] = grad.astype(BF16)
-        dc[rows, :] = lax.dot_general(
-            grad.astype(BF16), wo[...], NT, preferred_element_type=F32
-        ).astype(BF16)
         return carry
 
     lax.fori_loop(0, 4, out_step, 0)
+    dc[...] = lax.dot_general(db[...], wo[...], NT, preferred_element_type=F32).astype(BF16)
     loads[4].wait()
 
     def wo_step(t, carry):
@@ -608,16 +787,38 @@
         return carry
 
     lax.fori_loop(0, 2, wo_step, 0)
-    g[3] = (
+    gl[1] = (
         jnp.concatenate([wof[0].reshape(16, 40, 640), wof[1].reshape(16, 40, 640)], axis=1)
         .astype(BF16)
         .reshape(8, 2, 80, 640)
     )
-    core_copy(3).start()
+    cl_copy(1).start()
 
     DP[...] = jnp.zeros_like(DP)
     loads[5].wait()
+
+    def value_step(h, carry):
+        lanes, mask = head_lanes(h)
+        for b in range(4):
+            grad = dc[pl.ds(128 * b, 128), lanes] * mask
+            DP[2, pl.ds(KEYS[b], 256), lanes] += lax.dot_general(
+                prob[h, b], grad, TN, preferred_element_type=F32
+            )
+        return carry
+
+    lax.fori_loop(0, 8, value_step, 0)
+    summed_l(1)
+    loads[7].wait()
+    dpb[2] = DP[2].astype(BF16)
+    gl[0] = jnp.dot(normt[...], dpb[2], preferred_element_type=F32).astype(BF16).reshape(8, 2, 80, 640)
+    cl_copy(0).start()
     loads[6].wait()
+
+    def part_grad(p, first, width):
+        cols = slice(first, first + width)
+        dpb[p, :, cols] = DP[p, :, cols].astype(BF16)
+        grad = jnp.dot(normt[...], dpb[p, :, cols], preferred_element_type=F32)
+        return grad.astype(BF16).reshape(8, 2, 80, width)
 
     def head_step(h, carry):
         lanes, mask = head_lanes(h)
@@ -626,44 +827,86 @@
             query = proj[0, rows, lanes] * mask
             key = proj[1, keys, lanes] * mask
             grad = dc[rows, lanes] * mask
-            share = prob[h, b]
-            wide = share.astype(F32)
+            wide = prob[h, b].astype(F32)
             slope = lax.dot_general(grad, proj[2, keys, lanes], NT, preferred_element_type=F32)
             slope = wide * (slope - jnp.sum(slope * wide, axis=-1, keepdims=True)) * HEAD_DIM ** (-0.5)
             slope = slope.astype(BF16)
             DP[0, rows, lanes] += jnp.dot(slope, key, preferred_element_type=F32)
             DP[1, keys, lanes] += lax.dot_general(slope, query, TN, preferred_element_type=F32)
-            DP[2, keys, lanes] += lax.dot_general(share, grad, TN, preferred_element_type=F32)
-
-        @pl.when(h == 3)
-        def _():
-            summed(3)
-            z_start(1)
+
+        @pl.when(h == 1)
+        def _():
+            summed_l(0)
+
+        @pl.when(h == 4)
+        def _():
+            for p in range(2):
+                ga[p] = part_grad(p, 0, N_LEFT)
+                ca_copy(p).start()
+
+        @pl.when(h == 6)
+        def _():
+            summed_a(0)
+            summed_a(1)
 
         return carry
 
     lax.fori_loop(0, 8, head_step, 0)
-    loads[7].wait()
+    for p in range(2):
+        gb[p] = part_grad(p, N_LEFT, 640 - N_LEFT)
+        cb_copy(p).start()
+
+    for i in range(3):
+        z_copy(i).wait_recv()
+    mine = Z[z % 2, z // 2].astype(F32)
+    for i in range(3):
+        mine = mine + ZR[i].astype(F32)
+    E2[...] = mine.astype(BF16)
+    for i in (0, 2, 1):
+        x2_copy(i).start()
     loads[8].wait()
 
-    def weight_grad(p):
-        dpb[p] = DP[p].astype(BF16)
-        g[p] = (
-            jnp.dot(normt[...], dpb[p], preferred_element_type=F32).astype(BF16).reshape(8, 2, 80, 640)
-        )
-        core_copy(p).start()
-
-    def input_step(t, carry):
-        rows = pl.ds(pl.multiple_of(t * 128, 128), 128)
-        slope = jnp.zeros((128, 1280), F32)
+    def input_dot(half):
+        total = jnp.zeros((512, 640), F32)
         for p in range(3):
-            slope += lax.dot_general(
-                dpb[p, rows, :],
-                wq[:, :, 640 * p : 640 * p + 640].reshape(1280, 640),
+            total += lax.dot_general(
+                dpb[p],
+                wq[8 * half : 8 * half + 8, :, 640 * p : 640 * p + 640].reshape(640, 640),
                 NT,
                 preferred_element_type=F32,
             )
-        slope = slope.astype(BF16).astype(F32) * ng[...]
+        wof[half, 0:512, :] = total
+
+    input_dot(0)
+    summed_b(0)
+    summed_b(1)
+    for i in range(3):
+        yb_copy(i).start()
+    for i in range(3):
+        x2_copy(i).wait_recv()
+    mine = E2[x].astype(F32)
+    for i in range(3):
+        mine = mine + XR2[i].astype(F32)
+    El[...] = mine.astype(BF16)
+    owners_send(*last_l)
+    input_dot(1)
+
+    for p in range(2):
+        for i in range(3):
+            xa_copy(p, i).wait_recv()
+        mine = Sa[p, pl.ds(2 * x, 2)].astype(F32)
+        for i in range(3):
+            mine = mine + XRa[i, p].astype(F32)
+        E1[0, p] = mine[0].astype(BF16)
+        E1[1, p] = mine[1].astype(BF16)
+    for i in (0, 2, 1):
+        z2_copy(i).start()
+    owners_sum(*last_l, *more_l)
+
+    def input_step(t, carry):
+        rows = pl.ds(pl.multiple_of(t * 128, 128), 128)
+        slope = jnp.concatenate([wof[0, rows, :], wof[1, rows, :]], axis=1)
+        slope = slope.astype(BF16).astype(F32) * ng[...].reshape(1, 1280)
         value = xin[rows, :].astype(F32)
         factor = lax.rsqrt(jnp.mean(value * value, axis=-1, keepdims=True) + EPSILON)
         unit = value * factor
@@ -671,126 +914,74 @@
         lg[rows, :] = (grad + n2[rows, :]).astype(BF16)
         return carry
 
-    weight_grad(0)
-    weight_grad(1)
-    summed(0)
+    lax.fori_loop(0, 4, input_step, 0)
+
+    for i in range(3):
+        yb_copy(i).wait_recv()
+    mine = Sb[yl, yh].astype(F32)
+    for i in range(3):
+        mine = mine + YRb[i].astype(F32)
+    Eb2[...] = mine.astype(BF16)
     for i in (0, 2, 1):
-        x_copy(0, i).start()
-    weight_grad(2)
-    summed(1)
-    for i in (0, 2, 1):
-        x_copy(1, i).start()
-    lax.fori_loop(0, 1, input_step, 0)
-    summed(2)
-    z_start(0)
-    lax.fori_loop(1, 4, input_step, 0)
-
-    for i in range(3):
-        z_copy(i).wait_recv()
-    mine = Z[z % 2, z // 2].astype(F32)
-    for i in range(3):
-        mine = mine + ZR[i].astype(F32)
-    E2[...] = mine.astype(BF16)
-
-    def x2_copy(i):
-        return remote(E2.at[(x + i + 1) % 4], XR2.at[i], x2s.at[i], x2r.at[i], xp[i])
-
-    for i in (0, 2, 1):
-        x2_copy(i).start()
-    for p in range(2):
-        for i in range(3):
-            x_copy(p, i).wait_recv()
-        mine = S[p, pl.ds(2 * x, 2)].astype(F32)
-        for i in range(3):
-            mine = mine + XR[i, p].astype(F32)
-        E1[0, p] = mine[0].astype(BF16)
-        E1[1, p] = mine[1].astype(BF16)
-
-    def z2_copy(i):
-        t = (z + i + 1) % 4
-        return remote(E1.at[t // 2, t % 2], ZR2.at[i], z2s.at[i], z2r.at[i], zp[i])
-
-    for i in (0, 2, 1):
-        z2_copy(i).start()
-    for i in range(3):
-        x2_copy(i).wait_recv()
-    mine = E2[x].astype(F32)
-    for i in range(3):
-        mine = mine + XR2[i].astype(F32)
-    E[1] = mine.astype(BF16)
+        xb_copy(i).start()
+
     for i in range(3):
         z2_copy(i).wait_recv()
     mine = E1[z // 2, z % 2].astype(F32)
     for i in range(3):
         mine = mine + ZR2[i].astype(F32)
-    E[0] = mine.astype(BF16)
-
-    def y_copy(i):
-        return remote(E, YR.at[i], ys.at[i], yr.at[i], (p1, p2, yhp)[i])
-
-    owner = yh == z // 2
-
-    @pl.when(owner)
-    def _():
-        y_copy(0).start()
-        for i in range(3):
-            y_copy(i).wait_recv()
-        F[...] = (
-            (E[...].astype(F32) + YR[0].astype(F32) + YR[1].astype(F32) + YR[2].astype(F32)) * (1.0 / 128.0)
-        ).astype(BF16)
-        y_copy(0).wait_send()
-
-    @pl.when(jnp.logical_not(owner))
-    def _():
-        for i in (1, 2):
-            y_copy(i).start()
-        for i in (1, 2):
-            y_copy(i).wait_send()
-
-    def f_copy(i):
-        return remote(F, FR.at[z % 2], fs.at[i], fr.at[z % 2], zp[i])
-
-    @pl.when(owner)
-    def _():
-        for i in range(3):
-            f_copy(i).start()
-        FR[z % 2] = F[...]
-
-    def f_wait(slot):
-        pltpu.make_async_copy(FR.at[slot], FR.at[slot], fr.at[slot]).wait()
-
-    @pl.when(owner)
-    def _():
-        f_wait(1 - z % 2)
-        for i in range(3):
-            f_copy(i).wait_send()
-
-    @pl.when(jnp.logical_not(owner))
-    def _():
-        f_wait(0)
-        f_wait(1)
-
-    for p in range(3):
-        pout[:, 640 * p : 640 * p + 640] = FR[p % 2, p // 2].astype(F32)
-    last = FR[1, 1].astype(F32)
+    Ea[...] = mine.astype(BF16)
+    owners_send(*last_a)
+
+    for i in range(3):
+        xb_copy(i).wait_recv()
+    mine = Eb2[x].astype(F32)
+    for i in range(3):
+        mine = mine + XRb[i].astype(F32)
+    Zb[z] = mine.astype(BF16)
+    for i in (0, 2, 1):
+        zb_copy(i).start()
+    owners_sum(*last_a, *more_a)
+    for i in range(3):
+        there = (z + 3 - i) % 4
+        pltpu.make_async_copy(Zb.at[there], Zb.at[there], zbr.at[i]).wait()
+    total = (Zb[0].astype(F32) + Zb[1].astype(F32)) + (Zb[2].astype(F32) + Zb[3].astype(F32))
+    Fb[yl] = (total * (1.0 / 128.0)).astype(BF16)
+    pb_copy().start()
+
+    owners_end(*last_l, *more_l)
+    pout[:, 1280:1920] = FRl[0].astype(F32)
+    last = FRl[1].astype(F32)
     oout[:, 0:640] = last[0:40]
     oout[:, 640:1280] = last[40:80]
-
-    for p in range(4):
-        core_copy(p).wait_send()
+    owners_end(*last_a, *more_a)
+    other = 1 - yl
+    pltpu.make_async_copy(Fb.at[other], Fb.at[other], pbr.at[0]).wait()
+    for p in range(2):
+        pout[:, 640 * p : 640 * p + N_LEFT] = FRa[p].astype(F32)
+        pout[:, 640 * p + N_LEFT : 640 * p + 640] = Fb[p].astype(F32)
+
+    pb_copy().wait_send()
+    for p in range(2):
+        cl_copy(p).wait_send()
+        ca_copy(p).wait_send()
+        cb_copy(p).wait_send()
     for i in range(3):
         for p in range(2):
-            x_copy(p, i).wait_send()
+            xa_copy(p, i).wait_send()
         z_copy(i).wait_send()
         x2_copy(i).wait_send()
         z2_copy(i).wait_send()
+        yb_copy(i).wait_send()
+        xb_copy(i).wait_send()
+        zb_copy(i).wait_send()
 
 
 def block_grads(cot, wq, wo, normt, proj, prob, combt, n2, r2, xin, ng, mg):
     vm = pl.BlockSpec(memory_space=pltpu.VMEM)
     hbm = pl.BlockSpec(memory_space=pl.ANY)
     dma = pltpu.SemaphoreType.DMA
-    t = (80, 640)
+    t, ta, tb = (80, 640), (80, N_LEFT), (80, 640 - N_LEFT)
     held = (cot, wq, wo, normt, proj, prob, combt, n2, r2)
     return pl.pallas_call(
         block_kernel,
@@ -809,28 +1000,39 @@
             pltpu.VMEM((2, 640, 640), F32),
             pltpu.VMEM((3, 512, 640), F32),
             pltpu.VMEM((3, 512, 640), BF16),
-            pltpu.VMEM((4, 8, 2) + t, BF16),
-            pltpu.VMEM((4, 8) + t, BF16),
+            pltpu.VMEM((2, 8, 2) + t, BF16),
+            pltpu.VMEM((2, 8, 2) + ta, BF16),
+            pltpu.VMEM((2, 8, 2) + tb, BF16),
             pltpu.VMEM((2, 8) + t, BF16),
+            pltpu.VMEM((2, 8) + ta, BF16),
+            pltpu.VMEM((2, 8) + tb, BF16),
             pltpu.VMEM((2, 2, 4) + t, BF16),
-            pltpu.VMEM((3, 2, 2) + t, BF16),
             pltpu.VMEM((3, 4) + t, BF16),
-            pltpu.VMEM((2, 2) + t, BF16),
             pltpu.VMEM((4,) + t, BF16),
             pltpu.VMEM((3,) + t, BF16),
+            pltpu.VMEM(t, BF16),
             pltpu.VMEM((3,) + t, BF16),
+            pltpu.VMEM(t, BF16),
             pltpu.VMEM((2,) + t, BF16),
-            pltpu.VMEM((3, 2) + t, BF16),
-            pltpu.VMEM((2,) + t, BF16),
-            pltpu.VMEM((2, 2) + t, BF16),
+            pltpu.VMEM((2, 8) + ta, BF16),
+            pltpu.VMEM((3, 2, 2) + ta, BF16),
+            pltpu.VMEM((2, 2) + ta, BF16),
+            pltpu.VMEM((3,) + ta, BF16),
+            pltpu.VMEM(ta, BF16),
+            pltpu.VMEM((3,) + ta, BF16),
+            pltpu.VMEM(ta, BF16),
+            pltpu.VMEM((2,) + ta, BF16),
+            pltpu.VMEM((2, 2, 4) + tb, BF16),
+            pltpu.VMEM((3, 4) + tb, BF16),
+            pltpu.VMEM((4,) + tb, BF16),
+            pltpu.VMEM((3,) + tb, BF16),
+            pltpu.VMEM((4,) + tb, BF16),
+            pltpu.VMEM((2,) + tb, BF16),
             dma((9,)),
-            dma((4,)), dma((4,)),
-            dma((2, 3)), dma((2, 3)),
-            dma((3,)), dma((3,)),
-            dma((3,)), dma((3,)),
-            dma((3,)), dma((3,)),
-            dma((3,)), dma((3,)),
-            dma((3,)), dma((2,)),
+            dma((2,)), dma((2,)), dma((2,)), dma((2,)), dma((2,)), dma((2,)),
+            dma((3,)), dma((3,)), dma((3,)), dma((3,)), dma((3,)), dma((3,)), dma((3,)), dma((2,)),
+            dma((2, 3)), dma((2, 3)), dma((3,)), dma((3,)), dma((3,)), dma((3,)), dma((3,)), dma((2,)),
+            dma((3,)), dma((3,)), dma((3,)), dma((3,)), dma((3,)), dma((3,)), dma((1,)), dma((1,)),
         ],
         compiler_params=pltpu.CompilerParams(
             collective_id=2, has_side_effects=True, vmem_limit_bytes=62 << 20
@@ -852,12 +1054,11 @@
     qkv_weight,
     proj_weight,
 ):
-    norm_row, merge_row = norm_gain.reshape(1, 1280), merge_gain.reshape(1, 1280)
     kept = merger(
         token_grads, token_dest.reshape(1, 64), merger_down, merger_up, merger_pre, qkv_weight, proj_weight,
-        layer_input, window_ids, norm_row, merge_row,
+        layer_input, window_ids, norm_gain, merge_gain,
     )
-    return block_grads(*kept, layer_input, norm_row, merge_row)
+    return block_grads(*kept, layer_input, norm_gain, merge_gain)
 
 
 def solution(mesh):

time: 216 us -> 187 us (0.87)
  Pallas kernels: 204 us -> 179 us
  local copies, waits for them, and re-layouts: 6.63 us -> 4.04 us
    pallas_call x1, Pallas kernels: 78.2 us -> 64.6 us  [block_grads(): pl.pallas_call(block_kernel, name='block', out_shape=(jax.ShapeDtypeStruc...]
    pallas_call x1, Pallas kernels: 126 us -> 115 us  [merger(): pl.pallas_call(merger_kernel, name='merger', out_shape=tuple((jax.ShapeDt...]
    reshape x2 -> x0, local copies, waits for them, and re-layouts: 2.59 us -> none  [the longest x1 1.29 us: local(): norm_gain.reshape(1, 1280)]
where the time goes in v3:
time: 187 us; the launch traced here: 184 us
  Pallas kernels  179 us (96%)
  local copies, waits for them, and re-layouts  4.04 us (2%)
    pallas_call x1, Pallas kernels, merger(): pl.pallas_call(merger_kernel, name='merger', out_shape=tuple((jax.ShapeDt...  115 us
    pallas_call x1, Pallas kernels, block_grads(): pl.pallas_call(block_kernel, name='block', out_shape=(jax.ShapeDtypeStruc...  64.6 us
    unnamed x7, local copies, waits for them, and re-layouts  4.04 us

profile of v3, /device:TPU:0, one launch (start us, length us, event | category | flops | bytes accessed | tf_op | source)
XLA Modules:
  0.0 184.1 jit_solution(3158274849458495002)
XLA Ops:
  0.6 114.8 %merger.1 = (bf16[512,1280]{1,0:T(8,128)(2,1)}, bf16[16,80,1920]{2,1,0:T(8,128)(2,1)}, bf16[640,1280]{1,0:T(8,128)(2,1)}, bf16[1280,512]{1,0:T(8,128)(2,1)}, bf1...) custom-call(bf16[64,8192]{1,0:T(8,128)(2,1)} %tok.1, ...), custom_call_target="tpu_custom_call" | custom-call | flops 8999999488 | bytes 40000000 | tf_op jit(solution)/shard_map/merger/pallas_call | solution.py:569
  115.5 64.6 %block.1 = (bf16[512,1280]{1,0:T(8,128)(2,1)}, f32[80,1920]{1,0:T(8,128)}, f32[40,1280]{1,0:T(8,128)}) custom-call(bf16[512,1280]{1,0:T(8,128)(2,1)} %get-tuple-element.12.cot_i, bf16[16,80,1920]{2,1,0:T(8,128)(2,1)} %get-tuple-element.13.wq_i, bf16[640,1280]{1,0:T(8,128)(2,1)} %get-tuple-element.14.wo_i, bf16[1280,512]{1,0:T(8,128)(2,1)} %get-tuple-element.15.normt_i, ...), custom_call_target="tpu_custom_call" | custom-call | flops 8000000000 | bytes 40000000 | tf_op jit(solution)/shard_map/block/pallas_call | solution.py:986
  180.1 0.0 copy-start
  180.1 0.0 copy-start.1
  180.1 2.5 %copy.17 = bf16[512,1280]{1,0:T(8,128)(2,1)} copy(bf16[512,1280]{1,0:T(8,128)(2,1)} %get-tuple-element.24) | data formatting | bytes 2621440
  182.6 0.0 copy-done
  182.6 0.8 copy.18
  183.4 0.0 copy-done.1
  183.4 0.7 copy.19
Async XLA Ops:
  180.1 2.6 %copy-start = (f32[80,1920]{1,0:T(8,128)S(1)}, f32[80,1920]{1,0:T(8,128)}, u32[]{:S(2)}) copy-start(f32[80,1920]{1,0:T(8,128)} %get-tuple-element.25) | copy-start | bytes 1843204
  180.1 3.4 %copy-start.1 = (f32[40,1280]{1,0:T(8,128)S(1)}, f32[40,1280]{1,0:T(8,128)}, u32[]{:S(2)}) copy-start(f32[40,1280]{1,0:T(8,128)} %get-tuple-element.26) | copy-start | bytes 614404

commit v4 on v3

--- a/solution.py
+++ b/solution.py
@@ -42,6 +42,21 @@
     return pl.ds(pl.multiple_of(start, 128), 256), mask
 
 
+def overlap(parts):
+    a, b, c, d = parts
+    return jnp.concatenate(
+        [
+            a[0:64],
+            a[64:192] + b[0:128],
+            a[192:256] + b[128:192] + c[0:64],
+            b[192:256] + c[64:128] + d[0:64],
+            c[128:256] + d[64:192],
+            d[192:256],
+        ],
+        axis=0,
+    )
+
+
 def place():
     d, l = lax.axis_index("dp"), lax.axis_index("llm")
     return d // 4, (d // 2) % 2, d % 2, l // 2, l % 2
@@ -61,16 +76,19 @@
     barrier = pltpu.get_barrier_semaphore()
     for device in devices:
         pl.semaphore_signal(barrier, inc=1, device_id=device, device_id_type=MESH)
-    pl.semaphore_wait(barrier, len(devices))
+
+
+def met(devices):
+    pl.semaphore_wait(pltpu.get_barrier_semaphore(), len(devices))
 
 
 def merger_kernel(
     tok, dest, down, up, pre, qw, ow, xin, win, ng, mg,
     cot_o, wq_o, wo_o, normt_o, proj_o, prob_o, combt_o, n2_o, r2_o,
     G, down_v, slope, acc, pg, pre2,
-    S, R, own, T, T0, ZR, M, OUT, A,
+    S, R, own, T, T0, ZR, QS, QR, Q0, M, OUT, A,
     cot, wq, wo, wo2, norm, normt, proj, prob, combt, n2, r2, bias,
-    loc, dsem, os_, or_, outs, zs, zr, ns, nr, ys, yr, ps, pr, ws, wr, xs, xr, cs, cr, rys, ryr, rzs, rzr, as_, ar,
+    loc, dsem, os_, or_, outs, zs, zr, ns, nr, ys, yr, ps, pr, ws, wr, xs, xr, cs, cr, rys, ryr, rzs, rzr, qs, qr, as_, ar,
 ):
     x, yh, c, z, yl = place()
     d = (x * 2 + yh) * 2 + c
@@ -88,6 +106,7 @@
     for k in range(4):
         pltpu.make_async_copy(down.at[:, pl.ds(1024 * k, 1024)], down_v.at[k], dsem.at[k]).start()
     greet(zp + [p1, p2] + dps)
+    met(zp + [p1, p2] + dps)
     cp_tok.wait()
 
     W = G.shape[2] // N_TOK
@@ -221,16 +240,24 @@
 
     def head_step(h):
         lanes, mask = head_lanes(h)
+        shares = []
         for b in range(4):
-            rows, keys = pl.ds(128 * b, 128), pl.ds(KEYS[b], 256)
             scores = lax.dot_general(
-                proj[0, rows, lanes] * mask, proj[1, keys, lanes], NT, preferred_element_type=F32
+                proj[0, pl.ds(128 * b, 128), lanes] * mask,
+                proj[1, pl.ds(KEYS[b], 256), lanes],
+                NT,
+                preferred_element_type=F32,
             )
             scores = scores * HEAD_DIM ** (-0.5) + bias[b]
             powers = jnp.exp(scores - jnp.max(scores, axis=-1, keepdims=True))
-            share = (powers / jnp.sum(powers, axis=-1, keepdims=True)).astype(BF16)
-            prob[h, b] = share
-            combf[rows, lanes] += jnp.dot(share, proj[2, keys, lanes] * mask, preferred_element_type=F32)
+            shares.append((powers * (1.0 / jnp.sum(powers, axis=-1, keepdims=True))).astype(BF16))
+        parts = [
+            jnp.dot(shares[b], proj[2, pl.ds(KEYS[b], 256), lanes] * mask, preferred_element_type=F32)
+            for b in range(4)
+        ]
+        for b in range(4):
+            prob[h, b] = shares[b]
+        combf[:, lanes] += jnp.concatenate(parts, axis=0)
 
     def output_step():
         comb = combf[...].astype(BF16)
@@ -316,9 +343,9 @@
         def _():
             z_forward(k)
 
-        @pl.when(k == N_TOK)
-        def _():
-            multiply(k - 2)
+        @pl.when(k >= 3)
+        def _():
+            multiply(jnp.where(k == N_TOK, N_TOK - 2, k - 3))
 
         @pl.when(k >= 1)
         def _():
@@ -333,10 +360,6 @@
                     cp.start()
             for cp in w_copies(None, d2, cs.at[1], cr.at[1], core):
                 cp.start()
-
-        @pl.when((k >= 3) & (k < N_TOK))
-        def _():
-            multiply(k - 3)
 
         @pl.when(k >= N_TOK - 1)
         def _():
@@ -405,7 +428,7 @@
         emit(1, wq, wq_o).start()
         emit(2, wo2, wo_o).start()
 
-    def first_product(i):
+    def product(i):
         up_copy(i).wait()
         part = lax.dot_general(pg[...], down_v[i % 4, :, 0:V], NT, preferred_element_type=F32)
 
@@ -413,12 +436,47 @@
         def _():
             up_copy(i + 4).start()
 
-        part = part.reshape(4, 128, V)
-        S[i, 0] = part[:, 64:96, :].astype(BF16)
-        S[i, 1] = part[:, 96:128, :].astype(BF16)
+        return part.reshape(4, 128, V)
+
+    def q_copy(f, i):
+        return remote(QS.at[f, i], QR.at[f, i], qs.at[f, i], qr.at[f, i], zp[i])
+
+    def z_product(f, carry):
+        part = product(f)
+        QS[f] = part[1:4].astype(BF16)
+        for i in (0, 2, 1):
+            q_copy(f, i).start()
+        Q0[f] = part[0]
+        return carry
+
+    def z_sum(f):
+        for i in range(3):
+            q_copy(f, i).wait_recv()
+        total = Q0[f] + QR[f, 0].astype(F32) + QR[f, 1].astype(F32) + QR[f, 2].astype(F32)
+        S[f, 0, 0] = total[64:96].astype(BF16)
+        S[f, 1, 0] = total[96:128].astype(BF16)
+        Q0[f, 0:64] = total[0:64]
+        for i in range(2):
+            qy_copy(f, i).start()
+
+    def qy_copy(f, i):
+        return remote(S.at[f, i, 0], R.at[f, i, 0], rys.at[f, i], ryr.at[f, i], (p1, p2)[i])
+
+    def z_end(f):
+        for i in range(2):
+            qy_copy(f, i).wait_recv()
+        M[f] = (
+            Q0[f, 0:64] + jnp.concatenate([R[f, 0, 0].astype(F32), R[f, 1, 0].astype(F32)], axis=0)
+        ).astype(BF16)
+
+    def y_product(f, carry):
+        part = product(f)
+        S[f, 0] = part[:, 64:96, :].astype(BF16)
+        S[f, 1] = part[:, 96:128, :].astype(BF16)
         for h in range(2):
-            ry_copy(i, h).start()
-        own[i % 4] = part[:, 0:64, :]
+            ry_copy(f, h).start()
+        own[f % 4] = part[:, 0:64, :]
+        return carry
 
     def over_y(f):
         for h in range(2):
@@ -444,46 +502,66 @@
         here = pl.ds(pl.multiple_of(d * 16, 16), 16)
         A[j, here, :] = OUT[j, here, :]
 
-    def open_step(i, carry):
-        first_product(i)
+    lax.fori_loop(0, 2, z_product, 0)
+    lax.fori_loop(2, 5, y_product, 0)
+    x_arrive(1)
+
+    def late_head(h, carry):
+        head_step(h)
         return carry
-
-    lax.fori_loop(0, 3, open_step, 0)
-    x_arrive(1)
 
     def sum_step(f, carry):
         over_y(f)
 
         @pl.when(f + 3 < N_FEAT)
         def _():
-            first_product(f + 3)
-
-        @pl.when(f >= 2)
-        def _():
-            over_z(f - 2)
-
-        @pl.when((f >= 3) & (f % 2 == 1))
-        def _():
-            send_rows(f // 2 - 1)
-
-        @pl.when(f == 0)
+            y_product(f + 3, 0)
+
+        @pl.when(f == 2)
         def _():
             weights_arrive()
+
+        @pl.when(f == 3)
+        def _():
             lax.fori_loop(0, 3, qkv_step, 0)
             emit(4, proj, proj_o).start()
 
-        @pl.when(f >= 1)
-        def _():
-            head_step(f - 1)
+        @pl.when((f == 4) | (f == 5))
+        def _():
+            head_step(f - 4)
+
+        @pl.when(f >= 6)
+        def _():
+            lax.fori_loop(2 * f - 10, 2 * f - 8, late_head, 0)
+
+        @pl.when(f >= 4)
+        def _():
+            over_z(f - 2)
+
+        @pl.when((f == 3) | (f == 4))
+        def _():
+            z_sum(f - 3)
+
+        @pl.when(f == 5)
+        def _():
+            z_end(0)
+            z_end(1)
+            send_rows(jnp.int32(0))
+
+        @pl.when((f == 5) | (f == 7))
+        def _():
+            send_rows((f - 3) // 2)
 
         return carry
 
-    lax.fori_loop(0, N_FEAT, sum_step, 0)
+    lax.fori_loop(2, N_FEAT, sum_step, 0)
     over_z(N_FEAT - 2)
+    head_step(6)
+    over_z(N_FEAT - 1)
+    send_rows(3)
+
     head_step(7)
     emit(5, prob, prob_o).start()
-    over_z(N_FEAT - 1)
-    send_rows(3)
     normt[...] = norm[...].astype(F32).T.astype(BF16)
     emit(3, normt, normt_o).start()
     output_step()
@@ -537,7 +615,12 @@
             rz_copy(f, i).wait_send()
         return carry
 
-    lax.fori_loop(0, N_FEAT, drain2, 0)
+    lax.fori_loop(2, N_FEAT, drain2, 0)
+    for f in range(2):
+        for i in range(3):
+            q_copy(f, i).wait_send()
+        for i in range(2):
+            qy_copy(f, i).wait_send()
     for j in range(4):
         pltpu.make_async_copy(OUT.at[j, fifteen], OUT.at[j, fifteen], as_.at[j]).wait()
     pairs = [
@@ -585,6 +668,9 @@
             pltpu.VMEM((N_FEAT, 3, 64, V), BF16),
             pltpu.VMEM((4, 64, V), F32),
             pltpu.VMEM((N_FEAT, 3, 64, V), BF16),
+            pltpu.VMEM((2, 3, 128, V), BF16),
+            pltpu.VMEM((2, 3, 128, V), BF16),
+            pltpu.VMEM((2, 128, V), F32),
             pltpu.VMEM((N_FEAT, 64, V), BF16),
             pltpu.VMEM((4, 256, V), BF16),
             pltpu.VMEM((4, 256, V), BF16),
@@ -611,6 +697,7 @@
             dma((8, 2)), dma((8, 2)),
             dma((N_FEAT, 2)), dma((N_FEAT, 2)),
             dma((N_FEAT, 3)), dma((N_FEAT, 3)),
+            dma((2, 3)), dma((2, 3)),
             dma((4,)), dma((4,)),
         ],
         compiler_params=pltpu.CompilerParams(
@@ -625,10 +712,14 @@
     lg, pout, oout,
     cot, wq, wo, normt, proj, prob, combt, n2, r2,
     db, dc, wof, DP, dpb,
-    gl, ga, gb, Cl, Ca, Cb, Z, ZR, E2, XR2, El, YRl, Fl, FRl,
-    Sa, XRa, E1, ZR2, Ea, YRa, Fa, FRa, Sb, YRb, Eb2, XRb, Zb, Fb,
-    ins, cls, clr, cas, car, cbs, cbr, zs, zr, x2s, x2r, yls, ylr, fls, flr,
-    xas, xar, z2s, z2r, yas, yar, fas, far, ybs, ybr, xbs, xbr, zbs, zbr, pbs, pbr,
+    gl, ga, Cl, Ca, Z, ZR, E2, XR2, El, YRl, Fl, FRl,
+    Sa, XRa, E1, ZR2, Ea, YRa, Fa, FRa,
+    gm, Cm, Sm, YRm, Em, XRm, Zm, Fm,
+    gb, Cb, Sb, YRb, Eb, XRb, Zb, Fb,
+    ins, cls, clr, cas, car, zs, zr, x2s, x2r, yls, ylr, fls, flr,
+    xas, xar, z2s, z2r, yas, yar, fas, far,
+    cms, cmr, yms, ymr, xms, xmr, zms, zmr, pms, pmr,
+    cbs, cbr, ybs, ybr, xbs, xbr, zbs, zbr, pbs, pbr,
 ):
     x, yh, c, z, yl = place()
     pairs = [
@@ -636,24 +727,22 @@
         (normt_i, normt), (wq_i, wq),
     ]
     loads = [pltpu.make_async_copy(a, b, ins.at[n]) for n, (a, b) in enumerate(pairs)]
-    for cp in loads:
-        cp.start()
     zp = [at(x, yh, c, (z + s) % 4, yl) for s in (1, 2, 3)]
     xp = [at((x + s) % 4, yh, c, z, yl) for s in (1, 2, 3)]
     core = at(x, yh, 1 - c, z, yl)
     p1 = at(x, yh, c, z, 1 - yl)
     p2 = at(x, 1 - yh, c, z, 1 - yl)
     yhp = at(x, 1 - yh, c, z, yl)
+
     greet(zp + xp + [core, p1, p2, yhp])
+    for cp in loads[:3]:
+        cp.start()
 
     def cl_copy(p):
         return remote(gl.at[p, :, 1 - c], Cl.at[p], cls.at[p], clr.at[p], core)
 
     def ca_copy(p):
         return remote(ga.at[p, :, 1 - c], Ca.at[p], cas.at[p], car.at[p], core)
-
-    def cb_copy(p):
-        return remote(gb.at[p, :, 1 - c], Cb.at[p], cbs.at[p], cbr.at[p], core)
 
     def z_copy(i):
         t = (z + i + 1) % 4
@@ -661,7 +750,7 @@
 
     def summed_l(p):
         cl_copy(p).wait_recv()
-        total = (gl[p, :, c].astype(F32) + Cl[p].astype(F32)).astype(BF16).reshape(4, 2, 80, 640)
+        total = (gl[p, :, c].astype(F32) + Cl[p].astype(F32)).astype(BF16).reshape(4, 2, 80, N_LEFT)
         Z[p, 0] = total[:, 0]
         Z[p, 1] = total[:, 1]
         for i in (0, 2, 1):
@@ -688,30 +777,88 @@
         t = (z + i + 1) % 4
         return remote(E1.at[t // 2, t % 2], ZR2.at[i], z2s.at[i], z2r.at[i], zp[i])
 
-    def yb_copy(i):
-        return remote(
-            Sb.at[(1 - yl, 1 - yl, yl)[i], (yh, 1 - yh, 1 - yh)[i]],
-            YRb.at[i],
-            ybs.at[i],
-            ybr.at[i],
-            (p1, p2, yhp)[i],
-        )
-
-    def summed_b(p):
-        cb_copy(p).wait_recv()
-        total = (gb[p, :, c].astype(F32) + Cb[p].astype(F32)).astype(BF16)
-        total = total.reshape((4, 2) + total.shape[1:])
-        Sb[p, 0] = total[:, 0]
-        Sb[p, 1] = total[:, 1]
-
-    def xb_copy(i):
-        return remote(Eb2.at[(x + i + 1) % 4], XRb.at[i], xbs.at[i], xbr.at[i], xp[i])
-
-    def zb_copy(i):
-        return remote(Zb.at[z], Zb.at[z], zbs.at[i], zbr.at[i], zp[i])
-
-    def pb_copy():
-        return remote(Fb.at[yl], Fb.at[yl], pbs.at[0], pbr.at[0], p1)
+    def y_first(g, C, S, YR, E, XR, ZZ, F, cs, cr, ys, yr, xs, xr, zs, zr, ps, pr):
+        def c_copy(p):
+            return remote(g.at[p, :, 1 - c], C.at[p], cs.at[p], cr.at[p], core)
+
+        def y_copy(i):
+            return remote(
+                S.at[(1 - yl, 1 - yl, yl)[i], (yh, 1 - yh, 1 - yh)[i]],
+                YR.at[i],
+                ys.at[i],
+                yr.at[i],
+                (p1, p2, yhp)[i],
+            )
+
+        def x_copy(i):
+            return remote(E.at[(x + i + 1) % 4], XR.at[i], xs.at[i], xr.at[i], xp[i])
+
+        def z_copy(i):
+            return remote(ZZ.at[z], ZZ.at[z], zs.at[i], zr.at[i], zp[i])
+
+        def p_copy():
+            return remote(F.at[yl], F.at[yl], ps.at[0], pr.at[0], p1)
+
+        def add_cores(p):
+            c_copy(p).wait_recv()
+            total = (g[p, :, c].astype(F32) + C[p].astype(F32)).astype(BF16)
+            total = total.reshape((4, 2) + total.shape[1:])
+            S[p, 0] = total[:, 0]
+            S[p, 1] = total[:, 1]
+
+        def start_y():
+            for i in range(3):
+                y_copy(i).start()
+
+        def add_y():
+            for i in range(3):
+                y_copy(i).wait_recv()
+            mine = S[yl, yh].astype(F32)
+            for i in range(3):
+                mine = mine + YR[i].astype(F32)
+            E[...] = mine.astype(BF16)
+            for i in (0, 2, 1):
+                x_copy(i).start()
+
+        def add_x():
+            for i in range(3):
+                x_copy(i).wait_recv()
+            mine = E[x].astype(F32)
+            for i in range(3):
+                mine = mine + XR[i].astype(F32)
+            ZZ[z] = mine.astype(BF16)
+            for i in (0, 2, 1):
+                z_copy(i).start()
+
+        def add_z():
+            for i in range(3):
+                there = (z + 3 - i) % 4
+                pltpu.make_async_copy(ZZ.at[there], ZZ.at[there], zr.at[i]).wait()
+            total = (ZZ[0].astype(F32) + ZZ[1].astype(F32)) + (ZZ[2].astype(F32) + ZZ[3].astype(F32))
+            F[yl] = (total * (1.0 / 128.0)).astype(BF16)
+            p_copy().start()
+
+        def finish():
+            other = 1 - yl
+            pltpu.make_async_copy(F.at[other], F.at[other], pr.at[0]).wait()
+
+        def drain():
+            p_copy().wait_send()
+            for p in range(2):
+                c_copy(p).wait_send()
+            for i in range(3):
+                y_copy(i).wait_send()
+                x_copy(i).wait_send()
+                z_copy(i).wait_send()
+
+        return c_copy, add_cores, start_y, add_y, add_x, add_z, finish, drain
+
+    m_core, m_cores, m_start, m_y, m_x, m_z, m_finish, m_drain = y_first(
+        gm, Cm, Sm, YRm, Em, XRm, Zm, Fm, cms, cmr, yms, ymr, xms, xmr, zms, zmr, pms, pmr
+    )
+    b_core, b_cores, b_start, b_y, b_x, b_z, b_finish, b_drain = y_first(
+        gb, Cb, Sb, YRb, Eb, XRb, Zb, Fb, cbs, cbr, ybs, ybr, xbs, xbr, zbs, zbr, pbs, pbr
+    )
 
     owner = yh == z // 2
 
@@ -766,7 +913,8 @@
     loads[0].wait()
     loads[1].wait()
     loads[2].wait()
-    loads[3].wait()
+    for cp in loads[3:]:
+        cp.start()
 
     def out_step(t, carry):
         rows = pl.ds(pl.multiple_of(t * 128, 128), 128)
@@ -778,6 +926,7 @@
         return carry
 
     lax.fori_loop(0, 4, out_step, 0)
+    loads[3].wait()
     dc[...] = lax.dot_general(db[...], wo[...], NT, preferred_element_type=F32).astype(BF16)
     loads[4].wait()
 
@@ -787,56 +936,76 @@
         return carry
 
     lax.fori_loop(0, 2, wo_step, 0)
-    gl[1] = (
+    grad_o = (
         jnp.concatenate([wof[0].reshape(16, 40, 640), wof[1].reshape(16, 40, 640)], axis=1)
         .astype(BF16)
         .reshape(8, 2, 80, 640)
     )
+    gl[1] = grad_o[..., :N_LEFT]
+    gm[1] = grad_o[..., N_LEFT:]
+    met(zp + xp + [core, p1, p2, yhp])
     cl_copy(1).start()
+    m_core(1).start()
 
     DP[...] = jnp.zeros_like(DP)
     loads[5].wait()
 
     def value_step(h, carry):
         lanes, mask = head_lanes(h)
-        for b in range(4):
-            grad = dc[pl.ds(128 * b, 128), lanes] * mask
-            DP[2, pl.ds(KEYS[b], 256), lanes] += lax.dot_general(
-                prob[h, b], grad, TN, preferred_element_type=F32
+        parts = [
+            lax.dot_general(
+                prob[h, b], dc[pl.ds(128 * b, 128), lanes] * mask, TN, preferred_element_type=F32
             )
+            for b in range(4)
+        ]
+        DP[2, :, lanes] += overlap(parts)
         return carry
 
     lax.fori_loop(0, 8, value_step, 0)
-    summed_l(1)
     loads[7].wait()
-    dpb[2] = DP[2].astype(BF16)
-    gl[0] = jnp.dot(normt[...], dpb[2], preferred_element_type=F32).astype(BF16).reshape(8, 2, 80, 640)
-    cl_copy(0).start()
-    loads[6].wait()
-
     def part_grad(p, first, width):
         cols = slice(first, first + width)
         dpb[p, :, cols] = DP[p, :, cols].astype(BF16)
         grad = jnp.dot(normt[...], dpb[p, :, cols], preferred_element_type=F32)
         return grad.astype(BF16).reshape(8, 2, 80, width)
 
+    gl[0] = part_grad(2, 0, N_LEFT)
+    cl_copy(0).start()
+    gm[0] = part_grad(2, N_LEFT, 640 - N_LEFT)
+    m_core(0).start()
+    summed_l(1)
+    m_cores(1)
+    loads[6].wait()
+
     def head_step(h, carry):
         lanes, mask = head_lanes(h)
+        slopes = []
         for b in range(4):
-            rows, keys = pl.ds(128 * b, 128), pl.ds(KEYS[b], 256)
-            query = proj[0, rows, lanes] * mask
-            key = proj[1, keys, lanes] * mask
-            grad = dc[rows, lanes] * mask
+            grad = dc[pl.ds(128 * b, 128), lanes] * mask
             wide = prob[h, b].astype(F32)
-            slope = lax.dot_general(grad, proj[2, keys, lanes], NT, preferred_element_type=F32)
+            slope = lax.dot_general(
+                grad, proj[2, pl.ds(KEYS[b], 256), lanes], NT, preferred_element_type=F32
+            )
             slope = wide * (slope - jnp.sum(slope * wide, axis=-1, keepdims=True)) * HEAD_DIM ** (-0.5)
-            slope = slope.astype(BF16)
-            DP[0, rows, lanes] += jnp.dot(slope, key, preferred_element_type=F32)
-            DP[1, keys, lanes] += lax.dot_general(slope, query, TN, preferred_element_type=F32)
-
-        @pl.when(h == 1)
+            slopes.append(slope.astype(BF16))
+        parts = [
+            jnp.dot(slopes[b], proj[1, pl.ds(KEYS[b], 256), lanes] * mask, preferred_element_type=F32)
+            for b in range(4)
+        ]
+        DP[0, :, lanes] += jnp.concatenate(parts, axis=0)
+        parts = [
+            lax.dot_general(
+                slopes[b], proj[0, pl.ds(128 * b, 128), lanes] * mask, TN, preferred_element_type=F32
+            )
+            for b in range(4)
+        ]
+        DP[1, :, lanes] += overlap(parts)
+
+        @pl.when(h == 0)
         def _():
             summed_l(0)
+            m_cores(0)
+            m_start()
 
         @pl.when(h == 4)
         def _():
@@ -848,23 +1017,14 @@
         def _():
             summed_a(0)
             summed_a(1)
+            m_y()
 
         return carry
 
     lax.fori_loop(0, 8, head_step, 0)
     for p in range(2):
         gb[p] = part_grad(p, N_LEFT, 640 - N_LEFT)
-        cb_copy(p).start()
-
-    for i in range(3):
-        z_copy(i).wait_recv()
-    mine = Z[z % 2, z // 2].astype(F32)
-    for i in range(3):
-        mine = mine + ZR[i].astype(F32)
-    E2[...] = mine.astype(BF16)
-    for i in (0, 2, 1):
-        x2_copy(i).start()
-    loads[8].wait()
+        b_core(p).start()
 
     def input_dot(half):
         total = jnp.zeros((512, 640), F32)
@@ -877,19 +1037,34 @@
             )
         wof[half, 0:512, :] = total
 
+    loads[8].wait()
     input_dot(0)
-    summed_b(0)
-    summed_b(1)
+    b_cores(0)
+    b_cores(1)
+    b_start()
+
     for i in range(3):
-        yb_copy(i).start()
+        z_copy(i).wait_recv()
+    mine = Z[z % 2, z // 2].astype(F32)
     for i in range(3):
-        x2_copy(i).wait_recv()
-    mine = E2[x].astype(F32)
-    for i in range(3):
-        mine = mine + XR2[i].astype(F32)
-    El[...] = mine.astype(BF16)
-    owners_send(*last_l)
+        mine = mine + ZR[i].astype(F32)
+    E2[...] = mine.astype(BF16)
+    for i in (0, 2, 1):
+        x2_copy(i).start()
     input_dot(1)
+
+    def input_step(t, carry):
+        rows = pl.ds(pl.multiple_of(t * 128, 128), 128)
+        slope = jnp.concatenate([wof[0, rows, :], wof[1, rows, :]], axis=1)
+        slope = slope.astype(BF16).astype(F32) * ng[...].reshape(1, 1280)
+        value = xin[rows, :].astype(F32)
+        factor = lax.rsqrt(jnp.mean(value * value, axis=-1, keepdims=True) + EPSILON)
+        unit = value * factor
+        grad = factor * (slope - unit * jnp.mean(slope * unit, axis=-1, keepdims=True))
+        lg[rows, :] = (grad + n2[rows, :]).astype(BF16)
+        return carry
+
+    lax.fori_loop(0, 4, input_step, 0)
 
     for p in range(2):
         for i in range(3):
@@ -901,30 +1076,15 @@
         E1[1, p] = mine[1].astype(BF16)
     for i in (0, 2, 1):
         z2_copy(i).start()
-    owners_sum(*last_l, *more_l)
-
-    def input_step(t, carry):
-        rows = pl.ds(pl.multiple_of(t * 128, 128), 128)
-        slope = jnp.concatenate([wof[0, rows, :], wof[1, rows, :]], axis=1)
-        slope = slope.astype(BF16).astype(F32) * ng[...].reshape(1, 1280)
-        value = xin[rows, :].astype(F32)
-        factor = lax.rsqrt(jnp.mean(value * value, axis=-1, keepdims=True) + EPSILON)
-        unit = value * factor
-        grad = factor * (slope - unit * jnp.mean(slope * unit, axis=-1, keepdims=True))
-        lg[rows, :] = (grad + n2[rows, :]).astype(BF16)
-        return carry
-
-    lax.fori_loop(0, 4, input_step, 0)
-
+    m_x()
+    b_y()
     for i in range(3):
-        yb_copy(i).wait_recv()
-    mine = Sb[yl, yh].astype(F32)
+        x2_copy(i).wait_recv()
+    mine = E2[x].astype(F32)
     for i in range(3):
-        mine = mine + YRb[i].astype(F32)
-    Eb2[...] = mine.astype(BF16)
-    for i in (0, 2, 1):
-        xb_copy(i).start()
-
+        mine = mine + XR2[i].astype(F32)
+    El[...] = mine.astype(BF16)
+    owners_send(*last_l)
     for i in range(3):
         z2_copy(i).wait_recv()
     mine = E1[z // 2, z % 2].astype(F32)
@@ -932,56 +1092,45 @@
         mine = mine + ZR2[i].astype(F32)
     Ea[...] = mine.astype(BF16)
     owners_send(*last_a)
-
-    for i in range(3):
-        xb_copy(i).wait_recv()
-    mine = Eb2[x].astype(F32)
-    for i in range(3):
-        mine = mine + XRb[i].astype(F32)
-    Zb[z] = mine.astype(BF16)
-    for i in (0, 2, 1):
-        zb_copy(i).start()
+    m_z()
+    b_x()
+    owners_sum(*last_l, *more_l)
     owners_sum(*last_a, *more_a)
-    for i in range(3):
-        there = (z + 3 - i) % 4
-        pltpu.make_async_copy(Zb.at[there], Zb.at[there], zbr.at[i]).wait()
-    total = (Zb[0].astype(F32) + Zb[1].astype(F32)) + (Zb[2].astype(F32) + Zb[3].astype(F32))
-    Fb[yl] = (total * (1.0 / 128.0)).astype(BF16)
-    pb_copy().start()
-
+    b_z()
+
+    m_finish()
     owners_end(*last_l, *more_l)
-    pout[:, 1280:1920] = FRl[0].astype(F32)
-    last = FRl[1].astype(F32)
-    oout[:, 0:640] = last[0:40]
-    oout[:, 640:1280] = last[40:80]
+    pout[:, 1280 : 1280 + N_LEFT] = FRl[0].astype(F32)
+    pout[:, 1280 + N_LEFT : 1920] = Fm[0].astype(F32)
+    left, right = FRl[1].astype(F32), Fm[1].astype(F32)
+    oout[:, 0:N_LEFT] = left[0:40]
+    oout[:, N_LEFT:640] = right[0:40]
+    oout[:, 640 : 640 + N_LEFT] = left[40:80]
+    oout[:, 640 + N_LEFT : 1280] = right[40:80]
     owners_end(*last_a, *more_a)
-    other = 1 - yl
-    pltpu.make_async_copy(Fb.at[other], Fb.at[other], pbr.at[0]).wait()
+    b_finish()
     for p in range(2):
         pout[:, 640 * p : 640 * p + N_LEFT] = FRa[p].astype(F32)
         pout[:, 640 * p + N_LEFT : 640 * p + 640] = Fb[p].astype(F32)
 
-    pb_copy().wait_send()
+    m_drain()
+    b_drain()
     for p in range(2):
         cl_copy(p).wait_send()
         ca_copy(p).wait_send()
-        cb_copy(p).wait_send()
     for i in range(3):
         for p in range(2):
             xa_copy(p, i).wait_send()
         z_copy(i).wait_send()
         x2_copy(i).wait_send()
         z2_copy(i).wait_send()
-        yb_copy(i).wait_send()
-        xb_copy(i).wait_send()
-        zb_copy(i).wait_send()
 
 
 def block_grads(cot, wq, wo, normt, proj, prob, combt, n2, r2, xin, ng, mg):
     vm = pl.BlockSpec(memory_space=pltpu.VMEM)
     hbm = pl.BlockSpec(memory_space=pl.ANY)
     dma = pltpu.SemaphoreType.DMA
-    t, ta, tb = (80, 640), (80, N_LEFT), (80, 640 - N_LEFT)
+    ta, tb = (80, N_LEFT), (80, 640 - N_LEFT)
     held = (cot, wq, wo, normt, proj, prob, combt, n2, r2)
     return pl.pallas_call(
         block_kernel,
@@ -1000,20 +1149,18 @@
             pltpu.VMEM((2, 640, 640), F32),
             pltpu.VMEM((3, 512, 640), F32),
             pltpu.VMEM((3, 512, 640), BF16),
-            pltpu.VMEM((2, 8, 2) + t, BF16),
             pltpu.VMEM((2, 8, 2) + ta, BF16),
-            pltpu.VMEM((2, 8, 2) + tb, BF16),
-            pltpu.VMEM((2, 8) + t, BF16),
+            pltpu.VMEM((2, 8, 2) + ta, BF16),
             pltpu.VMEM((2, 8) + ta, BF16),
-            pltpu.VMEM((2, 8) + tb, BF16),
-            pltpu.VMEM((2, 2, 4) + t, BF16),
-            pltpu.VMEM((3, 4) + t, BF16),
-            pltpu.VMEM((4,) + t, BF16),
-            pltpu.VMEM((3,) + t, BF16),
-            pltpu.VMEM(t, BF16),
-            pltpu.VMEM((3,) + t, BF16),
-            pltpu.VMEM(t, BF16),
-            pltpu.VMEM((2,) + t, BF16),
+            pltpu.VMEM((2, 8) + ta, BF16),
+            pltpu.VMEM((2, 2, 4) + ta, BF16),
+            pltpu.VMEM((3, 4) + ta, BF16),
+            pltpu.VMEM((4,) + ta, BF16),
+            pltpu.VMEM((3,) + ta, BF16),
+            pltpu.VMEM(ta, BF16),
+            pltpu.VMEM((3,) + ta, BF16),
+            pltpu.VMEM(ta, BF16),
+            pltpu.VMEM((2,) + ta, BF16),
             pltpu.VMEM((2, 8) + ta, BF16),
             pltpu.VMEM((3, 2, 2) + ta, BF16),
             pltpu.VMEM((2, 2) + ta, BF16),
@@ -1022,18 +1169,29 @@
             pltpu.VMEM((3,) + ta, BF16),
             pltpu.VMEM(ta, BF16),
             pltpu.VMEM((2,) + ta, BF16),
+        ]
+        + [
+            pltpu.VMEM((2, 8, 2) + tb, BF16),
+            pltpu.VMEM((2, 8) + tb, BF16),
             pltpu.VMEM((2, 2, 4) + tb, BF16),
             pltpu.VMEM((3, 4) + tb, BF16),
             pltpu.VMEM((4,) + tb, BF16),
             pltpu.VMEM((3,) + tb, BF16),
             pltpu.VMEM((4,) + tb, BF16),
             pltpu.VMEM((2,) + tb, BF16),
+        ]
+        * 2
+        + [
             dma((9,)),
-            dma((2,)), dma((2,)), dma((2,)), dma((2,)), dma((2,)), dma((2,)),
+            dma((2,)), dma((2,)), dma((2,)), dma((2,)),
             dma((3,)), dma((3,)), dma((3,)), dma((3,)), dma((3,)), dma((3,)), dma((3,)), dma((2,)),
             dma((2, 3)), dma((2, 3)), dma((3,)), dma((3,)), dma((3,)), dma((3,)), dma((3,)), dma((2,)),
-            dma((3,)), dma((3,)), dma((3,)), dma((3,)), dma((3,)), dma((3,)), dma((1,)), dma((1,)),
-        ],
+        ]
+        + [
+            dma((2,)), dma((2,)), dma((3,)), dma((3,)), dma((3,)), dma((3,)), dma((3,)), dma((3,)),
+            dma((1,)), dma((1,)),
+        ]
+        * 2,
         compiler_params=pltpu.CompilerParams(
             collective_id=2, has_side_effects=True, vmem_limit_bytes=62 << 20
         ),

time: 187 us -> 169 us (0.904); the launches traced: 184 us -> 168 us
  Pallas kernels: 179 us -> 164 us
    pallas_call x1, Pallas kernels: 64.6 us -> 54.3 us  [block_grads(): pl.pallas_call(block_kernel, name='block', out_shape=(jax.ShapeDtypeStruc...]
    pallas_call x1, Pallas kernels: 115 us -> 109 us  [merger(): pl.pallas_call(merger_kernel, name='merger', out_shape=tuple((jax.ShapeDt...]
where the time goes in v4:
time: 169 us; the launch traced here: 168 us
  Pallas kernels  164 us (97%)
  local copies, waits for them, and re-layouts  4.04 us (2%)
    pallas_call x1, Pallas kernels, merger(): pl.pallas_call(merger_kernel, name='merger', out_shape=tuple((jax.ShapeDt...  109 us
    pallas_call x1, Pallas kernels, block_grads(): pl.pallas_call(block_kernel, name='block', out_shape=(jax.ShapeDtypeStruc...  54.3 us
    unnamed x7, local copies, waits for them, and re-layouts  4.04 us

profile of v4, /device:TPU:0, one launch (start us, length us, event | category | flops | bytes accessed | tf_op | source)
XLA Modules:
  0.0 168.4 jit_solution(6429122422693942047)
XLA Ops:
  0.6 109.4 %merger.1 = (bf16[512,1280]{1,0:T(8,128)(2,1)}, bf16[16,80,1920]{2,1,0:T(8,128)(2,1)}, bf16[640,1280]{1,0:T(8,128)(2,1)}, bf16[1280,512]{1,0:T(8,128)(2,1)}, bf1...) custom-call(bf16[64,8192]{1,0:T(8,128)(2,1)} %tok.1, ...), custom_call_target="tpu_custom_call" | custom-call | flops 8999999488 | bytes 40000000 | tf_op jit(solution)/shard_map/merger/pallas_call | solution.py:652
  110.1 54.3 %block.1 = (bf16[512,1280]{1,0:T(8,128)(2,1)}, f32[80,1920]{1,0:T(8,128)}, f32[40,1280]{1,0:T(8,128)}) custom-call(bf16[512,1280]{1,0:T(8,128)(2,1)} %get-tuple-element.12.cot_i, bf16[16,80,1920]{2,1,0:T(8,128)(2,1)} %get-tuple-element.13.wq_i, bf16[640,1280]{1,0:T(8,128)(2,1)} %get-tuple-element.14.wo_i, bf16[1280,512]{1,0:T(8,128)(2,1)} %get-tuple-element.15.normt_i, ...), custom_call_target="tpu_custom_call" | custom-call | flops 8000000000 | bytes 40000000 | tf_op jit(solution)/shard_map/block/pallas_call | solution.py:1135
  164.4 0.0 copy-start
  164.4 0.0 copy-start.1
  164.4 2.5 %copy.17 = bf16[512,1280]{1,0:T(8,128)(2,1)} copy(bf16[512,1280]{1,0:T(8,128)(2,1)} %get-tuple-element.24) | data formatting | bytes 2621440
  166.9 0.0 copy-done
  166.9 0.8 copy.18
  167.8 0.0 copy-done.1
  167.8 0.7 copy.19
Async XLA Ops:
  164.4 2.6 %copy-start = (f32[80,1920]{1,0:T(8,128)S(1)}, f32[80,1920]{1,0:T(8,128)}, u32[]{:S(2)}) copy-start(f32[80,1920]{1,0:T(8,128)} %get-tuple-element.25) | copy-start | bytes 1843204
  164.4 3.4 %copy-start.1 = (f32[40,1280]{1,0:T(8,128)S(1)}, f32[40,1280]{1,0:T(8,128)}, u32[]{:S(2)}) copy-start(f32[40,1280]{1,0:T(8,128)} %get-tuple-element.26) | copy-start | bytes 614404

commit v5 on v4

--- a/solution.py
+++ b/solution.py
@@ -15,9 +15,12 @@
 NT = (((1,), (1,)), ((), ()))
 TN = (((0,), (0,)), ((), ()))
 
-N_TOK = 8
-N_NARROW = 5
+N_TOK = 16
+N_NARROW = 10
 N_LEFT = 384
+N_X, N_Z = 256, 256
+AHEAD = 3
+LAG = 7
 N_FEAT = 8
 
 
@@ -86,7 +89,7 @@
     tok, dest, down, up, pre, qw, ow, xin, win, ng, mg,
     cot_o, wq_o, wo_o, normt_o, proj_o, prob_o, combt_o, n2_o, r2_o,
     G, down_v, slope, acc, pg, pre2,
-    S, R, own, T, T0, ZR, QS, QR, Q0, M, OUT, A,
+    S, R, own, T, T0, ZA, ZR, QS, QA, QR, Q0, M, OUT, A,
     cot, wq, wo, wo2, norm, normt, proj, prob, combt, n2, r2, bias,
     loc, dsem, os_, or_, outs, zs, zr, ns, nr, ys, yr, ps, pr, ws, wr, xs, xr, cs, cr, rys, ryr, rzs, rzr, qs, qr, as_, ar,
 ):
@@ -103,8 +106,6 @@
 
     cp_tok = pltpu.make_async_copy(tok, G.at[0, pl.ds(0, 64)], loc.at[0])
     cp_tok.start()
-    for k in range(4):
-        pltpu.make_async_copy(down.at[:, pl.ds(1024 * k, 1024)], down_v.at[k], dsem.at[k]).start()
     greet(zp + [p1, p2] + dps)
     met(zp + [p1, p2] + dps)
     cp_tok.wait()
@@ -114,9 +115,19 @@
     def col(k):
         return pl.ds(pl.multiple_of(k * W, W), W)
 
-    def down_copy(k):
-        return pltpu.make_async_copy(down.at[:, col(k)], down_v.at[k % 4], dsem.at[k % 4])
-
+    def chunk(p):
+        turn = N_NARROW - LAG + 2
+        return jnp.where(
+            p < turn, p, jnp.where((p - turn) % 2 == 0, N_NARROW + (p - turn) // 2, turn + (p - turn) // 2)
+        )
+
+    def down_copy(p):
+        return pltpu.make_async_copy(
+            down.at[:, col(chunk(p))], down_v.at[p % 4, :, pl.ds(0, W)], dsem.at[p % 4]
+        )
+
+    for k in range(4):
+        down_copy(jnp.int32(k)).start()
     V = M.shape[2]
 
     def up_copy(f):
@@ -171,7 +182,7 @@
         )
 
     o_copy(0).start()
-    for k in range(2):
+    for k in range(AHEAD):
         for i in range(2):
             z_copy(k, i, 64).start()
 
@@ -201,9 +212,6 @@
             cp.start()
     for cp in w_copies((qw, ow), d, cs.at[0], cr.at[0], core):
         cp.start()
-    for zz in range(4):
-        pre_copy(zz).start()
-
     def emit(n, source, target):
         return pltpu.make_async_copy(source, target, outs.at[n])
 
@@ -276,23 +284,25 @@
 
     acc[...] = jnp.zeros_like(acc)
 
-    def multiply(k):
+    def multiply(p):
+        k = chunk(p)
+
         @pl.when(k < N_NARROW)
         def _():
             for i in range(2):
                 y_copy(k, i).wait_recv()
 
         tile = G[:, :, col(k)].reshape(512, W)
-        down_copy(k).wait()
-        acc[...] += lax.dot_general(tile, down_v[k % 4], NT, preferred_element_type=F32)
-
-        @pl.when(k + 4 < N_TOK)
-        def _():
-            down_copy(k + 4).start()
-
-        @pl.when(k >= 4)
-        def _():
-            up_copy(k - 4).start()
+        down_copy(p).wait()
+        acc[...] += lax.dot_general(tile, down_v[p % 4, :, 0:W], NT, preferred_element_type=F32)
+
+        @pl.when(p + 4 < N_TOK)
+        def _():
+            down_copy(p + 4).start()
+
+        @pl.when(p >= N_TOK - 4)
+        def _():
+            up_copy(p - (N_TOK - 4)).start()
 
 
     def x_arrive(h):
@@ -330,28 +340,29 @@
         each(k, act)
 
     def gather_step(k, carry):
-        @pl.when(k == 3)
+        @pl.when(k == N_NARROW - AHEAD)
         def _():
             o_copy(0).wait_recv()
             o_copy(1).wait_recv()
 
-        @pl.when(k + 2 < N_TOK)
-        def _():
-            z_send(k + 2)
+        @pl.when(k + AHEAD < N_TOK)
+        def _():
+            z_send(k + AHEAD)
 
         @pl.when(k < N_TOK)
         def _():
             z_forward(k)
 
-        @pl.when(k >= 3)
-        def _():
-            multiply(jnp.where(k == N_TOK, N_TOK - 2, k - 3))
-
-        @pl.when(k >= 1)
-        def _():
-            y_forward(k - 1)
-
         @pl.when(k == 2)
+        def _():
+            for zz in range(4):
+                pre_copy(zz).start()
+
+        @pl.when((k >= 2) & (k < N_TOK + 2))
+        def _():
+            y_forward(k - 2)
+
+        @pl.when(k == 4)
         def _():
             for cp in w_copies((qw, ow), d2, ws.at[0], wr.at[0], p2):
                 cp.wait_recv()
@@ -361,25 +372,31 @@
             for cp in w_copies(None, d2, cs.at[1], cr.at[1], core):
                 cp.start()
 
-        @pl.when(k >= N_TOK - 1)
-        def _():
-            multiply(jnp.where(k == N_TOK, N_TOK - 1, N_TOK - 3))
+        both = N_NARROW + 2
+
+        @pl.when((k >= LAG) & (k <= N_TOK))
+        def _():
+            multiply(jnp.where(k < both, k - LAG, 2 * (k - both) + both - LAG))
+
+        @pl.when(k >= both)
+        def _():
+            multiply(jnp.where(k > N_TOK, N_TOK - 1, 2 * (k - both) + both - LAG + 1))
 
         @pl.when(k < 4)
         def _():
             norm_step(k)
 
-        @pl.when((k >= 4) & (k < 8))
-        def _():
-            slope_step(k - 4)
-
-        @pl.when(k == 6)
+        @pl.when((k >= 10) & (k < 14))
+        def _():
+            slope_step(k - 10)
+
+        @pl.when(k == 14)
         def _():
             x_arrive(0)
 
         return carry
 
-    lax.fori_loop(0, N_TOK + 1, gather_step, 0)
+    lax.fori_loop(0, N_TOK + 2, gather_step, 0)
     bias_step()
 
     pg[...] = (acc[...] * slope[...].reshape(512, slope.shape[2])).astype(BF16)
@@ -401,8 +418,8 @@
     def ry_copy(f, i):
         return remote(S.at[f, i], R.at[f, i], rys.at[f, i], ryr.at[f, i], (p1, p2)[i])
 
-    def rz_copy(f, i):
-        return remote(T.at[f, i], ZR.at[f, i], rzs.at[f, i], rzr.at[f, i], zp[i])
+    def rz_copy(f, n):
+        return z_parts(T, ZA, ZR, f, n, 64, rzs, rzr)
 
     def a_copy(j, s):
         dd = (d + s) % 16
@@ -438,21 +455,43 @@
 
         return part.reshape(4, 128, V)
 
-    def q_copy(f, i):
-        return remote(QS.at[f, i], QR.at[f, i], qs.at[f, i], qr.at[f, i], zp[i])
+    def z_parts(T, ZA, ZR, f, n, rows, sends, recvs):
+        low, high = pl.ds(0, rows // 2), pl.ds(rows // 2, rows // 2)
+        source, target = (
+            (T.at[f, 1, low], ZA.at[f, 0]),
+            (T.at[f, 0, high], ZR.at[f, 0, high]),
+            (T.at[f, 1, high], ZA.at[f, 1]),
+            (T.at[f, 2, low], ZR.at[f, 1, low]),
+            (T.at[f, 0, low], ZR.at[f, 0, low]),
+            (T.at[f, 2, high], ZR.at[f, 1, high]),
+        )[n]
+        up = n in (0, 1, 4)
+        return remote(source, target, sends.at[f, n], recvs.at[f, n], zp[0] if up else zp[2])
+
+    def z_pass(copy, T, ZA, f, rows):
+        half = rows // 2
+        copy(f, 0).wait_recv()
+        copy(f, 2).wait_recv()
+        T[f, 0, 0:half] = (T[f, 0, 0:half].astype(F32) + ZA[f, 0].astype(F32)).astype(BF16)
+        T[f, 2, half:rows] = (T[f, 2, half:rows].astype(F32) + ZA[f, 1].astype(F32)).astype(BF16)
+        copy(f, 4).start()
+        copy(f, 5).start()
+
+    def q_copy(f, n):
+        return z_parts(QS, QA, QR, f, n, 128, qs, qr)
 
     def z_product(f, carry):
         part = product(f)
         QS[f] = part[1:4].astype(BF16)
-        for i in (0, 2, 1):
-            q_copy(f, i).start()
+        for n in range(4):
+            q_copy(f, n).start()
         Q0[f] = part[0]
         return carry
 
     def z_sum(f):
-        for i in range(3):
-            q_copy(f, i).wait_recv()
-        total = Q0[f] + QR[f, 0].astype(F32) + QR[f, 1].astype(F32) + QR[f, 2].astype(F32)
+        for n in (1, 3, 4, 5):
+            q_copy(f, n).wait_recv()
+        total = Q0[f] + QR[f, 0].astype(F32) + QR[f, 1].astype(F32)
         S[f, 0, 0] = total[64:96].astype(BF16)
         S[f, 1, 0] = total[96:128].astype(BF16)
         Q0[f, 0:64] = total[0:64]
@@ -484,15 +523,13 @@
         total = own[f % 4] + jnp.concatenate([R[f, 0].astype(F32), R[f, 1].astype(F32)], axis=1)
         T[f] = total[1:4].astype(BF16)
         T0[f % 4] = total[0]
-        for h in (0, 2, 1):
-            rz_copy(f, h).start()
+        for n in range(4):
+            rz_copy(f, n).start()
 
     def over_z(f):
-        for h in range(3):
-            rz_copy(f, h).wait_recv()
-        M[f] = (
-            T0[f % 4] + ZR[f, 0].astype(F32) + ZR[f, 1].astype(F32) + ZR[f, 2].astype(F32)
-        ).astype(BF16)
+        for n in (1, 3, 4, 5):
+            rz_copy(f, n).wait_recv()
+        M[f] = (T0[f % 4] + ZR[f, 0].astype(F32) + ZR[f, 1].astype(F32)).astype(BF16)
 
     def send_rows(j):
         both = jnp.concatenate([M[2 * j], M[2 * j + 1]], axis=0)
@@ -517,9 +554,21 @@
         def _():
             y_product(f + 3, 0)
 
+        @pl.when(f < 4)
+        def _():
+            z_pass(q_copy, QS, QA, f - 2, 128)
+
         @pl.when(f == 2)
         def _():
             weights_arrive()
+
+        @pl.when((f == 3) | (f == 4))
+        def _():
+            z_sum(f - 3)
+
+        @pl.when(f >= 3)
+        def _():
+            z_pass(rz_copy, T, ZA, f - 1, 64)
 
         @pl.when(f == 3)
         def _():
@@ -528,8 +577,13 @@
 
         @pl.when((f == 4) | (f == 5))
         def _():
+            z_end(f - 4)
             head_step(f - 4)
 
+        @pl.when(f == 5)
+        def _():
+            send_rows(jnp.int32(0))
+
         @pl.when(f >= 6)
         def _():
             lax.fori_loop(2 * f - 10, 2 * f - 8, late_head, 0)
@@ -538,16 +592,6 @@
         def _():
             over_z(f - 2)
 
-        @pl.when((f == 3) | (f == 4))
-        def _():
-            z_sum(f - 3)
-
-        @pl.when(f == 5)
-        def _():
-            z_end(0)
-            z_end(1)
-            send_rows(jnp.int32(0))
-
         @pl.when((f == 5) | (f == 7))
         def _():
             send_rows((f - 3) // 2)
@@ -555,11 +599,11 @@
         return carry
 
     lax.fori_loop(2, N_FEAT, sum_step, 0)
+    z_pass(rz_copy, T, ZA, N_FEAT - 1, 64)
     over_z(N_FEAT - 2)
     head_step(6)
     over_z(N_FEAT - 1)
     send_rows(3)
-
     head_step(7)
     emit(5, prob, prob_o).start()
     normt[...] = norm[...].astype(F32).T.astype(BF16)
@@ -611,14 +655,14 @@
     def drain2(f, carry):
         for i in range(2):
             ry_copy(f, i).wait_send()
-        for i in range(3):
-            rz_copy(f, i).wait_send()
+        for n in range(6):
+            rz_copy(f, n).wait_send()
         return carry
 
     lax.fori_loop(2, N_FEAT, drain2, 0)
     for f in range(2):
-        for i in range(3):
-            q_copy(f, i).wait_send()
+        for n in range(6):
+            q_copy(f, n).wait_send()
         for i in range(2):
             qy_copy(f, i).wait_send()
     for j in range(4):
@@ -657,7 +701,7 @@
         out_specs=(hbm,) * len(kept),
         scratch_shapes=[
             pltpu.VMEM((4, 128, tok.shape[1]), BF16),
-            pltpu.VMEM((4, 640, 1024), BF16),
+            pltpu.VMEM((4, 640, 640), BF16),
             pltpu.VMEM((4, 128, hid), F32),
             pltpu.VMEM((512, hid), F32),
             pltpu.VMEM((512, hid), BF16),
@@ -667,9 +711,11 @@
             pltpu.VMEM((4, 4, 64, V), F32),
             pltpu.VMEM((N_FEAT, 3, 64, V), BF16),
             pltpu.VMEM((4, 64, V), F32),
-            pltpu.VMEM((N_FEAT, 3, 64, V), BF16),
+            pltpu.VMEM((N_FEAT, 2, 32, V), BF16),
+            pltpu.VMEM((N_FEAT, 2, 64, V), BF16),
             pltpu.VMEM((2, 3, 128, V), BF16),
-            pltpu.VMEM((2, 3, 128, V), BF16),
+            pltpu.VMEM((2, 2, 64, V), BF16),
+            pltpu.VMEM((2, 2, 128, V), BF16),
             pltpu.VMEM((2, 128, V), F32),
             pltpu.VMEM((N_FEAT, 64, V), BF16),
             pltpu.VMEM((4, 256, V), BF16),
@@ -696,8 +742,8 @@
             dma((2, 3, 2)), dma((2, 3, 2)),
             dma((8, 2)), dma((8, 2)),
             dma((N_FEAT, 2)), dma((N_FEAT, 2)),
-            dma((N_FEAT, 3)), dma((N_FEAT, 3)),
-            dma((2, 3)), dma((2, 3)),
+            dma((N_FEAT, 6)), dma((N_FEAT, 6)),
+            dma((2, 6)), dma((2, 6)),
             dma((4,)), dma((4,)),
         ],
         compiler_params=pltpu.CompilerParams(
@@ -712,12 +758,14 @@
     lg, pout, oout,
     cot, wq, wo, normt, proj, prob, combt, n2, r2,
     db, dc, wof, DP, dpb,
-    gl, ga, Cl, Ca, Z, ZR, E2, XR2, El, YRl, Fl, FRl,
-    Sa, XRa, E1, ZR2, Ea, YRa, Fa, FRa,
+    ga, Ca, Sa, XRa, E1, ZR2, Ea, YRa, Fa, FRa,
+    gl, Cl, Zl, ZRl, El2, XRl, El, YRl, Fl, FRl,
+    gc, Cc, Zc, ZRc, Ec2, XRc, Ec, YRc, Fc, FRc,
     gm, Cm, Sm, YRm, Em, XRm, Zm, Fm,
     gb, Cb, Sb, YRb, Eb, XRb, Zb, Fb,
-    ins, cls, clr, cas, car, zs, zr, x2s, x2r, yls, ylr, fls, flr,
-    xas, xar, z2s, z2r, yas, yar, fas, far,
+    ins, cas, car, xas, xar, z2s, z2r, yas, yar, fas, far,
+    cls, clr, zls, zlr, xls, xlr, yls, ylr, fls, flr,
+    ccs, ccr, zcs, zcr, xcs, xcr, ycs, ycr, fcs, fcr,
     cms, cmr, yms, ymr, xms, xmr, zms, zmr, pms, pmr,
     cbs, cbr, ybs, ybr, xbs, xbr, zbs, zbr, pbs, pbr,
 ):
@@ -738,29 +786,8 @@
     for cp in loads[:3]:
         cp.start()
 
-    def cl_copy(p):
-        return remote(gl.at[p, :, 1 - c], Cl.at[p], cls.at[p], clr.at[p], core)
-
     def ca_copy(p):
         return remote(ga.at[p, :, 1 - c], Ca.at[p], cas.at[p], car.at[p], core)
-
-    def z_copy(i):
-        t = (z + i + 1) % 4
-        return remote(Z.at[t % 2, t // 2], ZR.at[i], zs.at[i], zr.at[i], zp[i])
-
-    def summed_l(p):
-        cl_copy(p).wait_recv()
-        total = (gl[p, :, c].astype(F32) + Cl[p].astype(F32)).astype(BF16).reshape(4, 2, 80, N_LEFT)
-        Z[p, 0] = total[:, 0]
-        Z[p, 1] = total[:, 1]
-        for i in (0, 2, 1):
-
-            @pl.when((z + i + 1) % 2 == p)
-            def _():
-                z_copy(i).start()
-
-    def x2_copy(i):
-        return remote(E2.at[(x + i + 1) % 4], XR2.at[i], x2s.at[i], x2r.at[i], xp[i])
 
     def xa_copy(p, i):
         return remote(
@@ -905,9 +932,70 @@
             for there in range(2):
                 pltpu.make_async_copy(fr.at[there], fr.at[there], fr_sem.at[there]).wait()
 
-    last_l = (El, YRl, yls, ylr)
+    def z_first(g, C, Z, ZR, E2, XR, E, YR, F, FR, cs, cr, zs, zr, xs, xr, ys, yr, fs, fr):
+        def c_copy(p):
+            return remote(g.at[p, :, 1 - c], C.at[p], cs.at[p], cr.at[p], core)
+
+        def z_copy(i):
+            t = (z + i + 1) % 4
+            return remote(Z.at[t % 2, t // 2], ZR.at[i], zs.at[i], zr.at[i], zp[i])
+
+        def x_copy(i):
+            return remote(E2.at[(x + i + 1) % 4], XR.at[i], xs.at[i], xr.at[i], xp[i])
+
+        def add_cores(p):
+            c_copy(p).wait_recv()
+            total = (g[p, :, c].astype(F32) + C[p].astype(F32)).astype(BF16)
+            total = total.reshape((4, 2) + total.shape[1:])
+            Z[p, 0] = total[:, 0]
+            Z[p, 1] = total[:, 1]
+            for i in (0, 2, 1):
+
+                @pl.when((z + i + 1) % 2 == p)
+                def _():
+                    z_copy(i).start()
+
+        def add_z():
+            for i in range(3):
+                z_copy(i).wait_recv()
+            mine = Z[z % 2, z // 2].astype(F32)
+            for i in range(3):
+                mine = mine + ZR[i].astype(F32)
+            E2[...] = mine.astype(BF16)
+            for i in (0, 2, 1):
+                x_copy(i).start()
+
+        def add_x():
+            for i in range(3):
+                x_copy(i).wait_recv()
+            mine = E2[x].astype(F32)
+            for i in range(3):
+                mine = mine + XR[i].astype(F32)
+            E[...] = mine.astype(BF16)
+            owners_send(E, YR, ys, yr)
+
+        def add_y():
+            owners_sum(E, YR, ys, yr, F, FR, fs, fr)
+
+        def finish():
+            owners_end(E, YR, ys, yr, F, FR, fs, fr)
+
+        def drain():
+            for p in range(2):
+                c_copy(p).wait_send()
+            for i in range(3):
+                z_copy(i).wait_send()
+                x_copy(i).wait_send()
+
+        return c_copy, add_cores, add_z, add_x, add_y, finish, drain
+
+    l_core, l_cores, l_z, l_x, l_y, l_finish, l_drain = z_first(
+        gl, Cl, Zl, ZRl, El2, XRl, El, YRl, Fl, FRl, cls, clr, zls, zlr, xls, xlr, yls, ylr, fls, flr
+    )
+    c_core, c_cores, c_z, c_x, c_y, c_finish, c_drain = z_first(
+        gc, Cc, Zc, ZRc, Ec2, XRc, Ec, YRc, Fc, FRc, ccs, ccr, zcs, zcr, xcs, xcr, ycs, ycr, fcs, fcr
+    )
     last_a = (Ea, YRa, yas, yar)
-    more_l = (Fl, FRl, fls, flr)
     more_a = (Fa, FRa, fas, far)
 
     loads[0].wait()
@@ -944,7 +1032,7 @@
     gl[1] = grad_o[..., :N_LEFT]
     gm[1] = grad_o[..., N_LEFT:]
     met(zp + xp + [core, p1, p2, yhp])
-    cl_copy(1).start()
+    l_core(1).start()
     m_core(1).start()
 
     DP[...] = jnp.zeros_like(DP)
@@ -970,10 +1058,10 @@
         return grad.astype(BF16).reshape(8, 2, 80, width)
 
     gl[0] = part_grad(2, 0, N_LEFT)
-    cl_copy(0).start()
+    l_core(0).start()
     gm[0] = part_grad(2, N_LEFT, 640 - N_LEFT)
     m_core(0).start()
-    summed_l(1)
+    l_cores(1)
     m_cores(1)
     loads[6].wait()
 
@@ -1003,28 +1091,36 @@
 
         @pl.when(h == 0)
         def _():
-            summed_l(0)
+            l_cores(0)
             m_cores(0)
             m_start()
 
-        @pl.when(h == 4)
+        @pl.when(h == 3)
         def _():
             for p in range(2):
-                ga[p] = part_grad(p, 0, N_LEFT)
+                ga[p] = part_grad(p, 0, N_X)
                 ca_copy(p).start()
 
-        @pl.when(h == 6)
+        @pl.when(h == 5)
         def _():
             summed_a(0)
             summed_a(1)
-            m_y()
+
+        @pl.when(h == 6)
+        def _():
+            for p in range(2):
+                gc[p] = part_grad(p, N_X, N_Z)
+                c_core(p).start()
 
         return carry
 
     lax.fori_loop(0, 8, head_step, 0)
     for p in range(2):
-        gb[p] = part_grad(p, N_LEFT, 640 - N_LEFT)
+        gb[p] = part_grad(p, N_X + N_Z, 640 - N_X - N_Z)
         b_core(p).start()
+    m_y()
+    c_cores(0)
+    c_cores(1)
 
     def input_dot(half):
         total = jnp.zeros((512, 640), F32)
@@ -1042,16 +1138,21 @@
     b_cores(0)
     b_cores(1)
     b_start()
-
-    for i in range(3):
-        z_copy(i).wait_recv()
-    mine = Z[z % 2, z // 2].astype(F32)
-    for i in range(3):
-        mine = mine + ZR[i].astype(F32)
-    E2[...] = mine.astype(BF16)
+    l_z()
+
+    for p in range(2):
+        for i in range(3):
+            xa_copy(p, i).wait_recv()
+        mine = Sa[p, pl.ds(2 * x, 2)].astype(F32)
+        for i in range(3):
+            mine = mine + XRa[i, p].astype(F32)
+        E1[0, p] = mine[0].astype(BF16)
+        E1[1, p] = mine[1].astype(BF16)
     for i in (0, 2, 1):
-        x2_copy(i).start()
+        z2_copy(i).start()
     input_dot(1)
+    m_x()
+    l_x()
 
     def input_step(t, carry):
         rows = pl.ds(pl.multiple_of(t * 128, 128), 128)
@@ -1066,25 +1167,8 @@
 
     lax.fori_loop(0, 4, input_step, 0)
 
-    for p in range(2):
-        for i in range(3):
-            xa_copy(p, i).wait_recv()
-        mine = Sa[p, pl.ds(2 * x, 2)].astype(F32)
-        for i in range(3):
-            mine = mine + XRa[i, p].astype(F32)
-        E1[0, p] = mine[0].astype(BF16)
-        E1[1, p] = mine[1].astype(BF16)
-    for i in (0, 2, 1):
-        z2_copy(i).start()
-    m_x()
+    c_z()
     b_y()
-    for i in range(3):
-        x2_copy(i).wait_recv()
-    mine = E2[x].astype(F32)
-    for i in range(3):
-        mine = mine + XR2[i].astype(F32)
-    El[...] = mine.astype(BF16)
-    owners_send(*last_l)
     for i in range(3):
         z2_copy(i).wait_recv()
     mine = E1[z // 2, z % 2].astype(F32)
@@ -1093,13 +1177,15 @@
     Ea[...] = mine.astype(BF16)
     owners_send(*last_a)
     m_z()
+    l_y()
     b_x()
-    owners_sum(*last_l, *more_l)
+    c_x()
     owners_sum(*last_a, *more_a)
     b_z()
+    c_y()
 
     m_finish()
-    owners_end(*last_l, *more_l)
+    l_finish()
     pout[:, 1280 : 1280 + N_LEFT] = FRl[0].astype(F32)
     pout[:, 1280 + N_LEFT : 1920] = Fm[0].astype(F32)
     left, right = FRl[1].astype(F32), Fm[1].astype(F32)
@@ -1108,21 +1194,21 @@
     oout[:, 640 : 640 + N_LEFT] = left[40:80]
     oout[:, 640 + N_LEFT : 1280] = right[40:80]
     owners_end(*last_a, *more_a)
+    c_finish()
     b_finish()
     for p in range(2):
-        pout[:, 640 * p : 640 * p + N_LEFT] = FRa[p].astype(F32)
-        pout[:, 640 * p + N_LEFT : 640 * p + 640] = Fb[p].astype(F32)
-
-    m_drain()
-    b_drain()
+        first = 640 * p
+        pout[:, first : first + N_X] = FRa[p].astype(F32)
+        pout[:, first + N_X : first + N_X + N_Z] = FRc[p].astype(F32)
+        pout[:, first + N_X + N_Z : first + 640] = Fb[p].astype(F32)
+
+    for drain in (m_drain, b_drain, l_drain, c_drain):
+        drain()
     for p in range(2):
-        cl_copy(p).wait_send()
         ca_copy(p).wait_send()
+        for i in range(3):
+            xa_copy(p, i).wait_send()
     for i in range(3):
-        for p in range(2):
-            xa_copy(p, i).wait_send()
-        z_copy(i).wait_send()
-        x2_copy(i).wait_send()
         z2_copy(i).wait_send()
 
 
@@ -1130,7 +1216,8 @@
     vm = pl.BlockSpec(memory_space=pltpu.VMEM)
     hbm = pl.BlockSpec(memory_space=pl.ANY)
     dma = pltpu.SemaphoreType.DMA
-    ta, tb = (80, N_LEFT), (80, 640 - N_LEFT)
+    tl, tm = (80, N_LEFT), (80, 640 - N_LEFT)
+    ta, tc, tb = (80, N_X), (80, N_Z), (80, 640 - N_X - N_Z)
     held = (cot, wq, wo, normt, proj, prob, combt, n2, r2)
     return pl.pallas_call(
         block_kernel,
@@ -1150,17 +1237,7 @@
             pltpu.VMEM((3, 512, 640), F32),
             pltpu.VMEM((3, 512, 640), BF16),
             pltpu.VMEM((2, 8, 2) + ta, BF16),
-            pltpu.VMEM((2, 8, 2) + ta, BF16),
             pltpu.VMEM((2, 8) + ta, BF16),
-            pltpu.VMEM((2, 8) + ta, BF16),
-            pltpu.VMEM((2, 2, 4) + ta, BF16),
-            pltpu.VMEM((3, 4) + ta, BF16),
-            pltpu.VMEM((4,) + ta, BF16),
-            pltpu.VMEM((3,) + ta, BF16),
-            pltpu.VMEM(ta, BF16),
-            pltpu.VMEM((3,) + ta, BF16),
-            pltpu.VMEM(ta, BF16),
-            pltpu.VMEM((2,) + ta, BF16),
             pltpu.VMEM((2, 8) + ta, BF16),
             pltpu.VMEM((3, 2, 2) + ta, BF16),
             pltpu.VMEM((2, 2) + ta, BF16),
@@ -1171,32 +1248,44 @@
             pltpu.VMEM((2,) + ta, BF16),
         ]
         + [
-            pltpu.VMEM((2, 8, 2) + tb, BF16),
-            pltpu.VMEM((2, 8) + tb, BF16),
-            pltpu.VMEM((2, 2, 4) + tb, BF16),
-            pltpu.VMEM((3, 4) + tb, BF16),
-            pltpu.VMEM((4,) + tb, BF16),
-            pltpu.VMEM((3,) + tb, BF16),
-            pltpu.VMEM((4,) + tb, BF16),
-            pltpu.VMEM((2,) + tb, BF16),
-        ]
-        * 2
-        + [
-            dma((9,)),
-            dma((2,)), dma((2,)), dma((2,)), dma((2,)),
-            dma((3,)), dma((3,)), dma((3,)), dma((3,)), dma((3,)), dma((3,)), dma((3,)), dma((2,)),
-            dma((2, 3)), dma((2, 3)), dma((3,)), dma((3,)), dma((3,)), dma((3,)), dma((3,)), dma((2,)),
+            pltpu.VMEM(lead + t, BF16)
+            for t in (tl, tc)
+            for lead in ((2, 8, 2), (2, 8), (2, 2, 4), (3, 4), (4,), (3,), (), (3,), (), (2,))
         ]
         + [
-            dma((2,)), dma((2,)), dma((3,)), dma((3,)), dma((3,)), dma((3,)), dma((3,)), dma((3,)),
-            dma((1,)), dma((1,)),
+            pltpu.VMEM(lead + t, BF16)
+            for t in (tm, tb)
+            for lead in ((2, 8, 2), (2, 8), (2, 2, 4), (3, 4), (4,), (3,), (4,), (2,))
         ]
-        * 2,
+        + [dma((9,))]
+        + [
+            dma(n)
+            for n in ((2,), (2,), (2, 3), (2, 3), (3,), (3,), (3,), (3,), (3,), (2,))
+        ]
+        + [dma((n,)) for n in (2, 2, 3, 3, 3, 3, 3, 3, 3, 2) * 2]
+        + [dma((n,)) for n in (2, 2, 3, 3, 3, 3, 3, 3, 1, 1) * 2],
         compiler_params=pltpu.CompilerParams(
             collective_id=2, has_side_effects=True, vmem_limit_bytes=62 << 20
         ),
         cost_estimate=pl.CostEstimate(flops=8 * 10**9, bytes_accessed=40 * 10**6, transcendentals=0),
     )(cot, wq, wo, normt, proj, prob, combt, n2, r2, xin, ng, mg)
+
+
+def finish_kernel(a, b, c, out_a, out_b, out_c):
+    out_a[...] = a[...]
+    out_b[...] = b[...]
+    out_c[...] = c[...]
+
+
+def finish(*arrays):
+    vm = pl.BlockSpec(memory_space=pltpu.VMEM)
+    return pl.pallas_call(
+        finish_kernel,
+        name="finish",
+        out_shape=tuple(jax.ShapeDtypeStruct(k.shape, k.dtype) for k in arrays),
+        in_specs=[vm] * 3,
+        out_specs=(vm,) * 3,
+    )(*arrays)
 
 
 def local(
@@ -1216,7 +1305,7 @@
         token_grads, token_dest.reshape(1, 64), merger_down, merger_up, merger_pre, qkv_weight, proj_weight,
         layer_input, window_ids, norm_gain, merge_gain,
     )
-    return block_grads(*kept, layer_input, norm_gain, merge_gain)
+    return finish(*block_grads(*kept, layer_input, norm_gain, merge_gain))
 
 
 def solution(mesh):

time: 169 us -> 167 us (0.988)
  local copies, waits for them, and re-layouts: 4.04 us -> 0 us
  Pallas kernels: 164 us -> 166 us
    unnamed x7 -> x0, local copies, waits for them, and re-layouts: 4.04 us -> none
    pallas_call x0 -> x1, Pallas kernels: none -> 2.87 us  [finish(): pl.pallas_call(finish_kernel, name='finish', out_shape=tuple((jax.ShapeDt...]
where the time goes in v5:
time: 167 us
  Pallas kernels  166 us (99%)
    pallas_call x1, Pallas kernels, merger(): pl.pallas_call(merger_kernel, name='merger', out_shape=tuple((jax.ShapeDt...  110 us
    pallas_call x1, Pallas kernels, block_grads(): pl.pallas_call(block_kernel, name='block', out_shape=(jax.ShapeDtypeStruc...  53.4 us

profile of v5, /device:TPU:0, one launch (start us, length us, event | category | flops | bytes accessed | tf_op | source)
XLA Modules:
  0.0 166.6 jit_solution(10582729122621993815)
XLA Ops:
  0.6 109.7 %merger.1 = (bf16[512,1280]{1,0:T(8,128)(2,1)}, bf16[16,80,1920]{2,1,0:T(8,128)(2,1)}, bf16[640,1280]{1,0:T(8,128)(2,1)}, bf16[1280,512]{1,0:T(8,128)(2,1)}, bf1...) custom-call(bf16[64,8192]{1,0:T(8,128)(2,1)} %tok.1, ...), custom_call_target="tpu_custom_call" | custom-call | flops 8999999488 | bytes 40000000 | tf_op jit(solution)/shard_map/merger/pallas_call | solution.py:696
  110.3 53.4 %block.1 = (bf16[512,1280]{1,0:T(8,128)(2,1)}, f32[80,1920]{1,0:T(8,128)}, f32[40,1280]{1,0:T(8,128)}) custom-call(bf16[512,1280]{1,0:T(8,128)(2,1)} %get-tuple-element.15.cot_i, bf16[16,80,1920]{2,1,0:T(8,128)(2,1)} %get-tuple-element.16.wq_i, bf16[640,1280]{1,0:T(8,128)(2,1)} %get-tuple-element.17.wo_i, bf16[1280,512]{1,0:T(8,128)(2,1)} %get-tuple-element.18.normt_i, ...), custom_call_target="tpu_custom_call" | custom-call | flops 8000000000 | bytes 40000000 | tf_op jit(solution)/shard_map/block/pallas_call | solution.py:1222
  163.8 2.9 %finish.1 = (bf16[512,1280]{1,0:T(8,128)(2,1)}, f32[80,1920]{1,0:T(8,128)}, f32[40,1280]{1,0:T(8,128)}) custom-call(bf16[512,1280]{1,0:T(8,128)(2,1)} %get-tuple-element.24.a, f32[80,1920]{1,0:T(8,128)} %get-tuple-element.25.b, f32[40,1280]{1,0:T(8,128)} %get-tuple-element.26.c), custom_call_target="tpu_custom_call" | custom-call | tf_op jit(solution)/shard_map/finish/pallas_call | solution.py:1282

commit v6 on v5

--- a/solution.py
+++ b/solution.py
@@ -75,6 +75,10 @@
     )
 
 
+def settle(ref, sem):
+    pltpu.make_async_copy(ref, ref, sem).wait()
+
+
 def greet(devices):
     barrier = pltpu.get_barrier_semaphore()
     for device in devices:
@@ -91,7 +95,7 @@
     G, down_v, slope, acc, pg, pre2,
     S, R, own, T, T0, ZA, ZR, QS, QA, QR, Q0, M, OUT, A,
     cot, wq, wo, wo2, norm, normt, proj, prob, combt, n2, r2, bias,
-    loc, dsem, os_, or_, outs, zs, zr, ns, nr, ys, yr, ps, pr, ws, wr, xs, xr, cs, cr, rys, ryr, rzs, rzr, qs, qr, as_, ar,
+    loc, dsem, os_, or_, outs, zs, zr, ns, nr, ys, yr, ps, pr, ws, wr, xs, xr, cs, cr, rys, qys, ryr, rzs, rzr, qs, qr, as_, ar,
 ):
     x, yh, c, z, yl = place()
     d = (x * 2 + yh) * 2 + c
@@ -138,8 +142,8 @@
         return remote(
             G.at[0, pl.ds(0, rows), col(k)],
             G.at[(3, 1)[i], pl.ds(0, rows), col(k)],
-            zs.at[k, i],
-            zr.at[k, i],
+            zs.at[rows // 128, i],
+            zr.at[k],
             (zp[0], zp[2])[i],
         )
 
@@ -148,8 +152,8 @@
         return remote(
             G.at[(3, 1)[i], pl.ds(0, rows), half],
             G.at[2, pl.ds(0, rows), half],
-            ns.at[k, i],
-            nr.at[k, i],
+            ns.at[rows // 128, i],
+            nr.at[k],
             (zp[0], zp[2])[i],
         )
 
@@ -166,8 +170,8 @@
         return remote(
             G.at[:, pl.ds(32 * i, 32), col(k)],
             G.at[:, pl.ds(64 + 32 * i, 32), col(k)],
-            ys.at[k, i],
-            yr.at[k, i],
+            ys.at[i],
+            yr.at[k],
             (p1, p2)[i],
         )
 
@@ -188,7 +192,7 @@
 
     def pre_copy(zz):
         rows = pl.ds(pl.multiple_of((2 * zz + 1 - yl) * 64 + 32, 32), 32)
-        return remote(pre.at[rows], pre2.at[pl.ds(32 * zz, 32)], ps.at[zz], pr.at[zz], yhp)
+        return remote(pre.at[rows], pre2.at[pl.ds(32 * zz, 32)], ps.at[0], pr.at[0], yhp)
 
     def w_copies(source, index, sends, recvs, device):
         first = wq.at[index] if source is None else source[0]
@@ -208,9 +212,9 @@
         cp.start()
     o_copy(1).start()
     for i in (0, 2, 1):
-        for cp in w_copies((qw, ow), d, xs.at[0, i], xr.at[0, i], xp[i]):
+        for cp in w_copies((qw, ow), d, xs, xr.at[0], xp[i]):
             cp.start()
-    for cp in w_copies((qw, ow), d, cs.at[0], cr.at[0], core):
+    for cp in w_copies((qw, ow), d, cs, cr, core):
         cp.start()
     def emit(n, source, target):
         return pltpu.make_async_copy(source, target, outs.at[n])
@@ -218,8 +222,7 @@
     def slope_step(r):
         @pl.when(r == 0)
         def _():
-            for zz in range(4):
-                pre_copy(zz).wait_recv()
+            settle(pre2, pr.at[0])
 
         zz = (z + r) % 4
         mine = pre[pl.ds(pl.multiple_of((2 * zz + yl) * 64, 64), 64), :]
@@ -289,8 +292,7 @@
 
         @pl.when(k < N_NARROW)
         def _():
-            for i in range(2):
-                y_copy(k, i).wait_recv()
+            settle(G.at[:, pl.ds(64, 64), col(k)], yr.at[k])
 
         tile = G[:, :, col(k)].reshape(512, W)
         down_copy(p).wait()
@@ -306,12 +308,12 @@
 
 
     def x_arrive(h):
+        settle(wq.at[pl.ds(0, 3)], xr.at[h, 0])
+        settle(wo.at[pl.ds(0, 3)], xr.at[h, 1])
         for i in range(3):
             other = ((x + i + 1) % 4 * 2 + yh) * 2 + c
             other = flipped(other) if h else other
-            for cp in w_copies(None, other, xs.at[h, 2 - i], xr.at[h, 2 - i], xp[2 - i]):
-                cp.wait_recv()
-            for cp in w_copies(None, other, cs.at[2 + 3 * h + i], cr.at[2 + 3 * h + i], core):
+            for cp in w_copies(None, other, cs, cr, core):
                 cp.start()
 
     def z_send(k):
@@ -323,16 +325,15 @@
 
     def z_forward(k):
         def act(rows):
+            settle(G.at[pl.ds(0, 2), pl.ds(0, rows), col(k)], zr.at[k])
             for i in range(2):
-                z_copy(k, i, rows).wait_recv()
                 on_copy(k, i, rows).start()
 
         each(k, act)
 
     def y_forward(k):
         def act(rows):
-            for i in range(2):
-                on_copy(k, i, rows).wait_recv()
+            settle(G.at[2, pl.ds(0, rows), col(k)], nr.at[k])
             if rows == 64:
                 for i in range(2):
                     y_copy(k, i).start()
@@ -367,9 +368,9 @@
             for cp in w_copies((qw, ow), d2, ws.at[0], wr.at[0], p2):
                 cp.wait_recv()
             for i in (0, 2, 1):
-                for cp in w_copies(None, d2, xs.at[1, i], xr.at[1, i], xp[i]):
+                for cp in w_copies(None, d2, xs, xr.at[1], xp[i]):
                     cp.start()
-            for cp in w_copies(None, d2, cs.at[1], cr.at[1], core):
+            for cp in w_copies(None, d2, cs, cr, core):
                 cp.start()
 
         both = N_NARROW + 2
@@ -416,7 +417,7 @@
     ).astype(BF16)
 
     def ry_copy(f, i):
-        return remote(S.at[f, i], R.at[f, i], rys.at[f, i], ryr.at[f, i], (p1, p2)[i])
+        return remote(S.at[f, i], R.at[f, i], rys.at[i], ryr.at[f], (p1, p2)[i])
 
     def rz_copy(f, n):
         return z_parts(T, ZA, ZR, f, n, 64, rzs, rzr)
@@ -431,16 +432,9 @@
             dps[s - 1],
         )
 
-    cidx = [d, d2]
-    for h in range(2):
-        for i in range(3):
-            other = ((x + i + 1) % 4 * 2 + yh) * 2 + c
-            cidx.append(flipped(other) if h else other)
-
     def weights_arrive():
-        for n, index in enumerate(cidx):
-            for cp in w_copies(None, index + 1 - 2 * c, cs.at[n], cr.at[n], core):
-                cp.wait_recv()
+        settle(wq.at[pl.ds(0, 8)], cr.at[0])
+        settle(wo.at[pl.ds(0, 8)], cr.at[1])
         wo2[...] = wo[...].astype(F32).reshape(wo2.shape).astype(BF16)
         emit(1, wq, wq_o).start()
         emit(2, wo2, wo_o).start()
@@ -466,12 +460,13 @@
             (T.at[f, 2, high], ZR.at[f, 1, high]),
         )[n]
         up = n in (0, 1, 4)
-        return remote(source, target, sends.at[f, n], recvs.at[f, n], zp[0] if up else zp[2])
-
-    def z_pass(copy, T, ZA, f, rows):
+        return remote(
+            source, target, sends.at[n], recvs.at[f, 0 if n in (0, 2) else 1], zp[0] if up else zp[2]
+        )
+
+    def z_pass(copy, T, ZA, recvs, f, rows):
         half = rows // 2
-        copy(f, 0).wait_recv()
-        copy(f, 2).wait_recv()
+        settle(ZA.at[f], recvs.at[f, 0])
         T[f, 0, 0:half] = (T[f, 0, 0:half].astype(F32) + ZA[f, 0].astype(F32)).astype(BF16)
         T[f, 2, half:rows] = (T[f, 2, half:rows].astype(F32) + ZA[f, 1].astype(F32)).astype(BF16)
         copy(f, 4).start()
@@ -489,8 +484,7 @@
         return carry
 
     def z_sum(f):
-        for n in (1, 3, 4, 5):
-            q_copy(f, n).wait_recv()
+        settle(QR.at[f], qr.at[f, 1])
         total = Q0[f] + QR[f, 0].astype(F32) + QR[f, 1].astype(F32)
         S[f, 0, 0] = total[64:96].astype(BF16)
         S[f, 1, 0] = total[96:128].astype(BF16)
@@ -499,11 +493,10 @@
             qy_copy(f, i).start()
 
     def qy_copy(f, i):
-        return remote(S.at[f, i, 0], R.at[f, i, 0], rys.at[f, i], ryr.at[f, i], (p1, p2)[i])
+        return remote(S.at[f, i, 0], R.at[f, i, 0], qys.at[i], ryr.at[f], (p1, p2)[i])
 
     def z_end(f):
-        for i in range(2):
-            qy_copy(f, i).wait_recv()
+        settle(R.at[f, :, 0], ryr.at[f])
         M[f] = (
             Q0[f, 0:64] + jnp.concatenate([R[f, 0, 0].astype(F32), R[f, 1, 0].astype(F32)], axis=0)
         ).astype(BF16)
@@ -518,8 +511,7 @@
         return carry
 
     def over_y(f):
-        for h in range(2):
-            ry_copy(f, h).wait_recv()
+        settle(R.at[f], ryr.at[f])
         total = own[f % 4] + jnp.concatenate([R[f, 0].astype(F32), R[f, 1].astype(F32)], axis=1)
         T[f] = total[1:4].astype(BF16)
         T0[f % 4] = total[0]
@@ -527,8 +519,7 @@
             rz_copy(f, n).start()
 
     def over_z(f):
-        for n in (1, 3, 4, 5):
-            rz_copy(f, n).wait_recv()
+        settle(ZR.at[f], rzr.at[f, 1])
         M[f] = (T0[f % 4] + ZR[f, 0].astype(F32) + ZR[f, 1].astype(F32)).astype(BF16)
 
     def send_rows(j):
@@ -556,7 +547,7 @@
 
         @pl.when(f < 4)
         def _():
-            z_pass(q_copy, QS, QA, f - 2, 128)
+            z_pass(q_copy, QS, QA, qr, f - 2, 128)
 
         @pl.when(f == 2)
         def _():
@@ -568,7 +559,7 @@
 
         @pl.when(f >= 3)
         def _():
-            z_pass(rz_copy, T, ZA, f - 1, 64)
+            z_pass(rz_copy, T, ZA, rzr, f - 1, 64)
 
         @pl.when(f == 3)
         def _():
@@ -599,7 +590,7 @@
         return carry
 
     lax.fori_loop(2, N_FEAT, sum_step, 0)
-    z_pass(rz_copy, T, ZA, N_FEAT - 1, 64)
+    z_pass(rz_copy, T, ZA, rzr, N_FEAT - 1, 64)
     over_z(N_FEAT - 2)
     head_step(6)
     over_z(N_FEAT - 1)
@@ -625,46 +616,30 @@
             ).astype(BF16)
     emit(0, cot, cot_o).start()
 
-    for n, index in enumerate(cidx):
-        for cp in w_copies(None, index, cs.at[n], cr.at[n], core):
-            cp.wait_send()
+    settle(wq.at[pl.ds(0, 8)], cs.at[0])
+    settle(wo.at[pl.ds(0, 8)], cs.at[1])
+    settle(wq.at[pl.ds(0, 6)], xs.at[0])
+    settle(wo.at[pl.ds(0, 6)], xs.at[1])
     for cp in w_copies((qw, ow), d, ws.at[0], wr.at[0], p2):
         cp.wait_send()
-    for h in range(2):
-        for i in range(3):
-            for cp in w_copies(None, d2 if h else d, xs.at[h, i], xr.at[h, i], xp[i]):
-                cp.wait_send()
-    for zz in range(4):
-        pre_copy(zz).wait_send()
-
-    def drain(k, carry):
-        def act(rows):
-            for i in range(2):
-                z_copy(k, i, rows).wait_send()
-                on_copy(k, i, rows).wait_send()
-                if rows == 64:
-                    y_copy(k, i).wait_send()
-
-        each(k, act)
-        return carry
-
-    lax.fori_loop(0, N_TOK, drain, 0)
+    settle(pre2, ps.at[0])
+
+    edge = N_NARROW * W
+    for i in range(2):
+        settle(G.at[0, pl.ds(0, 64), pl.ds(0, edge)], zs.at[0, i])
+        settle(G.at[0, pl.ds(0, 128), pl.ds(edge, N_TOK * W - edge)], zs.at[1, i])
+        settle(G.at[0, pl.ds(0, 64), pl.ds(0, edge // 2)], ns.at[0, i])
+        settle(G.at[0, pl.ds(0, 128), pl.ds(0, (N_TOK * W - edge) // 2)], ns.at[1, i])
+        settle(G.at[:, pl.ds(0, 32), pl.ds(0, edge)], ys.at[i])
     o_copy(0).wait_send()
     o_copy(1).wait_send()
 
-    def drain2(f, carry):
-        for i in range(2):
-            ry_copy(f, i).wait_send()
-        for n in range(6):
-            rz_copy(f, n).wait_send()
-        return carry
-
-    lax.fori_loop(2, N_FEAT, drain2, 0)
-    for f in range(2):
-        for n in range(6):
-            q_copy(f, n).wait_send()
-        for i in range(2):
-            qy_copy(f, i).wait_send()
+    for n in range(6):
+        settle(T.at[pl.ds(2, N_FEAT - 2), 0, pl.ds(0, 32)], rzs.at[n])
+        settle(QS.at[:, 0, pl.ds(0, 64)], qs.at[n])
+    for i in range(2):
+        settle(S.at[pl.ds(2, N_FEAT - 2), i], rys.at[i])
+        settle(S.at[pl.ds(0, 2), i, 0], qys.at[i])
     for j in range(4):
         pltpu.make_async_copy(OUT.at[j, fifteen], OUT.at[j, fifteen], as_.at[j]).wait()
     pairs = [
@@ -736,14 +711,14 @@
             dma((4,)),
             dma((2,)), dma((2,)),
             dma((9,)),
-            dma((N_TOK, 2)), dma((N_TOK, 2)), dma((N_TOK, 2)), dma((N_TOK, 2)), dma((N_TOK, 2)), dma((N_TOK, 2)),
-            dma((4,)), dma((4,)),
+            dma((2, 2)), dma((N_TOK,)), dma((2, 2)), dma((N_TOK,)), dma((2,)), dma((N_NARROW,)),
+            dma((1,)), dma((1,)),
             dma((1, 2)), dma((1, 2)),
-            dma((2, 3, 2)), dma((2, 3, 2)),
-            dma((8, 2)), dma((8, 2)),
-            dma((N_FEAT, 2)), dma((N_FEAT, 2)),
-            dma((N_FEAT, 6)), dma((N_FEAT, 6)),
-            dma((2, 6)), dma((2, 6)),
+            dma((2,)), dma((2, 2)),
+            dma((2,)), dma((2,)),
+            dma((2,)), dma((2,)), dma((N_FEAT,)),
+            dma((6,)), dma((N_FEAT, 2)),
+            dma((6,)), dma((2, 2)),
             dma((4,)), dma((4,)),
         ],
         compiler_params=pltpu.CompilerParams(
@@ -791,7 +766,7 @@
 
     def xa_copy(p, i):
         return remote(
-            Sa.at[p, pl.ds((x + i + 1) % 4 * 2, 2)], XRa.at[i, p], xas.at[p, i], xar.at[p, i], xp[i]
+            Sa.at[p, pl.ds((x + i + 1) % 4 * 2, 2)], XRa.at[i, p], xas.at[0], xar.at[p], xp[i]
         )
 
     def summed_a(p):
@@ -802,7 +777,7 @@
 
     def z2_copy(i):
         t = (z + i + 1) % 4
-        return remote(E1.at[t // 2, t % 2], ZR2.at[i], z2s.at[i], z2r.at[i], zp[i])
+        return remote(E1.at[t // 2, t % 2], ZR2.at[i], z2s.at[0], z2r.at[0], zp[i])
 
     def y_first(g, C, S, YR, E, XR, ZZ, F, cs, cr, ys, yr, xs, xr, zs, zr, ps, pr):
         def c_copy(p):
@@ -812,16 +787,16 @@
             return remote(
                 S.at[(1 - yl, 1 - yl, yl)[i], (yh, 1 - yh, 1 - yh)[i]],
                 YR.at[i],
-                ys.at[i],
-                yr.at[i],
+                ys.at[0],
+                yr.at[0],
                 (p1, p2, yhp)[i],
             )
 
         def x_copy(i):
-            return remote(E.at[(x + i + 1) % 4], XR.at[i], xs.at[i], xr.at[i], xp[i])
+            return remote(E.at[(x + i + 1) % 4], XR.at[i], xs.at[0], xr.at[0], xp[i])
 
         def z_copy(i):
-            return remote(ZZ.at[z], ZZ.at[z], zs.at[i], zr.at[i], zp[i])
+            return remote(ZZ.at[z], ZZ.at[z], zs.at[0], zr.at[0], zp[i])
 
         def p_copy():
             return remote(F.at[yl], F.at[yl], ps.at[0], pr.at[0], p1)
@@ -838,8 +813,7 @@
                 y_copy(i).start()
 
         def add_y():
-            for i in range(3):
-                y_copy(i).wait_recv()
+            settle(YR, yr.at[0])
             mine = S[yl, yh].astype(F32)
             for i in range(3):
                 mine = mine + YR[i].astype(F32)
@@ -848,8 +822,7 @@
                 x_copy(i).start()
 
         def add_x():
-            for i in range(3):
-                x_copy(i).wait_recv()
+            settle(XR, xr.at[0])
             mine = E[x].astype(F32)
             for i in range(3):
                 mine = mine + XR[i].astype(F32)
@@ -858,9 +831,7 @@
                 z_copy(i).start()
 
         def add_z():
-            for i in range(3):
-                there = (z + 3 - i) % 4
-                pltpu.make_async_copy(ZZ.at[there], ZZ.at[there], zr.at[i]).wait()
+            settle(ZZ.at[pl.ds(0, 3)], zr.at[0])
             total = (ZZ[0].astype(F32) + ZZ[1].astype(F32)) + (ZZ[2].astype(F32) + ZZ[3].astype(F32))
             F[yl] = (total * (1.0 / 128.0)).astype(BF16)
             p_copy().start()
@@ -873,10 +844,9 @@
             p_copy().wait_send()
             for p in range(2):
                 c_copy(p).wait_send()
-            for i in range(3):
-                y_copy(i).wait_send()
-                x_copy(i).wait_send()
-                z_copy(i).wait_send()
+            settle(YR, ys.at[0])
+            settle(XR, xs.at[0])
+            settle(ZZ.at[pl.ds(0, 3)], zs.at[0])
 
         return c_copy, add_cores, start_y, add_y, add_x, add_z, finish, drain
 
@@ -890,10 +860,10 @@
     owner = yh == z // 2
 
     def y_copy(i, e, yr, s_sem, r_sem):
-        return remote(e, yr.at[i], s_sem.at[i], r_sem.at[i], (p1, p2, yhp)[i])
+        return remote(e, yr.at[i], s_sem.at[0], r_sem.at[0], (p1, p2, yhp)[i])
 
     def f_copy(i, f, fr, s_sem, r_sem):
-        return remote(f, fr.at[z % 2], s_sem.at[i], r_sem.at[z % 2], zp[i])
+        return remote(f, fr.at[z % 2], s_sem.at[0], r_sem.at[z % 2], zp[i])
 
     def owners_send(e, yr, s_sem, r_sem):
         @pl.when(owner)
@@ -908,8 +878,7 @@
     def owners_sum(e, yr, s_sem, r_sem, f, fr, fs_sem, fr_sem):
         @pl.when(owner)
         def _():
-            for i in range(3):
-                y_copy(i, e, yr, s_sem, r_sem).wait_recv()
+            settle(yr, r_sem.at[0])
             total = (e[...].astype(F32) + yr[0].astype(F32)) + (yr[1].astype(F32) + yr[2].astype(F32))
             f[...] = (total * (1.0 / 128.0)).astype(BF16)
             for i in (0, 2, 1):
@@ -919,16 +888,14 @@
     def owners_end(e, yr, s_sem, r_sem, f, fr, fs_sem, fr_sem):
         @pl.when(owner)
         def _():
-            y_copy(0, e, yr, s_sem, r_sem).wait_send()
+            settle(e, s_sem.at[0])
             there = 1 - z % 2
             pltpu.make_async_copy(fr.at[there], fr.at[there], fr_sem.at[there]).wait()
-            for i in range(3):
-                f_copy(i, f, fr, fs_sem, fr_sem).wait_send()
+            settle(yr, fs_sem.at[0])
 
         @pl.when(jnp.logical_not(owner))
         def _():
-            for i in (1, 2):
-                y_copy(i, e, yr, s_sem, r_sem).wait_send()
+            settle(yr.at[pl.ds(0, 2)], s_sem.at[0])
             for there in range(2):
                 pltpu.make_async_copy(fr.at[there], fr.at[there], fr_sem.at[there]).wait()
 
@@ -938,10 +905,10 @@
 
         def z_copy(i):
             t = (z + i + 1) % 4
-            return remote(Z.at[t % 2, t // 2], ZR.at[i], zs.at[i], zr.at[i], zp[i])
+            return remote(Z.at[t % 2, t // 2], ZR.at[i], zs.at[0], zr.at[0], zp[i])
 
         def x_copy(i):
-            return remote(E2.at[(x + i + 1) % 4], XR.at[i], xs.at[i], xr.at[i], xp[i])
+            return remote(E2.at[(x + i + 1) % 4], XR.at[i], xs.at[0], xr.at[0], xp[i])
 
         def add_cores(p):
             c_copy(p).wait_recv()
@@ -956,8 +923,7 @@
                     z_copy(i).start()
 
         def add_z():
-            for i in range(3):
-                z_copy(i).wait_recv()
+            settle(ZR, zr.at[0])
             mine = Z[z % 2, z // 2].astype(F32)
             for i in range(3):
                 mine = mine + ZR[i].astype(F32)
@@ -966,8 +932,7 @@
                 x_copy(i).start()
 
         def add_x():
-            for i in range(3):
-                x_copy(i).wait_recv()
+            settle(XR, xr.at[0])
             mine = E2[x].astype(F32)
             for i in range(3):
                 mine = mine + XR[i].astype(F32)
@@ -983,9 +948,8 @@
         def drain():
             for p in range(2):
                 c_copy(p).wait_send()
-            for i in range(3):
-                z_copy(i).wait_send()
-                x_copy(i).wait_send()
+            settle(ZR, zs.at[0])
+            settle(XR, xs.at[0])
 
         return c_copy, add_cores, add_z, add_x, add_y, finish, drain
 
@@ -1141,8 +1105,7 @@
     l_z()
 
     for p in range(2):
-        for i in range(3):
-            xa_copy(p, i).wait_recv()
+        settle(XRa.at[:, p], xar.at[p])
         mine = Sa[p, pl.ds(2 * x, 2)].astype(F32)
         for i in range(3):
             mine = mine + XRa[i, p].astype(F32)
@@ -1169,8 +1132,7 @@
 
     c_z()
     b_y()
-    for i in range(3):
-        z2_copy(i).wait_recv()
+    settle(ZR2, z2r.at[0])
     mine = E1[z // 2, z % 2].astype(F32)
     for i in range(3):
         mine = mine + ZR2[i].astype(F32)
@@ -1206,10 +1168,8 @@
         drain()
     for p in range(2):
         ca_copy(p).wait_send()
-        for i in range(3):
-            xa_copy(p, i).wait_send()
-    for i in range(3):
-        z2_copy(i).wait_send()
+    settle(XRa, xas.at[0])
+    settle(ZR2, z2s.at[0])
 
 
 def block_grads(cot, wq, wo, normt, proj, prob, combt, n2, r2, xin, ng, mg):
@@ -1258,12 +1218,9 @@
             for lead in ((2, 8, 2), (2, 8), (2, 2, 4), (3, 4), (4,), (3,), (4,), (2,))
         ]
         + [dma((9,))]
-        + [
-            dma(n)
-            for n in ((2,), (2,), (2, 3), (2, 3), (3,), (3,), (3,), (3,), (3,), (2,))
-        ]
-        + [dma((n,)) for n in (2, 2, 3, 3, 3, 3, 3, 3, 3, 2) * 2]
-        + [dma((n,)) for n in (2, 2, 3, 3, 3, 3, 3, 3, 1, 1) * 2],
+        + [dma((n,)) for n in (2, 2, 1, 2, 1, 1, 1, 1, 1, 2)]
+        + [dma((n,)) for n in (2, 2, 1, 1, 1, 1, 1, 1, 1, 2) * 2]
+        + [dma((n,)) for n in (2, 2, 1, 1, 1, 1, 1, 1, 1, 1) * 2],
         compiler_params=pltpu.CompilerParams(
             collective_id=2, has_side_effects=True, vmem_limit_bytes=62 << 20
         ),

time: 167 us -> 163 us (0.976)
  Pallas kernels: 166 us -> 163 us
    pallas_call x1, Pallas kernels: 110 us -> 107 us  [merger(): pl.pallas_call(merger_kernel, name='merger', out_shape=tuple((jax.ShapeDt...]
where the time goes in v6:
time: 163 us
  Pallas kernels  163 us (100%)
    pallas_call x1, Pallas kernels, merger(): pl.pallas_call(merger_kernel, name='merger', out_shape=tuple((jax.ShapeDt...  107 us
    pallas_call x1, Pallas kernels, block_grads(): pl.pallas_call(block_kernel, name='block', out_shape=(jax.ShapeDtypeStruc...  52.8 us

profile of v6, /device:TPU:0, one launch (start us, length us, event | category | flops | bytes accessed | tf_op | source)
XLA Modules:
  0.0 163.2 jit_solution(2181293877129705499)
XLA Ops:
  0.6 106.9 %merger.1 = (bf16[512,1280]{1,0:T(8,128)(2,1)}, bf16[16,80,1920]{2,1,0:T(8,128)(2,1)}, bf16[640,1280]{1,0:T(8,128)(2,1)}, bf16[1280,512]{1,0:T(8,128)(2,1)}, bf1...) custom-call(bf16[64,8192]{1,0:T(8,128)(2,1)} %tok.1, ...), custom_call_target="tpu_custom_call" | custom-call | flops 8999999488 | bytes 40000000 | tf_op jit(solution)/shard_map/merger/pallas_call | solution.py:671
  107.5 52.8 %block.1 = (bf16[512,1280]{1,0:T(8,128)(2,1)}, f32[80,1920]{1,0:T(8,128)}, f32[40,1280]{1,0:T(8,128)}) custom-call(bf16[512,1280]{1,0:T(8,128)(2,1)} %get-tuple-element.15.cot_i, bf16[16,80,1920]{2,1,0:T(8,128)(2,1)} %get-tuple-element.16.wq_i, bf16[640,1280]{1,0:T(8,128)(2,1)} %get-tuple-element.17.wo_i, bf16[1280,512]{1,0:T(8,128)(2,1)} %get-tuple-element.18.normt_i, ...), custom_call_target="tpu_custom_call" | custom-call | flops 8000000000 | bytes 40000000 | tf_op jit(solution)/shard_map/block/pallas_call | solution.py:1182
  160.3 2.9 %finish.1 = (bf16[512,1280]{1,0:T(8,128)(2,1)}, f32[80,1920]{1,0:T(8,128)}, f32[40,1280]{1,0:T(8,128)}) custom-call(bf16[512,1280]{1,0:T(8,128)(2,1)} %get-tuple-element.24.a, f32[80,1920]{1,0:T(8,128)} %get-tuple-element.25.b, f32[40,1280]{1,0:T(8,128)} %get-tuple-element.26.c), custom_call_target="tpu_custom_call" | custom-call | tf_op jit(solution)/shard_map/finish/pallas_call | solution.py:1239
